TPU v7x, 32 devices: a whole 2x2x4 slice. The times are simulated.
32 devices in a mesh: expert: 8 (over z, x), dp: 4 (over y, core).
Axes of the slice: x: 2, y: 2, z: 4, core: 2. Of those that a mesh axis runs over, the one named last changes fastest.
Arguments:
- tokens: bfloat16 [4096, 1024], P(('expert', 'dp')), may hold values from -6 to 6
- expert_ids: int32 [4096, 2], P(('expert', 'dp')), may hold values from 0 to 7, all different within a row; in each aligned block of 128 rows (0 to 127, 128 to 255, ...) at most 48 rows name the same one
- combine: float32 [4096, 2], P(('expert', 'dp')), may hold values from 0.25 to 1
- language: int32 [4096], P(('expert', 'dp')), may hold values from 0 to 7
- lang_slot: int32 [8], replicated, may hold values from 0 to 7, each once
- up_weight: bfloat16 [8, 1024, 4096], P('expert', None, 'dp'), may hold values from -0.1875 to 0.1875
- down_weight: bfloat16 [8, 4096, 1024], P('expert', 'dp'), may hold values from -0.09375 to 0.09375
- adapter_in: bfloat16 [8, 8, 16, 4096], P('dp', 'expert'), may hold values from -0.09375 to 0.09375
- adapter_out: bfloat16 [8, 8, 16, 1024], P('dp', 'expert'), may hold values from -1.5 to 1.5
Outputs:
- mixed: bfloat16 [4096, 1024], P(('expert', 'dp'))
Inputs may be any that keep to these rules, and one draw needn't show every extreme that they name: `expert_ids`: the two experts of a token differ; among the tokens of one device no expert is named by more than 48 choices, a bound that some block reaches. `lang_slot`: each slot holds exactly one language.
All inputs are finite; a program needn't handle non-finite values.
Results may differ from a plain program's by a relative error of at most 0.015.
Values may be sent and summed in bfloat16 or wider, within the bound.
No kernel may reach another device: no remote copies, remote signals or barrier semaphores. Data moves between devices by JAX's collectives and lax.ppermute only.
A program may use at most 128 MiB of HBM per device.

v0:
```python
import jax
import jax.numpy as jnp
from jax import lax
from jax.sharding import PartitionSpec as P


def expert_part(sent_rows, slot_codes, w_up, down_matrix, adapter_input_piece, adapter_output_full):
    language_count = adapter_input_piece.shape[0]
    adapter_rank = adapter_input_piece.shape[1]
    hidden_state = jnp.maximum(
        jnp.dot(sent_rows, w_up, preferred_element_type=jnp.float32), 0.0
    ).astype(jnp.bfloat16)
    input_flattened = adapter_input_piece.reshape(
        language_count * adapter_rank, adapter_input_piece.shape[2]
    )
    reduced_rank = lax.dot_general(
        hidden_state, input_flattened, (((1,), (1,)), ((), ())), preferred_element_type=jnp.float32
    )
    column_position = jnp.arange(language_count * adapter_rank, dtype=jnp.int32) // adapter_rank
    keep_mask = slot_codes[:, None] - 1 == column_position[None, :]
    reduced_rank = jnp.where(keep_mask, reduced_rank, 0.0).astype(jnp.bfloat16)
    output_flattened = adapter_output_full.reshape(
        language_count * adapter_rank, adapter_output_full.shape[2]
    )
    adapter_update = jnp.dot(reduced_rank, output_flattened, preferred_element_type=jnp.float32)
    return jnp.dot(hidden_state, down_matrix, preferred_element_type=jnp.float32) + adapter_update


def build_send(tokens, expert_ids, language, lang_slot, expert_count, capacity):
    tok_count = tokens.shape[0]
    flat_route = jnp.concatenate([expert_ids[:, 0], expert_ids[:, 1]])
    expert_range = jnp.arange(expert_count, dtype=jnp.int32)
    one_hot = (flat_route[:, None] == expert_range[None, :]).astype(jnp.int32)
    before = jnp.cumsum(one_hot, axis=0) - one_hot
    position = jnp.sum(before * one_hot, axis=1)
    slot_of_row = flat_route * capacity + position
    slot_range = jnp.arange(expert_count * capacity, dtype=jnp.int32)
    row_range = jnp.arange(2 * tok_count, dtype=jnp.int32)
    source = jnp.sum(
        jnp.where(slot_of_row[None, :] == slot_range[:, None], row_range[None, :] + 1, 0), axis=1
    )
    filled = source > 0
    token_index = jnp.where(filled, source - 1, 0) % tok_count
    lang_range = jnp.arange(lang_slot.shape[0], dtype=jnp.int32)
    token_slot = jnp.sum(
        jnp.where(language[:, None] == lang_range[None, :], lang_slot[None, :], 0), axis=1
    )
    sent_rows = jnp.where(
        filled[:, None], jnp.take(tokens, token_index, axis=0), jnp.zeros((), tokens.dtype)
    )
    slot_codes = jnp.where(filled, jnp.take(token_slot, token_index) + 1, 0)
    return (
        sent_rows.reshape(expert_count, capacity, -1),
        slot_codes.reshape(expert_count, capacity),
        slot_of_row,
    )


def local(
    tokens,
    expert_ids,
    combine,
    language,
    lang_slot,
    up_weight,
    down_weight,
    adapter_in,
    adapter_out,
):
    tok_count = tokens.shape[0]
    model_width = tokens.shape[1]
    expert_count = lax.axis_size("expert")
    dp_count = lax.axis_size("dp")
    capacity = 3 * tok_count // expert_count
    send_rows, send_codes, slot_of_row = build_send(
        tokens, expert_ids, language, lang_slot, expert_count, capacity
    )
    got_rows, got_codes = (
        lax.all_to_all(send_rows, "expert", split_axis=0, concat_axis=0, tiled=True),
        lax.all_to_all(send_codes, "expert", split_axis=0, concat_axis=0, tiled=True),
    )
    in_part = lax.all_to_all(adapter_in, "dp", split_axis=3, concat_axis=0, tiled=True)
    all_rows, all_codes, out_full = (
        lax.all_gather(got_rows, "dp", axis=0, tiled=True),
        lax.all_gather(got_codes, "dp", axis=0, tiled=True),
        lax.all_gather(adapter_out, "dp", axis=0, tiled=True),
    )
    partial_term = expert_part(
        all_rows.reshape(-1, model_width),
        all_codes.reshape(-1),
        up_weight[0],
        down_weight[0],
        in_part[:, 0],
        out_full[:, 0],
    )
    rounded_term = partial_term.astype(jnp.bfloat16)
    summed = lax.psum_scatter(
        rounded_term.reshape(dp_count, expert_count, capacity, model_width),
        "dp",
        scatter_dimension=0,
        tiled=True,
    ).astype(jnp.float32)
    result_rows = summed.astype(jnp.bfloat16).reshape(expert_count, capacity, model_width)
    returned = lax.all_to_all(result_rows, "expert", split_axis=0, concat_axis=0, tiled=True)
    flat_back = returned.reshape(expert_count * capacity, model_width)
    picked = jnp.take(flat_back, slot_of_row, axis=0).astype(jnp.float32)
    mixed_out = combine[:, 0:1] * picked[:tok_count] + combine[:, 1:2] * picked[tok_count:]
    return mixed_out.astype(jnp.bfloat16)


def solution(mesh):
    placed = (
        P(("expert", "dp"), None),
        P(("expert", "dp"), None),
        P(("expert", "dp"), None),
        P(("expert", "dp")),
        P(),
        P("expert", None, "dp"),
        P("expert", "dp", None),
        P("dp", "expert", None, None),
        P("dp", "expert", None, None),
    )
    return jax.shard_map(
        local, mesh=mesh, in_specs=placed, out_specs=P(("expert", "dp"), None), check_vma=False
    )
```

profile of v0, /device:TPU:0, one launch (start us, length us, event | category | flops | bytes accessed | tf_op | source)
XLA Modules:
  0.0 176.5 jit_solution(3492741450129488305)
XLA Ops:
  6.5 0.8 fusion.20
  7.4 0.6 reduce-window.6
  8.0 0.2 slice_reduce_fusion
  8.3 0.1 fusion.11
  8.4 0.1 select_reduce_fusion
  8.5 0.1 gt.44
  8.8 3.8 %gather_fusion = bf16[384,1024]{1,0:T(8,128)(2,1)S(1)} fusion(bf16[128,1024]{1,0:T(8,128)(2,1)} %param.9, s32[1024]{0:T(1024)S(1)} %pad_clamp_fusion.1), kind=kCustom, calls=%fused_computation | custom fusion | bytes 1574400 | tf_op jit(solution)/shard_map/jit(_take)/gather | solution.py:49
  12.6 0.2 select_select_fusion
  12.7 27.3 %all_to_all.34 = bf16[8,48,1024]{2,1,0:T(8,128)(2,1)} all-to-all(bf16[8,48,1024]{2,1,0:T(8,128)(2,1)S(1)} %select_select_fusion), channel_id=1, replica_groups=mesh['expert'=8,'dp'=4] {'expert'}, dimensions={0} | all-to-all | bytes 1572864 | tf_op jit(solution)/shard_map/all_to_all | solution.py:79
  40.2 0.1 gt.47
  40.3 0.1 select_reduce_fusion.1
  40.3 2.7 %gather_fusion.1 = s32[384]{0:T(512)S(1)} fusion(s32[128]{0:T(128)S(1)} %select_reduce_fusion.1, s32[1024]{0:T(1024)S(1)} %pad_clamp_fusion.1), kind=kCustom, calls=%fused_computation.1 | custom fusion | bytes 4608 | tf_op jit(solution)/shard_map/jit(_take)/gather | solution.py:51
  43.0 0.1 gather.19
  43.1 0.6 add_select_fusion.2
  43.7 3.6 %all-to-all-start.1 = ((s32[8,1,48]{2,1,0:T(1,128)}), s32[8,1,48]{2,1,0:T(1,128)S(1)}, u32[]{:S(2)}, u32[]{:S(2)}) async-start(s32[8,1,48]{2,1,0:T(1,128)} %bitcast.10), calls=%async_computation.1 | async-start | bytes 8192 | tf_op jit(solution)/shard_map/all_to_all | solution.py:80
  47.3 3.8 %copy.20 = bf16[2,1,16,4096]{2,0,1,3:T(2,128)(2,1)} copy(bf16[2,1,16,4096]{3,2,1,0:T(8,128)(2,1)S(1)} %copy-done.2) | data formatting | bytes 524288 | tf_op args[7]
  51.1 4.1 %reshape.357 = bf16[4,2,16384]{2,1,0:T(2,128)(2,1)} reshape(bf16[4096,1,2,16]{3,2,1,0:T(2,128)(2,1)} %bitcast.46) | data formatting | bytes 524288
  55.2 3.4 %all-to-all-start.2 = ((bf16[4,2,16384]{2,1,0:T(2,128)(2,1)}), bf16[4,2,16384]{2,1,0:T(2,128)(2,1)S(1)}, u32[]{:S(2)}, u32[]{:S(2)}) async-start(bf16[4,2,16384]{2,1,0:T(2,128)(2,1)} %reshape.357), calls=%async_computation.2 | async-start | bytes 524288 | tf_op jit(solution)/shard_map/all_to_all | solution.py:82
  58.7 12.6 %all_gather.11 = bf16[8,1,16,1024]{3,2,1,0:T(8,128)(2,1)S(1)} all-gather(bf16[2,1,16,1024]{3,2,1,0:T(8,128)(2,1)S(1)} %copy-done.3), channel_id=1, replica_groups=mesh['expert'=8,'dp'=4] {'dp'}, dimensions={0}, use_global_device_ids=true | all-gather | bytes 327680 | tf_op jit(solution)/shard_map/all_gather | solution.py:86
  71.2 5.2 %all-gather = s32[32,1,48]{2,1,0:T(1,128)S(1)} all-gather(s32[8,1,48]{2,1,0:T(1,128)S(1)} %all-to-all-done.1), channel_id=2, replica_groups=mesh['expert'=8,'dp'=4] {'dp'}, dimensions={0}, use_global_device_ids=true | all-gather | bytes 7680 | tf_op jit(solution)/shard_map/all_gather | solution.py:85
  76.5 2.4 %reshape.358 = bf16[4096,1,2,16]{3,2,1,0:T(2,128)(2,1)} reshape(bf16[4,2,16384]{2,1,0:T(2,128)(2,1)S(1)} %all-to-all-done.2) | data formatting | bytes 524288
  78.9 4.9 %copy.23 = bf16[2,1,16,4,1024]{4,3,2,0,1:T(4,128)(2,1)S(1)} copy(bf16[2,1,16,4,1024]{2,0,4,3,1:T(2,128)(2,1)} %bitcast.45) | data formatting | bytes 524288 | tf_op jit(solution)/shard_map/all_to_all | solution.py:82
  83.9 0.1 copy.22
  84.0 5.7 %maximum_convert_fusion = bf16[1536,1024]{1,0:T(8,128)(2,1)S(1)} fusion(bf16[1536,1024]{1,0:T(8,128)(2,1)} %bitcast.54, bf16[1,1024,1024]{2,1,0:T(8,128)(2,1)S(1)} %copy-done), kind=kOutput, calls=%fused_computation.4 | convolution fusion | flops 3224371200 | bytes 8388608 | tf_op jit(solution)/shard_map/dot_general | solution.py:11
  89.7 5.3 %fusion.1 = f32[1536,1024]{1,0:T(8,128)} fusion(bf16[1536,1024]{1,0:T(8,128)(2,1)S(1)} %maximum_convert_fusion, bf16[1,1024,1024]{2,1,0:T(8,128)(2,1)S(1)} %copy-done.5), kind=kOutput, calls=%fused_computation.7 | convolution fusion | flops 3221225472 | bytes 11534336 | tf_op jit(solution)/shard_map/dot_general | solution.py:26
  95.1 8.6 %add_convert_fusion = bf16[1536,1024]{1,0:T(8,128)(2,1)} fusion(f32[1536,1024]{1,0:T(8,128)} %fusion.1, bf16[128,1024]{1,0:T(8,128)(2,1)S(1)} %bitcast.48, bf16[1536,1024]{1,0:T(8,128)(2,1)} %copy-done.1, bf16[128,1024]{1,0:T(8,128)(2,1)S(1)} %bitcast.49, s32[128]{0:T(128)S(1)} %and_select_fusion.1, s32[1536]{0:T(1024)S(1)} %sub.27), kind=kOutput, calls=%fused_computation.3 | convolution fusion | flops 809041920 | bytes 13113856 | tf_op jit(solution)/shard_map/dot_general | solution.py:25
  103.7 38.1 %reduce-scatter.2.cloned.1.call-done = bf16[1,8,48,1024]{3,2,1,0:T(8,128)(2,1)} async-done(((bf16[4,8,48,1024]{3,2,1,0:T(8,128)(2,1)}), bf16[1,8,48,1024]{3,2,1,0:T(8,128)(2,1)}) %reduce-scatter.2.cloned.1.call-update) | async-done | bytes 786448 | tf_op jit(solution)/shard_map/reduce_scatter | solution.py:97
  141.8 5.5 %all-to-all-start.3 = ((bf16[8,48,1024]{2,1,0:T(8,128)(2,1)}), bf16[8,48,1024]{2,1,0:T(8,128)(2,1)S(1)}, u32[]{:S(2)}, u32[]{:S(2)}) async-start(bf16[8,48,1024]{2,1,0:T(8,128)(2,1)} %bitcast.51), calls=%async_computation.4 | async-start | bytes 1572864 | tf_op jit(solution)/shard_map/all_to_all | solution.py:104
  147.4 20.1 %all-to-all-done.3 = bf16[8,48,1024]{2,1,0:T(8,128)(2,1)S(1)} async-done(((bf16[8,48,1024]{2,1,0:T(8,128)(2,1)}), bf16[8,48,1024]{2,1,0:T(8,128)(2,1)S(1)}, u32[]{:S(2)}, u32[]{:S(2)}) %all-to-all-start.3) | async-done | bytes 786464 | tf_op jit(solution)/shard_map/all_to_all | solution.py:104
  167.5 1.2 gather_fusion.2
  168.7 0.1 select_convert_fusion
  168.8 0.8 fusion.6
  (41 shorter events, 0.6 us)
Async XLA Ops:
  6.5 77.5 %copy-start = (bf16[1,1024,1024]{2,1,0:T(8,128)(2,1)S(1)}, bf16[1,1024,1024]{2,1,0:T(8,128)(2,1)}, u32[]{:S(2)}) copy-start(bf16[1,1024,1024]{2,1,0:T(8,128)(2,1)} %param.14) | copy-start | bytes 6291460
  6.5 77.5 %all-gather.3.cloned.1.call-start = ((), (), s32[]{:S(2)}) async-start(), calls=%async_computation.5 | async-start | bytes 3932160 | tf_op jit(solution)/shard_map/all_gather | solution.py:84
  12.5 27.7 %copy-start.6 = (s32[8]{0:T(128)S(1)}, s32[8]{0:T(128)}, u32[]{:S(2)}) copy-start(s32[8]{0:T(128)} %param.13) | copy-start | bytes 100
  12.5 27.7 %copy-start.7 = (s32[128]{0:T(128)S(1)}, s32[128]{0:T(128)}, u32[]{:S(2)}) copy-start(s32[128]{0:T(128)} %param.12) | copy-start | bytes 1540
  12.6 34.8 %copy-start.2 = (bf16[2,1,16,4096]{3,2,1,0:T(8,128)(2,1)S(1)}, bf16[2,1,16,4096]{3,2,1,0:T(8,128)(2,1)}, u32[]{:S(2)}) copy-start(bf16[2,1,16,4096]{3,2,1,0:T(8,128)(2,1)} %param.16) | copy-start | bytes 786436
  43.0 15.6 %copy-start.3 = (bf16[2,1,16,1024]{3,2,1,0:T(8,128)(2,1)S(1)}, bf16[2,1,16,1024]{3,2,1,0:T(8,128)(2,1)}, u32[]{:S(2)}) copy-start(bf16[2,1,16,1024]{3,2,1,0:T(8,128)(2,1)} %param.17) | copy-start | bytes 196612
  43.7 11.5 %all-to-all-start.1 = ((s32[8,1,48]{2,1,0:T(1,128)}), s32[8,1,48]{2,1,0:T(1,128)S(1)}, u32[]{:S(2)}, u32[]{:S(2)}) async-start(s32[8,1,48]{2,1,0:T(1,128)} %bitcast.10), calls=%async_computation.1 | async-start | bytes 8192 | tf_op jit(solution)/shard_map/all_to_all | solution.py:80
  55.2 21.3 %all-to-all-start.2 = ((bf16[4,2,16384]{2,1,0:T(2,128)(2,1)}), bf16[4,2,16384]{2,1,0:T(2,128)(2,1)S(1)}, u32[]{:S(2)}, u32[]{:S(2)}) async-start(bf16[4,2,16384]{2,1,0:T(2,128)(2,1)} %reshape.357), calls=%async_computation.2 | async-start | bytes 524288 | tf_op jit(solution)/shard_map/all_to_all | solution.py:82
  58.6 83.2 %reduce-scatter.2.cloned.1.call-start = ((), (), s32[]{:S(2)}) async-start(), calls=%async_computation.6 | async-start | bytes 3932160 | tf_op jit(solution)/shard_map/reduce_scatter | solution.py:97
  84.0 5.7 %copy-start.5 = (bf16[1,1024,1024]{2,1,0:T(8,128)(2,1)S(1)}, bf16[1,1024,1024]{2,1,0:T(8,128)(2,1)}, u32[]{:S(2)}) copy-start(bf16[1,1024,1024]{2,1,0:T(8,128)(2,1)} %param.15) | copy-start | bytes 6291460
  89.7 5.3 %copy-start.1 = (bf16[1536,1024]{1,0:T(8,128)(2,1)}, bf16[1536,1024]{1,0:T(8,128)(2,1)S(1)}, u32[]{:S(2)}) copy-start(bf16[1536,1024]{1,0:T(8,128)(2,1)S(1)} %maximum_convert_fusion) | copy-start | bytes 9437188
  103.6 43.7 %copy-start.4 = (f32[128,2]{0,1:T(2,128)S(1)}, f32[128,2]{0,1:T(2,128)}, u32[]{:S(2)}) copy-start(f32[128,2]{0,1:T(2,128)} %param.11) | copy-start | bytes 3076
  141.8 25.7 %all-to-all-start.3 = ((bf16[8,48,1024]{2,1,0:T(8,128)(2,1)}), bf16[8,48,1024]{2,1,0:T(8,128)(2,1)S(1)}, u32[]{:S(2)}, u32[]{:S(2)}) async-start(bf16[8,48,1024]{2,1,0:T(8,128)(2,1)} %bitcast.51), calls=%async_computation.4 | async-start | bytes 1572864 | tf_op jit(solution)/shard_map/all_to_all | solution.py:104
Sparse Core Ops, SparseCore 0:
  40.2 31.7 all-gather.2
  103.8 37.9 reduce-scatter.1
where the time goes:
time: 177 us; the launch traced here: 176 us
  waiting for transfers between devices  58.3 us (33%)
  blocking collectives  45 us (25%)
  local copies, waits for them, and re-layouts  24.5 us (14%)
  matrix products  19.6 us (11%)
  between operations  13.6 us (8%)
  starting transfers between devices  12.6 us (7%)
  other arithmetic  2.86 us (2%)
    reduce_scatter x1, waiting for transfers between devices, local(): lax.psum_scatter(rounded_term.reshape(dp_count, expert_count, capacity, m...  38.1 us
    all_to_all x1, blocking collectives, local(): lax.all_to_all(send_rows, 'expert', split_axis=0, concat_axis=0, tiled=True)  27.3 us
    all_to_all x1, waiting for transfers between devices, local(): lax.all_to_all(result_rows, 'expert', split_axis=0, concat_axis=0, tiled=...  20.1 us
    all_gather x1, blocking collectives, local(): lax.all_gather(adapter_out, 'dp', axis=0, tiled=True)  12.6 us
    unnamed x19, local copies, waits for them, and re-layouts  10.3 us
    dot_general x1, matrix products, expert_part(): jnp.dot(reduced_rank, output_flattened, preferred_element_type=jnp.float32)  8.58 us
    dot_general x1, matrix products, expert_part(): jnp.dot(sent_rows, w_up, preferred_element_type=jnp.float32)  5.69 us
    all_to_all x1, starting transfers between devices, local(): lax.all_to_all(result_rows, 'expert', split_axis=0, concat_axis=0, tiled=...  5.51 us
  transfers between devices with their start and end apart: 5, of which 2 were waited for; matrix products, arithmetic and copies ran while one was open for 11% of the time, Pallas kernels for 0%

commit v1 on v0

--- a/solution.py
+++ b/solution.py
@@ -1,7 +1,230 @@
+import functools
+
 import jax
 import jax.numpy as jnp
 from jax import lax
+from jax.experimental import pallas as pl
+from jax.experimental.pallas import tpu as pltpu
 from jax.sharding import PartitionSpec as P
+
+F32 = jnp.float32
+BF16 = jnp.bfloat16
+VMEM = pl.BlockSpec(memory_space=pltpu.VMEM)
+SMEM = pl.BlockSpec(memory_space=pltpu.SMEM)
+ANY = pl.BlockSpec(memory_space=pl.ANY)
+
+
+def iota(shape, dim):
+    return lax.broadcasted_iota(jnp.int32, shape, dim)
+
+
+def row_places(hit):
+    count = hit.shape[1]
+    earlier = (iota((count, count), 0) < iota((count, count), 1)).astype(BF16)
+    place = jnp.dot(hit.astype(F32).astype(BF16), earlier, preferred_element_type=F32)
+    return jnp.where(hit, place, -1.0)
+
+
+def prep_kernel(cap, slot_ref, ids_ref, lang_ref, tok_ref, *outs):
+    experts = len(outs) - 1
+    count = tok_ref.shape[0]
+    me = lax.axis_index("expert")
+    first, second = ids_ref[0:1, :], ids_ref[1:2, :]
+    expert = iota((experts, count), 0) ^ me
+    place = row_places((first == expert) | (second == expert))
+    want = iota((cap, count), 0).astype(F32)
+    select = jnp.concatenate(
+        [(place[j : j + 1, :] == want).astype(F32).astype(BF16) for j in range(experts)], axis=0
+    )
+    rows = jnp.dot(select, tok_ref[...], preferred_element_type=F32).astype(BF16)
+    for j in range(experts):
+        outs[j][...] = rows[j * cap : (j + 1) * cap]
+    lang = lang_ref[...]
+    slot = jnp.zeros_like(lang)
+    for i in range(slot_ref.shape[0]):
+        slot = jnp.where(lang == i, slot_ref[i], slot)
+    outs[experts][...] = first + experts * second + experts * experts * slot
+
+
+def row_slots(codes, cap, experts):
+    me = lax.axis_index("expert")
+    sources, count = codes.shape
+    first = lax.rem(codes, experts)
+    second = lax.rem(lax.div(codes, experts), experts)
+    slot = lax.div(codes, experts * experts).astype(F32)
+    place = row_places((first == me) | (second == me))
+    want = iota((cap, count), 0).astype(F32)
+    found = [
+        jnp.sum(
+            jnp.where(place[s : s + 1, :] == want, slot[s : s + 1, :] + 1.0, 0.0),
+            axis=1,
+            keepdims=True,
+        )
+        for s in range(sources)
+    ]
+    return jnp.concatenate(found, axis=0) - 1.0
+
+
+def expert_kernel(
+    cap, experts, rank, blocks, codes_ref, peer_ref, own_a_ref, own_b_ref, up_a, up_b, down_a, down_b,
+    ain_ref, aout_ref, send_ref, keep_ref, up_buf, down_buf, sems,
+):
+    hid = up_a.shape[1]
+    step = hid // blocks
+    copies = []
+    for h, (up, down) in enumerate(((up_a, down_a), (up_b, down_b))):
+        for b in range(blocks):
+            span = pl.ds(b * step, step)
+            one = pltpu.make_async_copy(up.at[:, span], up_buf.at[h, :, span], sems.at[0, h, b])
+            two = pltpu.make_async_copy(down.at[span, :], down_buf.at[h, span, :], sems.at[1, h, b])
+            one.start()
+            two.start()
+            copies.append((one, two))
+    dp = lax.axis_index("dp")
+    slots = row_slots(codes_ref[...], cap, experts)
+    width = aout_ref.shape[0]
+    column = iota((1, width), 1)
+    part = lax.div(column, width // 4)
+    owner = dp ^ (lax.rem(part, 2) * 2 + lax.div(part, 2))
+    column_slot = owner * (width // 4 // rank) + lax.rem(lax.div(column, rank), width // 4 // rank)
+    keep = slots == column_slot.astype(F32)
+    rows = jnp.concatenate([peer_ref[...], own_a_ref[...], own_b_ref[...]], axis=0)
+    total = jnp.zeros((rows.shape[0], aout_ref.shape[1]), F32)
+    core = lax.rem(dp, 2)
+    for h in range(2):
+        low = jnp.zeros((rows.shape[0], width), F32)
+        base = (core ^ h) * hid
+        for b in range(blocks):
+            span = pl.ds(b * step, step)
+            one, two = copies[h * blocks + b]
+            one.wait()
+            hidden = jnp.dot(rows, up_buf[h, :, span], preferred_element_type=F32)
+            hidden = jnp.maximum(hidden, 0.0).astype(BF16)
+            two.wait()
+            total += jnp.dot(hidden, down_buf[h, span, :], preferred_element_type=F32)
+            where = pl.ds(pl.multiple_of(base + b * step, step), step)
+            low += lax.dot_general(
+                hidden, ain_ref[:, where], (((1,), (1,)), ((), ())), preferred_element_type=F32
+            )
+        low = jnp.where(keep, low, 0.0).astype(BF16)
+        total += jnp.dot(low, aout_ref[...], preferred_element_type=F32)
+    half = rows.shape[0] // 2
+    send_ref[...] = total[:half].astype(BF16)
+    keep_ref[...] = total[half:]
+
+
+def mix_kernel(cap, ids_ref, combine_ref, *refs):
+    backs, out_ref = refs[:-1], refs[-1]
+    experts = len(backs)
+    count = ids_ref.shape[0]
+    me = lax.axis_index("expert")
+    first, second = ids_ref[:, 0:1] ^ me, ids_ref[:, 1:2] ^ me
+    lane = iota((count, 128), 1)
+    hit = ((first == lane) | (second == lane)).astype(F32).astype(BF16)
+    earlier = (iota((count, count), 1) < iota((count, count), 0)).astype(F32).astype(BF16)
+    place = jnp.dot(earlier, hit, preferred_element_type=F32)
+    back = jnp.concatenate([b[...] for b in backs], axis=0)
+    spot = iota((count, experts * cap), 1).astype(F32)
+    mixed = None
+    for k, choice in enumerate((first, second)):
+        at = jnp.sum(jnp.where(choice == lane, place, 0.0), axis=1, keepdims=True)
+        at = at + (choice * cap).astype(F32)
+        select = (at == spot).astype(F32).astype(BF16)
+        picked = jnp.dot(select, back, preferred_element_type=F32)
+        term = combine_ref[:, k : k + 1] * picked
+        mixed = term if mixed is None else mixed + term
+    out_ref[...] = mixed.astype(BF16)
+
+
+def flip(x, axis, bit):
+    size = lax.axis_size(axis)
+    return lax.ppermute(x, axis, [(i, i ^ bit) for i in range(size)])
+
+
+def local_pairs(
+    tokens, expert_ids, combine, language, lang_slot, up_weight, down_weight, adapter_in, adapter_out
+):
+    count, width = tokens.shape
+    experts = lax.axis_size("expert")
+    cap = 3 * count // experts
+    slots, _, rank, hid_all = adapter_in.shape
+    up, down = up_weight[0], down_weight[0]
+    hid = up.shape[1]
+
+    up_other, down_other = flip(up, "dp", 1), flip(down, "dp", 1)
+
+    prep = pl.pallas_call(
+        functools.partial(prep_kernel, cap),
+        out_shape=[jax.ShapeDtypeStruct((cap, width), BF16)] * experts
+        + [jax.ShapeDtypeStruct((1, count), jnp.int32)],
+        in_specs=[SMEM, VMEM, VMEM, VMEM],
+        out_specs=[VMEM] * (experts + 1),
+        cost_estimate=pl.CostEstimate(flops=10**8, bytes_accessed=2 * 10**6, transcendentals=0),
+        name="prep",
+    )(lang_slot, expert_ids.T, language[None, :], tokens)
+    send, code = prep[:experts], prep[experts]
+
+    got = [send[0]] + [None] * (experts - 1)
+    order = [j ^ 1 for j in range(experts - 1, 0, -1)]
+    order = [j if j else 1 for j in order]
+    for j in order:
+        got[j] = flip(send[j], "expert", j)
+
+    bit = 1
+    while bit < experts:
+        code = jnp.concatenate([code, flip(code, "expert", bit)], axis=0)
+        bit *= 2
+    code_peer = flip(code, "dp", 2)
+
+    y = lax.axis_index("dp") // 2
+    flat_in = adapter_in.reshape(slots * rank, hid_all)
+    flat_out = adapter_out.reshape(slots * rank, width)
+    mine = lax.dynamic_slice_in_dim(flat_in, y * 2 * hid, 2 * hid, 1)
+    theirs = lax.dynamic_slice_in_dim(flat_in, (1 - y) * 2 * hid, 2 * hid, 1)
+    other = flip(jnp.concatenate([theirs, flat_out], axis=1), "dp", 2)
+    pair = jnp.concatenate([jnp.concatenate([mine, flat_out], axis=1), other], axis=0)
+    full = jnp.concatenate([pair, flip(pair, "dp", 1)], axis=0)
+    ain, aout = full[:, : 2 * hid], full[:, 2 * hid :]
+
+    blocks = 4
+    backs = [None] * experts
+    for k in range(experts // 2 - 1, -1, -1):
+        a, b = got[2 * k], got[2 * k + 1]
+        peer = flip(jnp.concatenate([a, b], axis=0), "dp", 2)
+        codes = jnp.concatenate([code_peer[2 * k : 2 * k + 2], code[2 * k : 2 * k + 2]], axis=0)
+        part, own = pl.pallas_call(
+            functools.partial(expert_kernel, cap, experts, rank, blocks),
+            out_shape=[
+                jax.ShapeDtypeStruct((2 * cap, width), BF16),
+                jax.ShapeDtypeStruct((2 * cap, width), F32),
+            ],
+            in_specs=[VMEM, VMEM, VMEM, VMEM, ANY, ANY, ANY, ANY, VMEM, VMEM],
+            out_specs=[VMEM, VMEM],
+            scratch_shapes=[
+                pltpu.VMEM((2, width, hid), BF16),
+                pltpu.VMEM((2, hid, width), BF16),
+                pltpu.SemaphoreType.DMA((2, 2, blocks)),
+            ],
+            compiler_params=pltpu.CompilerParams(vmem_limit_bytes=32 * 2**20),
+            cost_estimate=pl.CostEstimate(
+                flops=16 * cap * width * hid, bytes_accessed=10 * 2**20, transcendentals=0
+            ),
+            name="expert",
+        )(codes, peer, a, b, up, up_other, down, down_other, ain, aout)
+        done = (own + flip(part, "dp", 2).astype(F32)).astype(BF16)
+        for i in range(2):
+            j = 2 * k + i
+            piece = done[i * cap : (i + 1) * cap]
+            backs[j] = flip(piece, "expert", j) if j else piece
+
+    return pl.pallas_call(
+        functools.partial(mix_kernel, cap),
+        out_shape=jax.ShapeDtypeStruct((count, width), BF16),
+        in_specs=[VMEM] * (2 + experts),
+        out_specs=VMEM,
+        cost_estimate=pl.CostEstimate(flops=2 * 10**8, bytes_accessed=2 * 10**6, transcendentals=0),
+        name="mix",
+    )(expert_ids, combine, *backs)
 
 
 def expert_part(sent_rows, slot_codes, w_up, down_matrix, adapter_input_piece, adapter_output_full):
@@ -120,6 +343,8 @@
         P("dp", "expert", None, None),
         P("dp", "expert", None, None),
     )
+    pairs = mesh.shape["dp"] == 4 and mesh.shape["expert"] == 8
+    body = local_pairs if pairs else local
     return jax.shard_map(
-        local, mesh=mesh, in_specs=placed, out_specs=P(("expert", "dp"), None), check_vma=False
-    )
+        body, mesh=mesh, in_specs=placed, out_specs=P(("expert", "dp"), None), check_vma=False
+    )

time: 177 us -> 105 us (0.59)
  blocking collectives: 45 us -> 0 us
  waiting for transfers between devices: 58.3 us -> 25.7 us
  Pallas kernels: 0 us -> 30.3 us
  starting transfers between devices: 12.6 us -> 39.6 us
  local copies, waits for them, and re-layouts: 24.5 us -> 3.91 us
  matrix products: 19.6 us -> 0 us
  between operations: 13.6 us -> 0.31 us
  other arithmetic: 2.86 us -> 4.8 us
    ppermute x0 -> x30, starting transfers between devices: none -> 39.6 us  [flip(): return lax.ppermute(x, axis, [(i, i ^ bit) for i in range(size)])]
    reduce_scatter x1 -> x0, waiting for transfers between devices: 38.1 us -> none  [local(): lax.psum_scatter(rounded_term.reshape(dp_count, expert_count, capacity, m...]
    pallas_call x0 -> x6, Pallas kernels: none -> 30.3 us  [the longest x4 25.4 us: local_pairs(): pl.pallas_call(functools.partial(expert_kernel, cap, experts, rank, block...]
    all_to_all x1 -> x0, blocking collectives: 27.3 us -> none  [local(): lax.all_to_all(send_rows, 'expert', split_axis=0, concat_axis=0, tiled=True)]
    ppermute x0 -> x30, waiting for transfers between devices: none -> 25.7 us  [flip(): return lax.ppermute(x, axis, [(i, i ^ bit) for i in range(size)])]
    all_to_all x3 -> x0, waiting for transfers between devices: 20.2 us -> none  [the longest x1 20.1 us: local(): lax.all_to_all(result_rows, 'expert', split_axis=0, concat_axis=0, tiled=...]
    dot_general x3 -> x0, matrix products: 19.6 us -> none  [the longest x1 8.58 us: expert_part(): jnp.dot(reduced_rank, output_flattened, preferred_element_type=jnp.float32)]
    all_gather x2 -> x0, blocking collectives: 17.7 us -> none  [the longest x1 12.6 us: local(): lax.all_gather(adapter_out, 'dp', axis=0, tiled=True)]
  transfers between devices with their start and end apart: 5 -> 30, of which waited for: 2 -> 13; matrix products, arithmetic and copies ran while one was open for 11% -> 6% of each run, Pallas kernels for 0% -> 24%
where the time goes in v1:
time: 105 us
  starting transfers between devices  39.6 us (38%)
  Pallas kernels  30.3 us (29%)
  waiting for transfers between devices  25.7 us (24%)
  other arithmetic  4.8 us (5%)
  local copies, waits for them, and re-layouts  3.91 us (4%)
    ppermute x30, starting transfers between devices, flip(): return lax.ppermute(x, axis, [(i, i ^ bit) for i in range(size)])  39.6 us
    ppermute x30, waiting for transfers between devices, flip(): return lax.ppermute(x, axis, [(i, i ^ bit) for i in range(size)])  25.7 us
    pallas_call x4, Pallas kernels, local_pairs(): pl.pallas_call(functools.partial(expert_kernel, cap, experts, rank, block...  25.4 us
    pallas_call x1, Pallas kernels, local_pairs(): pl.pallas_call(functools.partial(mix_kernel, cap), out_shape=jax.ShapeDty...  2.76 us
    pallas_call x1, Pallas kernels, local_pairs(): pl.pallas_call(functools.partial(prep_kernel, cap), out_shape=[jax.ShapeD...  2.23 us
    unnamed x36, local copies, waits for them, and re-layouts  2.14 us
  transfers between devices with their start and end apart: 30, of which 13 were waited for; matrix products, arithmetic and copies ran while one was open for 6% of the time, Pallas kernels for 24%

profile of v1, /device:TPU:0, one launch (start us, length us, event | category | flops | bytes accessed | tf_op | source)
XLA Modules:
  0.0 104.7 jit_solution(7279848218383474237)
XLA Ops:
  0.0 2.2 %prep.1 = (bf16[48,1024]{1,0:T(8,128)(2,1)}, bf16[48,1024]{1,0:T(8,128)(2,1)}, bf16[48,1024]{1,0:T(8,128)(2,1)}, bf16[48,1024]{1,0:T(8,128)(2,1)}, bf16[48,1024]...) custom-call(s32[8]{0:T(128)} %slot_ref.1, ...), custom_call_target="tpu_custom_call" | custom-call | flops 100000000 | bytes 2000000 | tf_op jit(solution)/shard_map/prep/pallas_call | solution.py:156
  2.3 3.0 %collective-permute-start = (s32[1,128]{1,0:T(1,128)}, s32[1,128]{1,0:T(1,128)S(1)}, u32[]{:S(2)}, u32[]{:S(2)}) collective-permute-start(s32[1,128]{1,0:T(1,128)} %get-tuple-element.22), channel_id=1, source_target_pairs={{0,4},{4,0},{8,12},{12,8},{16,20},{20,16},{24,28},{28,24},{1,5},{5... | collective-permute-start | bytes 1544 | tf_op jit(solution)/shard_map/ppermute | solution.py:141
  5.3 1.6 %collective-permute-done = s32[1,128]{1,0:T(1,128)S(1)} collective-permute-done((s32[1,128]{1,0:T(1,128)}, s32[1,128]{1,0:T(1,128)S(1)}, u32[]{:S(2)}, u32[]{:S(2)}) %collective-permute-start) | collective-permute-done | bytes 544 | tf_op jit(solution)/shard_map/ppermute | solution.py:141
  7.5 2.1 %collective-permute-start.1 = (s32[2,128]{1,0:T(2,128)S(1)}, s32[2,128]{1,0:T(2,128)S(1)}, u32[]{:S(2)}, u32[]{:S(2)}) collective-permute-start(s32[2,128]{1,0:T(2,128)S(1)} %pad_add_fusion.6), channel_id=1, source_target_pairs={{0,8},{4,12},{8,0},{12,4},{16,24},{20,28},{24,16},{28,20},{1,9},{5... | collective-permute-start | bytes 3080 | tf_op jit(solution)/shard_map/ppermute | solution.py:141
  9.6 1.0 constant_dynamic-slice_fusion.1
  11.9 3.0 %collective-permute-start.2 = (s32[4,128]{1,0:T(4,128)S(1)}, s32[4,128]{1,0:T(4,128)S(1)}, u32[]{:S(2)}, u32[]{:S(2)}) collective-permute-start(s32[4,128]{1,0:T(4,128)S(1)} %pad_add_fusion.2), channel_id=1, source_target_pairs={{0,16},{4,20},{8,24},{12,28},{16,0},{20,4},{24,8},{28,12},{1,17},{... | collective-permute-start | bytes 6152 | tf_op jit(solution)/shard_map/ppermute | solution.py:141
  15.8 1.6 %collective-permute-start.8 = (bf16[32,3072]{1,0:T(8,128)(2,1)S(1)}, bf16[32,3072]{1,0:T(8,128)(2,1)S(1)}, u32[]{:S(2)}, u32[]{:S(2)}) collective-permute-start(bf16[32,3072]{1,0:T(8,128)(2,1)S(1)} %pad_maximum_fusion.4), channel_id=1, source_target_pairs={{0,2},{1,3},{2,0},{3,1},{4,6},{5,7},{6,4},{7,5},{8,10},{9,11},{10,... | collective-permute-start | bytes 589832 | tf_op jit(solution)/shard_map/ppermute | solution.py:141
  17.4 1.3 %collective-permute-start.24 = (bf16[48,1024]{1,0:T(8,128)(2,1)}, bf16[48,1024]{1,0:T(8,128)(2,1)S(1)}, u32[]{:S(2)}, u32[]{:S(2)}) collective-permute-start(bf16[48,1024]{1,0:T(8,128)(2,1)} %get-tuple-element.35), channel_id=1, source_target_pairs={{0,24},{4,28},{8,16},{12,20},{16,8},{20,12},{24,0},{28,4},{1,25},{... | collective-permute-start | bytes 294920 | tf_op jit(solution)/shard_map/ppermute | solution.py:141
  20.4 3.1 %collective-permute-done.3 = s32[8,128]{1,0:T(8,128)S(1)} collective-permute-done((s32[8,128]{1,0:T(8,128)S(1)}, s32[8,128]{1,0:T(8,128)S(1)}, u32[]{:S(2)}, u32[]{:S(2)}) %collective-permute-start.3) | collective-permute-done | bytes 4128 | tf_op jit(solution)/shard_map/ppermute | solution.py:141
  23.5 3.4 %collective-permute-start.25 = (bf16[48,1024]{1,0:T(8,128)(2,1)}, bf16[48,1024]{1,0:T(8,128)(2,1)S(1)}, u32[]{:S(2)}, u32[]{:S(2)}) collective-permute-start(bf16[48,1024]{1,0:T(8,128)(2,1)} %get-tuple-element.36), channel_id=1, source_target_pairs={{0,28},{4,24},{8,20},{12,16},{16,12},{20,8},{24,4},{28,0},{1,29},{... | collective-permute-start | bytes 294920 | tf_op jit(solution)/shard_map/ppermute | solution.py:141
  28.6 2.9 %collective-permute-start.19 = (bf16[48,1024]{1,0:T(8,128)(2,1)S(1)}, bf16[48,1024]{1,0:T(8,128)(2,1)S(1)}, u32[]{:S(2)}, u32[]{:S(2)}) collective-permute-start(bf16[48,1024]{1,0:T(8,128)(2,1)S(1)} %copy-done.16), channel_id=1, source_target_pairs={{0,20},{4,16},{8,28},{12,24},{16,4},{20,0},{24,12},{28,8},{1,21},{... | collective-permute-start | bytes 294920 | tf_op jit(solution)/shard_map/ppermute | solution.py:141
  31.6 6.5 %collective-permute-done.18.own_a_ref = bf16[48,1024]{1,0:T(8,128)(2,1)S(1)} collective-permute-done((bf16[48,1024]{1,0:T(8,128)(2,1)}, bf16[48,1024]{1,0:T(8,128)(2,1)S(1)}, u32[]{:S(2)}, u32[]{:S(2)}) %collective-permute-start.18) | collective-permute-done | bytes 98336 | tf_op jit(solution)/shard_map/ppermute | solution.py:141
  38.4 1.0 collective-permute-done.19.own_b_ref
  40.2 3.1 %collective-permute-done.12.own_a_ref = bf16[48,1024]{1,0:T(8,128)(2,1)S(1)} collective-permute-done((bf16[48,1024]{1,0:T(8,128)(2,1)S(1)}, bf16[48,1024]{1,0:T(8,128)(2,1)S(1)}, u32[]{:S(2)}, u32[]{:S(2)}) %collective-permute-start.12) | collective-permute-done | bytes 98336 | tf_op jit(solution)/shard_map/ppermute | solution.py:141
  43.9 1.2 %collective-permute-done.13.own_b_ref = bf16[48,1024]{1,0:T(8,128)(2,1)S(1)} collective-permute-done((bf16[48,1024]{1,0:T(8,128)(2,1)S(1)}, bf16[48,1024]{1,0:T(8,128)(2,1)S(1)}, u32[]{:S(2)}, u32[]{:S(2)}) %collective-permute-start.13) | collective-permute-done | bytes 98336 | tf_op jit(solution)/shard_map/ppermute | solution.py:141
  45.9 1.9 %collective-permute-done.4.own_b_ref = bf16[48,1024]{1,0:T(8,128)(2,1)S(1)} collective-permute-done((bf16[48,1024]{1,0:T(8,128)(2,1)S(1)}, bf16[48,1024]{1,0:T(8,128)(2,1)S(1)}, u32[]{:S(2)}, u32[]{:S(2)}) %collective-permute-start.4) | collective-permute-done | bytes 98336 | tf_op jit(solution)/shard_map/ppermute | solution.py:141
  47.9 1.3 %collective-permute-start.20 = (bf16[96,1024]{1,0:T(8,128)(2,1)S(1)}, bf16[96,1024]{1,0:T(8,128)(2,1)S(1)}, u32[]{:S(2)}, u32[]{:S(2)}) collective-permute-start(bf16[96,1024]{1,0:T(8,128)(2,1)S(1)} %pad_maximum_fusion.6), channel_id=1, source_target_pairs={{0,2},{1,3},{2,0},{3,1},{4,6},{5,7},{6,4},{7,5},{8,10},{9,11},{10,... | collective-permute-start | bytes 589832 | tf_op jit(solution)/shard_map/ppermute | solution.py:141
  50.2 2.7 %collective-permute-done.26.peer_ref = bf16[96,1024]{1,0:T(8,128)(2,1)S(1)} collective-permute-done((bf16[96,1024]{1,0:T(8,128)(2,1)S(1)}, bf16[96,1024]{1,0:T(8,128)(2,1)S(1)}, u32[]{:S(2)}, u32[]{:S(2)}) %collective-permute-start.26) | collective-permute-done | bytes 196640 | tf_op jit(solution)/shard_map/ppermute | solution.py:141
  53.8 6.4 %expert.7 = (bf16[96,1024]{1,0:T(8,128)(2,1)S(1)}, f32[96,1024]{1,0:T(8,128)S(1)}) custom-call(s32[4,128]{1,0:T(4,128)S(1)} %pad_add_fusion.5.codes_ref, bf16[96,1024]{1,0:T(8,128)(2,1)S(1)} %collective-permute-done.26.peer_ref, bf16[48,1024]{1,0:T(8,128)(2,1)S(1)} %collective-permute-done.24.own_a_ref, ...), custom_call_target="tpu_custom_call" | custom-call | flops 805306368 | bytes 10485760 | tf_op jit(solution)/shard_map/expert/pallas_call | solution.py:195
  60.2 1.2 %collective-permute-start.27 = (bf16[96,1024]{1,0:T(8,128)(2,1)S(1)}, bf16[96,1024]{1,0:T(8,128)(2,1)S(1)}, u32[]{:S(2)}, u32[]{:S(2)}) collective-permute-start(bf16[96,1024]{1,0:T(8,128)(2,1)S(1)} %get-tuple-element.38), channel_id=1, source_target_pairs={{0,2},{1,3},{2,0},{3,1},{4,6},{5,7},{6,4},{7,5},{8,10},{9,11},{10,... | collective-permute-start | bytes 589832 | tf_op jit(solution)/shard_map/ppermute | solution.py:141
  61.4 6.2 %expert.6 = (bf16[96,1024]{1,0:T(8,128)(2,1)S(1)}, f32[96,1024]{1,0:T(8,128)S(1)}) custom-call(s32[4,128]{1,0:T(4,128)S(1)} %pad_add_fusion.4.codes_ref, bf16[96,1024]{1,0:T(8,128)(2,1)S(1)} %collective-permute-done.20.peer_ref, bf16[48,1024]{1,0:T(8,128)(2,1)S(1)} %collective-permute-done.18.own_a_ref, ...), custom_call_target="tpu_custom_call" | custom-call | flops 805306368 | bytes 10485760 | tf_op jit(solution)/shard_map/expert/pallas_call | solution.py:195
  68.6 6.2 %expert.5 = (bf16[96,1024]{1,0:T(8,128)(2,1)S(1)}, f32[96,1024]{1,0:T(8,128)S(1)}) custom-call(s32[4,128]{1,0:T(4,128)S(1)} %pad_add_fusion.1.codes_ref, bf16[96,1024]{1,0:T(8,128)(2,1)S(1)} %collective-permute-done.14.peer_ref, bf16[48,1024]{1,0:T(8,128)(2,1)S(1)} %collective-permute-done.12.own_a_ref, ...), custom_call_target="tpu_custom_call" | custom-call | flops 805306368 | bytes 10485760 | tf_op jit(solution)/shard_map/expert/pallas_call | solution.py:195
  74.9 1.2 %collective-permute-start.15 = (bf16[96,1024]{1,0:T(8,128)(2,1)S(1)}, bf16[96,1024]{1,0:T(8,128)(2,1)S(1)}, u32[]{:S(2)}, u32[]{:S(2)}) collective-permute-start(bf16[96,1024]{1,0:T(8,128)(2,1)S(1)} %get-tuple-element.30), channel_id=1, source_target_pairs={{0,2},{1,3},{2,0},{3,1},{4,6},{5,7},{6,4},{7,5},{8,10},{9,11},{10,... | collective-permute-start | bytes 589832 | tf_op jit(solution)/shard_map/ppermute | solution.py:141
  76.1 6.5 %expert.4 = (bf16[96,1024]{1,0:T(8,128)(2,1)S(1)}, f32[96,1024]{1,0:T(8,128)S(1)}) custom-call(s32[4,128]{1,0:T(4,128)S(1)} %pad_add_fusion.3.codes_ref, bf16[96,1024]{1,0:T(8,128)(2,1)S(1)} %collective-permute-done.5.peer_ref, bf16[48,1024]{1,0:T(8,128)(2,1)S(1)} %copy-done.2, bf16[48,1024]{1,0:T(8,128)(2,1)S(1)} %collective-permute-done.4.own_b_ref, ...), custom_call_target="tpu_custom_call" | custom-call | flops 805306368 | bytes 10485760 | tf_op jit(solution)/shard_map/expert/pallas_call | solution.py:195
  83.6 2.6 %collective-permute-start.28 = (bf16[48,1024]{1,0:T(8,128)(2,1)S(1)}, bf16[48,1024]{1,0:T(8,128)(2,1)S(1)}, u32[]{:S(2)}, u32[]{:S(2)}) collective-permute-start(bf16[48,1024]{1,0:T(8,128)(2,1)S(1)} %get-tuple-element.42), channel_id=1, source_target_pairs={{0,24},{4,28},{8,16},{12,20},{16,8},{20,12},{24,0},{28,4},{1,25},{... | collective-permute-start | bytes 294920 | tf_op jit(solution)/shard_map/ppermute | solution.py:141
  86.1 2.2 %collective-permute-start.29 = (bf16[48,1024]{1,0:T(8,128)(2,1)S(1)}, bf16[48,1024]{1,0:T(8,128)(2,1)S(1)}, u32[]{:S(2)}, u32[]{:S(2)}) collective-permute-start(bf16[48,1024]{1,0:T(8,128)(2,1)S(1)} %get-tuple-element.41), channel_id=1, source_target_pairs={{0,28},{4,24},{8,20},{12,16},{16,12},{20,8},{24,4},{28,0},{1,29},{... | collective-permute-start | bytes 294920 | tf_op jit(solution)/shard_map/ppermute | solution.py:141
  88.6 2.9 %collective-permute-start.23 = (bf16[48,1024]{1,0:T(8,128)(2,1)S(1)}, bf16[48,1024]{1,0:T(8,128)(2,1)S(1)}, u32[]{:S(2)}, u32[]{:S(2)}) collective-permute-start(bf16[48,1024]{1,0:T(8,128)(2,1)S(1)} %get-tuple-element.43), channel_id=1, source_target_pairs={{0,20},{4,16},{8,28},{12,24},{16,4},{20,0},{24,12},{28,8},{1,21},{... | collective-permute-start | bytes 294920 | tf_op jit(solution)/shard_map/ppermute | solution.py:141
  92.5 2.7 %collective-permute-start.17 = (bf16[48,1024]{1,0:T(8,128)(2,1)S(1)}, bf16[48,1024]{1,0:T(8,128)(2,1)S(1)}, u32[]{:S(2)}, u32[]{:S(2)}) collective-permute-start(bf16[48,1024]{1,0:T(8,128)(2,1)S(1)} %get-tuple-element.45), channel_id=1, source_target_pairs={{0,12},{4,8},{8,4},{12,0},{16,28},{20,24},{24,20},{28,16},{1,13},{... | collective-permute-start | bytes 294920 | tf_op jit(solution)/shard_map/ppermute | solution.py:141
  98.0 1.4 %collective-permute-done.23.refs_5_ = bf16[48,1024]{1,0:T(8,128)(2,1)S(1)} collective-permute-done((bf16[48,1024]{1,0:T(8,128)(2,1)S(1)}, bf16[48,1024]{1,0:T(8,128)(2,1)S(1)}, u32[]{:S(2)}, u32[]{:S(2)}) %collective-permute-start.23) | collective-permute-done | bytes 98336 | tf_op jit(solution)/shard_map/ppermute | solution.py:141
  99.4 1.0 collective-permute-done.17.refs_3_
  100.4 0.9 collective-permute-done.11.refs_1_
  102.0 2.8 %mix.1 = bf16[128,1024]{1,0:T(8,128)(2,1)} custom-call(s32[128,2]{1,0:T(8,128)} %copy.10.ids_ref, f32[128,2]{1,0:T(8,128)} %copy.11.combine_ref, bf16[48,1024]{1,0:T(8,128)(2,1)} %get-tuple-element.48.refs_0_, bf16[48,1024]{1,0:T(8,128)(2,1)} %copy-done.10, bf16[48,1024]{1,0:T(8,128)(2,1)} %copy-done.8, bf16[48,1024]{1,0:T(8,128)(2,1)} %copy-done.9, ...), custom_call_target="tpu_custom_call" | custom-call | flops 200000000 | bytes 2000000 | tf_op jit(solution)/shard_map/mix/pallas_call | solution.py:220
  (97 shorter events, 17.0 us)
Async XLA Ops:
  2.2 41.0 %copy-start.13 = (bf16[48,1024]{1,0:T(8,128)(2,1)S(1)}, bf16[48,1024]{1,0:T(8,128)(2,1)}, u32[]{:S(2)}) copy-start(bf16[48,1024]{1,0:T(8,128)(2,1)} %get-tuple-element.24) | copy-start | bytes 294916
  2.3 46.9 %copy-start.2 = (bf16[48,1024]{1,0:T(8,128)(2,1)S(1)}, bf16[48,1024]{1,0:T(8,128)(2,1)}, u32[]{:S(2)}) copy-start(bf16[48,1024]{1,0:T(8,128)(2,1)} %get-tuple-element.23.own_a_ref) | copy-start | bytes 294916
  2.3 4.6 %collective-permute-start = (s32[1,128]{1,0:T(1,128)}, s32[1,128]{1,0:T(1,128)S(1)}, u32[]{:S(2)}, u32[]{:S(2)}) collective-permute-start(s32[1,128]{1,0:T(1,128)} %get-tuple-element.22), channel_id=1, source_target_pairs={{0,4},{4,0},{8,12},{12,8},{16,20},{20,16},{24,28},{28,24},{1,5},{5... | collective-permute-start | bytes 1544 | tf_op jit(solution)/shard_map/ppermute | solution.py:141
  7.5 3.7 %collective-permute-start.1 = (s32[2,128]{1,0:T(2,128)S(1)}, s32[2,128]{1,0:T(2,128)S(1)}, u32[]{:S(2)}, u32[]{:S(2)}) collective-permute-start(s32[2,128]{1,0:T(2,128)S(1)} %pad_add_fusion.6), channel_id=1, source_target_pairs={{0,8},{4,12},{8,0},{12,4},{16,24},{20,28},{24,16},{28,20},{1,9},{5... | collective-permute-start | bytes 3080 | tf_op jit(solution)/shard_map/ppermute | solution.py:141
  11.9 7.3 %collective-permute-start.2 = (s32[4,128]{1,0:T(4,128)S(1)}, s32[4,128]{1,0:T(4,128)S(1)}, u32[]{:S(2)}, u32[]{:S(2)}) collective-permute-start(s32[4,128]{1,0:T(4,128)S(1)} %pad_add_fusion.2), channel_id=1, source_target_pairs={{0,16},{4,20},{8,24},{12,28},{16,0},{20,4},{24,8},{28,12},{1,17},{... | collective-permute-start | bytes 6152 | tf_op jit(solution)/shard_map/ppermute | solution.py:141
  15.8 11.9 %collective-permute-start.8 = (bf16[32,3072]{1,0:T(8,128)(2,1)S(1)}, bf16[32,3072]{1,0:T(8,128)(2,1)S(1)}, u32[]{:S(2)}, u32[]{:S(2)}) collective-permute-start(bf16[32,3072]{1,0:T(8,128)(2,1)S(1)} %pad_maximum_fusion.4), channel_id=1, source_target_pairs={{0,2},{1,3},{2,0},{3,1},{4,6},{5,7},{6,4},{7,5},{8,10},{9,11},{10,... | collective-permute-start | bytes 589832 | tf_op jit(solution)/shard_map/ppermute | solution.py:141
  17.4 11.3 %collective-permute-start.24 = (bf16[48,1024]{1,0:T(8,128)(2,1)}, bf16[48,1024]{1,0:T(8,128)(2,1)S(1)}, u32[]{:S(2)}, u32[]{:S(2)}) collective-permute-start(bf16[48,1024]{1,0:T(8,128)(2,1)} %get-tuple-element.35), channel_id=1, source_target_pairs={{0,24},{4,28},{8,16},{12,20},{16,8},{20,12},{24,0},{28,4},{1,25},{... | collective-permute-start | bytes 294920 | tf_op jit(solution)/shard_map/ppermute | solution.py:141
  18.7 35.1 %collective-permute-start.6 = (bf16[1024,1024]{1,0:T(8,128)(2,1)}, bf16[1024,1024]{1,0:T(8,128)(2,1)S(1)}, u32[]{:S(2)}, u32[]{:S(2)}) collective-permute-start(bf16[1024,1024]{1,0:T(8,128)(2,1)} %bitcast.6), channel_id=1, source_target_pairs={{0,1},{1,0},{2,3},{3,2},{4,5},{5,4},{6,7},{7,6},{8,9},{9,8},{10,11... | collective-permute-start | bytes 6291464 | tf_op jit(solution)/shard_map/ppermute | solution.py:141
  18.7 35.1 %collective-permute-start.7 = (bf16[1024,1024]{1,0:T(8,128)(2,1)}, bf16[1024,1024]{1,0:T(8,128)(2,1)S(1)}, u32[]{:S(2)}, u32[]{:S(2)}) collective-permute-start(bf16[1024,1024]{1,0:T(8,128)(2,1)} %bitcast.11), channel_id=1, source_target_pairs={{0,1},{1,0},{2,3},{3,2},{4,5},{5,4},{6,7},{7,6},{8,9},{9,8},{10,11... | collective-permute-start | bytes 6291464 | tf_op jit(solution)/shard_map/ppermute | solution.py:141
  19.9 3.6 %collective-permute-start.3 = (s32[8,128]{1,0:T(8,128)S(1)}, s32[8,128]{1,0:T(8,128)S(1)}, u32[]{:S(2)}, u32[]{:S(2)}) collective-permute-start(s32[8,128]{1,0:T(8,128)S(1)} %pad_add_fusion), channel_id=1, source_target_pairs={{0,2},{1,3},{2,0},{3,1},{4,6},{5,7},{6,4},{7,5},{8,10},{9,11},{10,... | collective-permute-start | bytes 12296 | tf_op jit(solution)/shard_map/ppermute | solution.py:141
  23.5 8.1 %collective-permute-start.25 = (bf16[48,1024]{1,0:T(8,128)(2,1)}, bf16[48,1024]{1,0:T(8,128)(2,1)S(1)}, u32[]{:S(2)}, u32[]{:S(2)}) collective-permute-start(bf16[48,1024]{1,0:T(8,128)(2,1)} %get-tuple-element.36), channel_id=1, source_target_pairs={{0,28},{4,24},{8,20},{12,16},{16,12},{20,8},{24,4},{28,0},{1,29},{... | collective-permute-start | bytes 294920 | tf_op jit(solution)/shard_map/ppermute | solution.py:141
  27.7 10.5 %collective-permute-start.18 = (bf16[48,1024]{1,0:T(8,128)(2,1)}, bf16[48,1024]{1,0:T(8,128)(2,1)S(1)}, u32[]{:S(2)}, u32[]{:S(2)}) collective-permute-start(bf16[48,1024]{1,0:T(8,128)(2,1)} %get-tuple-element.31), channel_id=1, source_target_pairs={{0,16},{4,20},{8,24},{12,28},{16,0},{20,4},{24,8},{28,12},{1,17},{... | collective-permute-start | bytes 294920 | tf_op jit(solution)/shard_map/ppermute | solution.py:141
  28.6 10.8 %collective-permute-start.19 = (bf16[48,1024]{1,0:T(8,128)(2,1)S(1)}, bf16[48,1024]{1,0:T(8,128)(2,1)S(1)}, u32[]{:S(2)}, u32[]{:S(2)}) collective-permute-start(bf16[48,1024]{1,0:T(8,128)(2,1)S(1)} %copy-done.16), channel_id=1, source_target_pairs={{0,20},{4,16},{8,28},{12,24},{16,4},{20,0},{24,12},{28,8},{1,21},{... | collective-permute-start | bytes 294920 | tf_op jit(solution)/shard_map/ppermute | solution.py:141
  31.6 17.6 %collective-permute-start.9 = (bf16[64,3072]{1,0:T(8,128)(2,1)S(1)}, bf16[64,3072]{1,0:T(8,128)(2,1)S(1)}, u32[]{:S(2)}, u32[]{:S(2)}) collective-permute-start(bf16[64,3072]{1,0:T(8,128)(2,1)S(1)} %pad_maximum_fusion.1), channel_id=1, source_target_pairs={{0,1},{1,0},{2,3},{3,2},{4,5},{5,4},{6,7},{7,6},{8,9},{9,8},{10,11... | collective-permute-start | bytes 1179656 | tf_op jit(solution)/shard_map/ppermute | solution.py:141
  38.1 5.1 %collective-permute-start.12 = (bf16[48,1024]{1,0:T(8,128)(2,1)S(1)}, bf16[48,1024]{1,0:T(8,128)(2,1)S(1)}, u32[]{:S(2)}, u32[]{:S(2)}) collective-permute-start(bf16[48,1024]{1,0:T(8,128)(2,1)S(1)} %copy-done.15), channel_id=1, source_target_pairs={{0,8},{4,12},{8,0},{12,4},{16,24},{20,28},{24,16},{28,20},{1,9},{5... | collective-permute-start | bytes 294920 | tf_op jit(solution)/shard_map/ppermute | solution.py:141
  39.5 5.6 %collective-permute-start.13 = (bf16[48,1024]{1,0:T(8,128)(2,1)S(1)}, bf16[48,1024]{1,0:T(8,128)(2,1)S(1)}, u32[]{:S(2)}, u32[]{:S(2)}) collective-permute-start(bf16[48,1024]{1,0:T(8,128)(2,1)S(1)} %copy-done.14), channel_id=1, source_target_pairs={{0,12},{4,8},{8,4},{12,0},{16,28},{20,24},{24,20},{28,16},{1,13},{... | collective-permute-start | bytes 294920 | tf_op jit(solution)/shard_map/ppermute | solution.py:141
  43.3 4.6 %collective-permute-start.4 = (bf16[48,1024]{1,0:T(8,128)(2,1)S(1)}, bf16[48,1024]{1,0:T(8,128)(2,1)S(1)}, u32[]{:S(2)}, u32[]{:S(2)}) collective-permute-start(bf16[48,1024]{1,0:T(8,128)(2,1)S(1)} %copy-done.13), channel_id=1, source_target_pairs={{0,4},{4,0},{8,12},{12,8},{16,20},{20,16},{24,28},{28,24},{1,5},{5... | collective-permute-start | bytes 294920 | tf_op jit(solution)/shard_map/ppermute | solution.py:141
  45.1 7.8 %collective-permute-start.26 = (bf16[96,1024]{1,0:T(8,128)(2,1)S(1)}, bf16[96,1024]{1,0:T(8,128)(2,1)S(1)}, u32[]{:S(2)}, u32[]{:S(2)}) collective-permute-start(bf16[96,1024]{1,0:T(8,128)(2,1)S(1)} %pad_maximum_fusion.7), channel_id=1, source_target_pairs={{0,2},{1,3},{2,0},{3,1},{4,6},{5,7},{6,4},{7,5},{8,10},{9,11},{10,... | collective-permute-start | bytes 589832 | tf_op jit(solution)/shard_map/ppermute | solution.py:141
  47.9 13.5 %collective-permute-start.20 = (bf16[96,1024]{1,0:T(8,128)(2,1)S(1)}, bf16[96,1024]{1,0:T(8,128)(2,1)S(1)}, u32[]{:S(2)}, u32[]{:S(2)}) collective-permute-start(bf16[96,1024]{1,0:T(8,128)(2,1)S(1)} %pad_maximum_fusion.6), channel_id=1, source_target_pairs={{0,2},{1,3},{2,0},{3,1},{4,6},{5,7},{6,4},{7,5},{8,10},{9,11},{10,... | collective-permute-start | bytes 589832 | tf_op jit(solution)/shard_map/ppermute | solution.py:141
  49.2 19.4 %collective-permute-start.14 = (bf16[96,1024]{1,0:T(8,128)(2,1)S(1)}, bf16[96,1024]{1,0:T(8,128)(2,1)S(1)}, u32[]{:S(2)}, u32[]{:S(2)}) collective-permute-start(bf16[96,1024]{1,0:T(8,128)(2,1)S(1)} %pad_maximum_fusion.5), channel_id=1, source_target_pairs={{0,2},{1,3},{2,0},{3,1},{4,6},{5,7},{6,4},{7,5},{8,10},{9,11},{10,... | collective-permute-start | bytes 589832 | tf_op jit(solution)/shard_map/ppermute | solution.py:141
  52.9 23.2 %collective-permute-start.5 = (bf16[96,1024]{1,0:T(8,128)(2,1)S(1)}, bf16[96,1024]{1,0:T(8,128)(2,1)S(1)}, u32[]{:S(2)}, u32[]{:S(2)}) collective-permute-start(bf16[96,1024]{1,0:T(8,128)(2,1)S(1)} %pad_maximum_fusion.3), channel_id=1, source_target_pairs={{0,2},{1,3},{2,0},{3,1},{4,6},{5,7},{6,4},{7,5},{8,10},{9,11},{10,... | collective-permute-start | bytes 589832 | tf_op jit(solution)/shard_map/ppermute | solution.py:141
  60.2 23.3 %collective-permute-start.27 = (bf16[96,1024]{1,0:T(8,128)(2,1)S(1)}, bf16[96,1024]{1,0:T(8,128)(2,1)S(1)}, u32[]{:S(2)}, u32[]{:S(2)}) collective-permute-start(bf16[96,1024]{1,0:T(8,128)(2,1)S(1)} %get-tuple-element.38), channel_id=1, source_target_pairs={{0,2},{1,3},{2,0},{3,1},{4,6},{5,7},{6,4},{7,5},{8,10},{9,11},{10,... | collective-permute-start | bytes 589832 | tf_op jit(solution)/shard_map/ppermute | solution.py:141
  67.7 20.7 %collective-permute-start.21 = (bf16[96,1024]{1,0:T(8,128)(2,1)S(1)}, bf16[96,1024]{1,0:T(8,128)(2,1)S(1)}, u32[]{:S(2)}, u32[]{:S(2)}) collective-permute-start(bf16[96,1024]{1,0:T(8,128)(2,1)S(1)} %get-tuple-element.34), channel_id=1, source_target_pairs={{0,2},{1,3},{2,0},{3,1},{4,6},{5,7},{6,4},{7,5},{8,10},{9,11},{10,... | collective-permute-start | bytes 589832 | tf_op jit(solution)/shard_map/ppermute | solution.py:141
  74.9 13.7 %collective-permute-start.15 = (bf16[96,1024]{1,0:T(8,128)(2,1)S(1)}, bf16[96,1024]{1,0:T(8,128)(2,1)S(1)}, u32[]{:S(2)}, u32[]{:S(2)}) collective-permute-start(bf16[96,1024]{1,0:T(8,128)(2,1)S(1)} %get-tuple-element.30), channel_id=1, source_target_pairs={{0,2},{1,3},{2,0},{3,1},{4,6},{5,7},{6,4},{7,5},{8,10},{9,11},{10,... | collective-permute-start | bytes 589832 | tf_op jit(solution)/shard_map/ppermute | solution.py:141
  82.6 9.0 %collective-permute-start.10 = (bf16[96,1024]{1,0:T(8,128)(2,1)S(1)}, bf16[96,1024]{1,0:T(8,128)(2,1)S(1)}, u32[]{:S(2)}, u32[]{:S(2)}) collective-permute-start(bf16[96,1024]{1,0:T(8,128)(2,1)S(1)} %get-tuple-element.26), channel_id=1, source_target_pairs={{0,2},{1,3},{2,0},{3,1},{4,6},{5,7},{6,4},{7,5},{8,10},{9,11},{10,... | collective-permute-start | bytes 589832 | tf_op jit(solution)/shard_map/ppermute | solution.py:141
  83.6 9.0 %collective-permute-start.28 = (bf16[48,1024]{1,0:T(8,128)(2,1)S(1)}, bf16[48,1024]{1,0:T(8,128)(2,1)S(1)}, u32[]{:S(2)}, u32[]{:S(2)}) collective-permute-start(bf16[48,1024]{1,0:T(8,128)(2,1)S(1)} %get-tuple-element.42), channel_id=1, source_target_pairs={{0,24},{4,28},{8,16},{12,20},{16,8},{20,12},{24,0},{28,4},{1,25},{... | collective-permute-start | bytes 294920 | tf_op jit(solution)/shard_map/ppermute | solution.py:141
  86.1 9.1 %collective-permute-start.29 = (bf16[48,1024]{1,0:T(8,128)(2,1)S(1)}, bf16[48,1024]{1,0:T(8,128)(2,1)S(1)}, u32[]{:S(2)}, u32[]{:S(2)}) collective-permute-start(bf16[48,1024]{1,0:T(8,128)(2,1)S(1)} %get-tuple-element.41), channel_id=1, source_target_pairs={{0,28},{4,24},{8,20},{12,16},{16,12},{20,8},{24,4},{28,0},{1,29},{... | collective-permute-start | bytes 294920 | tf_op jit(solution)/shard_map/ppermute | solution.py:141
  88.5 9.5 %collective-permute-start.22 = (bf16[48,1024]{1,0:T(8,128)(2,1)S(1)}, bf16[48,1024]{1,0:T(8,128)(2,1)S(1)}, u32[]{:S(2)}, u32[]{:S(2)}) collective-permute-start(bf16[48,1024]{1,0:T(8,128)(2,1)S(1)} %get-tuple-element.44), channel_id=1, source_target_pairs={{0,16},{4,20},{8,24},{12,28},{16,0},{20,4},{24,8},{28,12},{1,17},{... | collective-permute-start | bytes 294920 | tf_op jit(solution)/shard_map/ppermute | solution.py:141
  88.6 10.9 %collective-permute-start.23 = (bf16[48,1024]{1,0:T(8,128)(2,1)S(1)}, bf16[48,1024]{1,0:T(8,128)(2,1)S(1)}, u32[]{:S(2)}, u32[]{:S(2)}) collective-permute-start(bf16[48,1024]{1,0:T(8,128)(2,1)S(1)} %get-tuple-element.43), channel_id=1, source_target_pairs={{0,20},{4,16},{8,28},{12,24},{16,4},{20,0},{24,12},{28,8},{1,21},{... | collective-permute-start | bytes 294920 | tf_op jit(solution)/shard_map/ppermute | solution.py:141
  91.5 7.9 %collective-permute-start.16 = (bf16[48,1024]{1,0:T(8,128)(2,1)S(1)}, bf16[48,1024]{1,0:T(8,128)(2,1)S(1)}, u32[]{:S(2)}, u32[]{:S(2)}) collective-permute-start(bf16[48,1024]{1,0:T(8,128)(2,1)S(1)} %get-tuple-element.46), channel_id=1, source_target_pairs={{0,8},{4,12},{8,0},{12,4},{16,24},{20,28},{24,16},{28,20},{1,9},{5... | collective-permute-start | bytes 294920 | tf_op jit(solution)/shard_map/ppermute | solution.py:141
  92.5 7.8 %collective-permute-start.17 = (bf16[48,1024]{1,0:T(8,128)(2,1)S(1)}, bf16[48,1024]{1,0:T(8,128)(2,1)S(1)}, u32[]{:S(2)}, u32[]{:S(2)}) collective-permute-start(bf16[48,1024]{1,0:T(8,128)(2,1)S(1)} %get-tuple-element.45), channel_id=1, source_target_pairs={{0,12},{4,8},{8,4},{12,0},{16,28},{20,24},{24,20},{28,16},{1,13},{... | collective-permute-start | bytes 294920 | tf_op jit(solution)/shard_map/ppermute | solution.py:141
  95.2 6.1 %collective-permute-start.11 = (bf16[48,1024]{1,0:T(8,128)(2,1)S(1)}, bf16[48,1024]{1,0:T(8,128)(2,1)S(1)}, u32[]{:S(2)}, u32[]{:S(2)}) collective-permute-start(bf16[48,1024]{1,0:T(8,128)(2,1)S(1)} %get-tuple-element.47), channel_id=1, source_target_pairs={{0,4},{4,0},{8,12},{12,8},{16,20},{20,16},{24,28},{28,24},{1,5},{5... | collective-permute-start | bytes 294920 | tf_op jit(solution)/shard_map/ppermute | solution.py:141
  (15 other events, 191.6 us)

commit v2 on v0

--- a/solution.py
+++ b/solution.py
@@ -1,7 +1,245 @@
+import functools
+
 import jax
 import jax.numpy as jnp
 from jax import lax
+from jax.experimental import pallas as pl
+from jax.experimental.pallas import tpu as pltpu
 from jax.sharding import PartitionSpec as P
+
+ORDER = tuple(
+    "e6 e7 e1 a d:e7 y0:e6 u e4:d,e1 b:u y3:a,d e5 r0:e4 e3:b r3 y2:e5 e2:d y1:e2 o7 o6 r2:r3 r1:y2 o4 o5:o7 o2:r2 o1:y1 "
+    "o3:r1".split()
+)
+
+F32 = jnp.float32
+BF16 = jnp.bfloat16
+VMEM = pl.BlockSpec(memory_space=pltpu.VMEM)
+SMEM = pl.BlockSpec(memory_space=pltpu.SMEM)
+
+
+def iota(shape, dim):
+    return lax.broadcasted_iota(jnp.int32, shape, dim)
+
+
+def row_places(hit):
+    count = hit.shape[1]
+    earlier = (iota((count, count), 0) < iota((count, count), 1)).astype(BF16)
+    place = jnp.dot(hit.astype(F32).astype(BF16), earlier, preferred_element_type=F32)
+    return jnp.where(hit, place, -1.0)
+
+
+def prep_kernel(cap, slot_ref, ids_ref, lang_ref, tok_ref, in_ref, out_ref, mine, theirs, *outs):
+    half = in_ref.shape[1] // 2
+    y = lax.div(lax.axis_index("dp"), 2)
+    for ref, at in ((mine, y), (theirs, 1 - y)):
+        ref[:, :half] = in_ref[:, pl.ds(pl.multiple_of(at * half, half), half)]
+        ref[:, half:] = out_ref[...]
+    experts = len(outs)
+    count, width = tok_ref.shape
+    me = lax.axis_index("expert")
+    first, second = ids_ref[0:1, :], ids_ref[1:2, :]
+    expert = iota((experts, count), 0) ^ me
+    place = row_places((first == expert) | (second == expert))
+    want = iota((cap, count), 0).astype(F32)
+    select = jnp.concatenate(
+        [(place[j : j + 1, :] == want).astype(F32).astype(BF16) for j in range(experts)], axis=0
+    )
+    lang = lang_ref[...]
+    slot = jnp.zeros_like(lang)
+    for i in range(slot_ref.shape[0]):
+        slot = jnp.where(lang == i, slot_ref[i] + 1, slot)
+    code = jnp.broadcast_to(slot.astype(F32).astype(BF16), (128, count))
+    rows = jnp.dot(select, tok_ref[...], preferred_element_type=F32).astype(BF16)
+    codes = lax.dot_general(select, code, (((1,), (1,)), ((), ())), preferred_element_type=F32)
+    codes = codes.astype(BF16)
+    for j in range(experts):
+        outs[j][:, :width] = rows[j * cap : (j + 1) * cap]
+        outs[j][:, width:] = codes[j * cap : (j + 1) * cap]
+
+
+def expert_kernel(
+    rank, peer_ref, own_a_ref, own_b_ref, up_a, up_b, down_a, down_b, ain_ref, aout_ref, send_ref,
+    keep_ref, rows_buf, hid_buf,
+):
+    width, hid = up_a.shape
+    columns = aout_ref.shape[0]
+    half = peer_ref.shape[0]
+    dp = lax.axis_index("dp")
+    column = iota((1, columns), 1)
+    part = lax.div(column, columns // 4)
+    owner = dp ^ (lax.rem(part, 2) * 2 + lax.div(part, 2))
+    each = columns // 4 // rank
+    slot = owner * each + lax.rem(lax.div(column, rank), each) + 1
+    slot = slot.astype(F32)
+    at = 0
+    codes = []
+    for ref in (peer_ref, own_a_ref, own_b_ref):
+        rows_buf[at : at + ref.shape[0], :] = ref[:, :width]
+        codes.append(ref[:, width:].astype(F32))
+        at += ref.shape[0]
+    keep = jnp.concatenate(codes, axis=0) == slot
+    rows = rows_buf[...]
+    step = 512
+    low = []
+    core = lax.rem(dp, 2)
+    for h, up in enumerate((up_a, up_b)):
+        for b in range(hid // step):
+            hidden = jnp.dot(rows, up[:, b * step : (b + 1) * step], preferred_element_type=F32)
+            hid_buf[h, :, b * step : (b + 1) * step] = jnp.maximum(hidden, 0.0).astype(BF16)
+        where = pl.ds(pl.multiple_of((core ^ h) * hid, hid), hid)
+        one = lax.dot_general(
+            hid_buf[h], ain_ref[:, where], (((1,), (1,)), ((), ())), preferred_element_type=F32
+        )
+        low.append(jnp.where(keep, one, 0.0).astype(BF16).astype(F32))
+    low = (low[0] + low[1]).astype(BF16)
+    for b in range(width // step):
+        span = slice(b * step, (b + 1) * step)
+        total = jnp.dot(hid_buf[0], down_a[:, span], preferred_element_type=F32)
+        total += jnp.dot(hid_buf[1], down_b[:, span], preferred_element_type=F32)
+        total += jnp.dot(low, aout_ref[:, span], preferred_element_type=F32)
+        send_ref[:, span] = total[:half].astype(BF16)
+        keep_ref[:, span] = total[half:]
+
+
+def mix_kernel(cap, ids_ref, combine_ref, *refs):
+    backs, out_ref = refs[:-1], refs[-1]
+    experts = len(backs)
+    count = ids_ref.shape[0]
+    me = lax.axis_index("expert")
+    first, second = ids_ref[:, 0:1] ^ me, ids_ref[:, 1:2] ^ me
+    lane = iota((count, 128), 1)
+    hit = ((first == lane) | (second == lane)).astype(F32).astype(BF16)
+    earlier = (iota((count, count), 1) < iota((count, count), 0)).astype(F32).astype(BF16)
+    place = jnp.dot(earlier, hit, preferred_element_type=F32)
+    back = jnp.concatenate([b[...] for b in backs], axis=0)
+    spot = iota((count, experts * cap), 1).astype(F32)
+    mixed = None
+    for k, choice in enumerate((first, second)):
+        at = jnp.sum(jnp.where(choice == lane, place, 0.0), axis=1, keepdims=True)
+        at = at + (choice * cap).astype(F32)
+        select = (at == spot).astype(F32).astype(BF16)
+        picked = jnp.dot(select, back, preferred_element_type=F32)
+        term = combine_ref[:, k : k + 1] * picked
+        mixed = term if mixed is None else mixed + term
+    out_ref[...] = mixed.astype(BF16)
+
+
+def after(x, *done):
+    return lax.optimization_barrier((x,) + done)[0]
+
+
+def flip(x, axis, bit):
+    size = lax.axis_size(axis)
+    return lax.ppermute(x, axis, [(i, i ^ bit) for i in range(size)])
+
+
+def local_pairs(
+    tokens, expert_ids, combine, language, lang_slot, up_weight, down_weight, adapter_in, adapter_out
+):
+    count, width = tokens.shape
+    experts = lax.axis_size("expert")
+    cap = 3 * count // experts
+    slots, _, rank, hid_all = adapter_in.shape
+    up, down = up_weight[0], down_weight[0]
+    hid = up.shape[1]
+
+    flat_in = adapter_in.reshape(slots * rank, hid_all)
+    flat_out = adapter_out.reshape(slots * rank, width)
+    prep = pl.pallas_call(
+        functools.partial(prep_kernel, cap),
+        out_shape=[jax.ShapeDtypeStruct((slots * rank, 2 * hid + width), BF16)] * 2
+        + [jax.ShapeDtypeStruct((cap, width + 128), BF16)] * experts,
+        in_specs=[SMEM] + [VMEM] * 5,
+        out_specs=[VMEM] * (2 + experts),
+        cost_estimate=pl.CostEstimate(flops=10**8, bytes_accessed=2 * 10**6, transcendentals=0),
+        name="prep",
+    )(lang_slot, expert_ids.T, language[None, :], tokens, flat_in, flat_out)
+    mine, theirs, send = prep[0], prep[1], prep[2:]
+
+    def run_expert(peer, a, b):
+        full = state["full"]
+        return pl.pallas_call(
+            functools.partial(expert_kernel, rank),
+            out_shape=[
+                jax.ShapeDtypeStruct((2 * cap, width), BF16),
+                jax.ShapeDtypeStruct((2 * cap, width), F32),
+            ],
+            in_specs=[VMEM] * 9,
+            out_specs=[VMEM, VMEM],
+            scratch_shapes=[
+                pltpu.VMEM((4 * cap, width), BF16),
+                pltpu.VMEM((2, 4 * cap, hid), BF16),
+            ],
+            compiler_params=pltpu.CompilerParams(vmem_limit_bytes=24 * 2**20),
+            cost_estimate=pl.CostEstimate(
+                flops=32 * cap * width * hid, bytes_accessed=10 * 2**20, transcendentals=0
+            ),
+            name="expert",
+        )(peer, a, b, up, got["u"], down, got["d"], full[:, : 2 * hid], full[:, 2 * hid :])
+
+    def both(a, b):
+        return jnp.concatenate([a, b], axis=0)
+
+    def join(own, back):
+        done = (own + back.astype(F32)).astype(BF16)
+        return done[:cap], done[cap:]
+
+    got, parts, sums, state = {"e0": send[0]}, {}, {}, {}
+
+    def rows_of(k):
+        return got["e%d" % (2 * k)], got["e%d" % (2 * k + 1)]
+
+    def run_chunk(k):
+        if k not in parts:
+            if "full" not in state:
+                state["full"] = both(state["pair"], got["b"])
+            peer = got["y%d" % k]
+            if "last" in state:
+                peer = after(peer, state["last"])
+            parts[k] = run_expert(peer, *rows_of(k))
+            state["last"] = parts[k][0]
+        return parts[k]
+
+    def run_sum(k):
+        if k not in sums:
+            sums[k] = join(run_chunk(k)[1], got["r%d" % k])
+        return sums[k]
+
+    def source(name):
+        kind, number = name[0], int(name[1:] or 0)
+        if kind == "e":
+            return send[number], "expert", number
+        if kind == "y":
+            return both(*rows_of(number)), "dp", 2
+        if kind == "r":
+            return run_chunk(number)[0], "dp", 2
+        if kind == "o":
+            return run_sum(number // 2)[number % 2], "expert", number
+        if kind == "a":
+            return theirs, "dp", 2
+        if kind == "b":
+            state["pair"] = both(mine, got["a"])
+            return state["pair"], "dp", 1
+        return (up if kind == "u" else down), "dp", 1
+
+    for item in ORDER:
+        name, _, gates = item.partition(":")
+        x, axis, bit = source(name)
+        if gates:
+            x = after(x, *[got[g] for g in gates.split(",")])
+        got[name] = flip(x, axis, bit)
+    backs = [run_sum(0)[0]] + [got["o%d" % j] for j in range(1, experts)]
+
+    return pl.pallas_call(
+        functools.partial(mix_kernel, cap),
+        out_shape=jax.ShapeDtypeStruct((count, width), BF16),
+        in_specs=[VMEM] * (2 + experts),
+        out_specs=VMEM,
+        compiler_params=pltpu.CompilerParams(vmem_limit_bytes=8 * 2**20),
+        cost_estimate=pl.CostEstimate(flops=2 * 10**8, bytes_accessed=2 * 10**6, transcendentals=0),
+        name="mix",
+    )(expert_ids, combine, *backs)
 
 
 def expert_part(sent_rows, slot_codes, w_up, down_matrix, adapter_input_piece, adapter_output_full):
@@ -120,6 +358,8 @@
         P("dp", "expert", None, None),
         P("dp", "expert", None, None),
     )
+    pairs = mesh.shape["dp"] == 4 and mesh.shape["expert"] == 8
+    body = local_pairs if pairs else local
     return jax.shard_map(
-        local, mesh=mesh, in_specs=placed, out_specs=P(("expert", "dp"), None), check_vma=False
-    )
+        body, mesh=mesh, in_specs=placed, out_specs=P(("expert", "dp"), None), check_vma=False
+    )

time: 177 us -> 73.7 us (0.42)
  blocking collectives: 45 us -> 0 us
  waiting for transfers between devices: 58.3 us -> 19.3 us
  starting transfers between devices: 12.6 us -> 37.3 us
  local copies, waits for them, and re-layouts: 24.5 us -> 1.36 us
  matrix products: 19.6 us -> 0 us
  between operations: 13.6 us -> 0.3 us
  Pallas kernels: 0 us -> 13.1 us
    reduce_scatter x1 -> x0, waiting for transfers between devices: 38.1 us -> none  [local(): lax.psum_scatter(rounded_term.reshape(dp_count, expert_count, capacity, m...]
    ppermute x0 -> x26, starting transfers between devices: none -> 37.3 us  [flip(): return lax.ppermute(x, axis, [(i, i ^ bit) for i in range(size)])]
    all_to_all x1 -> x0, blocking collectives: 27.3 us -> none  [local(): lax.all_to_all(send_rows, 'expert', split_axis=0, concat_axis=0, tiled=True)]
    all_to_all x3 -> x0, waiting for transfers between devices: 20.2 us -> none  [the longest x1 20.1 us: local(): lax.all_to_all(result_rows, 'expert', split_axis=0, concat_axis=0, tiled=...]
    dot_general x3 -> x0, matrix products: 19.6 us -> none  [the longest x1 8.58 us: expert_part(): jnp.dot(reduced_rank, output_flattened, preferred_element_type=jnp.float32)]
    ppermute x0 -> x26, waiting for transfers between devices: none -> 19.3 us  [flip(): return lax.ppermute(x, axis, [(i, i ^ bit) for i in range(size)])]
    all_gather x2 -> x0, blocking collectives: 17.7 us -> none  [the longest x1 12.6 us: local(): lax.all_gather(adapter_out, 'dp', axis=0, tiled=True)]
    pallas_call x0 -> x6, Pallas kernels: none -> 13.1 us  [the longest x4 9.01 us: run_expert(): pl.pallas_call(functools.partial(expert_kernel, rank), out_shape=[jax.Sha...]
  transfers between devices with their start and end apart: 5 -> 26, of which waited for: 2 -> 10; matrix products, arithmetic and copies ran while one was open for 11% -> 5% of each run, Pallas kernels for 0% -> 12%
where the time goes in v2:
time: 73.7 us; the launch traced here: 73.6 us
  starting transfers between devices  37.3 us (51%)
  waiting for transfers between devices  19.3 us (26%)
  Pallas kernels  13.1 us (18%)
  other arithmetic  2.27 us (3%)
  local copies, waits for them, and re-layouts  1.36 us (2%)
    ppermute x26, starting transfers between devices, flip(): return lax.ppermute(x, axis, [(i, i ^ bit) for i in range(size)])  37.3 us
    ppermute x26, waiting for transfers between devices, flip(): return lax.ppermute(x, axis, [(i, i ^ bit) for i in range(size)])  19.3 us
    pallas_call x4, Pallas kernels, run_expert(): pl.pallas_call(functools.partial(expert_kernel, rank), out_shape=[jax.Sha...  9.01 us
    pallas_call x1, Pallas kernels, local_pairs(): pl.pallas_call(functools.partial(prep_kernel, cap), out_shape=[jax.ShapeD...  2.55 us
    concatenate x5, other arithmetic, both(): return jnp.concatenate([a, b], axis=0)  2.08 us
    pallas_call x1, Pallas kernels, local_pairs(): pl.pallas_call(functools.partial(mix_kernel, cap), out_shape=jax.ShapeDty...  1.51 us
  transfers between devices with their start and end apart: 26, of which 10 were waited for; matrix products, arithmetic and copies ran while one was open for 5% of the time, Pallas kernels for 12%

profile of v2, /device:TPU:0, one launch (start us, length us, event | category | flops | bytes accessed | tf_op | source)
XLA Modules:
  0.0 73.6 jit_solution(18204233014603350584)
XLA Ops:
  0.0 2.5 %prep.1 = (bf16[32,3072]{1,0:T(8,128)(2,1)}, bf16[32,3072]{1,0:T(8,128)(2,1)}, bf16[48,1152]{1,0:T(8,128)(2,1)}, bf16[48,1152]{1,0:T(8,128)(2,1)}, bf16[48,1152]...) custom-call(s32[8]{0:T(128)} %slot_ref.1, ...), custom_call_target="tpu_custom_call" | custom-call | flops 100000000 | bytes 2000000 | tf_op jit(solution)/shard_map/prep/pallas_call | solution.py:149
  2.6 6.0 %collective-permute-start.4 = (bf16[48,1152]{1,0:T(8,128)(2,1)}, bf16[48,1152]{1,0:T(8,128)(2,1)S(1)}, u32[]{:S(2)}, u32[]{:S(2)}) collective-permute-start(bf16[48,1152]{1,0:T(8,128)(2,1)} %get-tuple-element.46), channel_id=1, source_target_pairs={{0,28},{4,24},{8,20},{12,16},{16,12},{20,8},{24,4},{28,0},{1,29},{... | collective-permute-start | bytes 331784 | tf_op jit(solution)/shard_map/ppermute | solution.py:134
  8.6 3.4 %collective-permute-done.4.own_b_ref = bf16[48,1152]{1,0:T(8,128)(2,1)S(1)} collective-permute-done((bf16[48,1152]{1,0:T(8,128)(2,1)}, bf16[48,1152]{1,0:T(8,128)(2,1)S(1)}, u32[]{:S(2)}, u32[]{:S(2)}) %collective-permute-start.4) | collective-permute-done | bytes 110624 | tf_op jit(solution)/shard_map/ppermute | solution.py:134
  11.9 1.5 %collective-permute-start.6 = (bf16[32,3072]{1,0:T(8,128)(2,1)}, bf16[32,3072]{1,0:T(8,128)(2,1)S(1)}, u32[]{:S(2)}, u32[]{:S(2)}) collective-permute-start(bf16[32,3072]{1,0:T(8,128)(2,1)} %get-tuple-element.49), channel_id=1, source_target_pairs={{0,2},{1,3},{2,0},{3,1},{4,6},{5,7},{6,4},{7,5},{8,10},{9,11},{10,... | collective-permute-start | bytes 589832 | tf_op jit(solution)/shard_map/ppermute | solution.py:134
  13.5 1.4 %collective-permute-start = (bf16[48,1152]{1,0:T(8,128)(2,1)}, bf16[48,1152]{1,0:T(8,128)(2,1)S(1)}, u32[]{:S(2)}, u32[]{:S(2)}) collective-permute-start(bf16[48,1152]{1,0:T(8,128)(2,1)} %get-tuple-element.43), channel_id=1, source_target_pairs={{0,4},{4,0},{8,12},{12,8},{16,20},{20,16},{24,28},{28,24},{1,5},{5... | collective-permute-start | bytes 331784 | tf_op jit(solution)/shard_map/ppermute | solution.py:134
  14.9 3.6 %collective-permute-start.1 = (bf16[48,1152]{1,0:T(8,128)(2,1)}, bf16[48,1152]{1,0:T(8,128)(2,1)S(1)}, u32[]{:S(2)}, u32[]{:S(2)}) collective-permute-start(bf16[48,1152]{1,0:T(8,128)(2,1)} %get-tuple-element.44), channel_id=1, source_target_pairs={{0,24},{4,28},{8,16},{12,20},{16,8},{20,12},{24,0},{28,4},{1,25},{... | collective-permute-start | bytes 331784 | tf_op jit(solution)/shard_map/ppermute | solution.py:134
  18.5 0.9 %constant_dynamic-update-slice_fusion.2 = bf16[128,3072]{1,0:T(8,128)(2,1)S(1)} fusion(bf16[32,3072]{1,0:T(8,128)(2,1)} %get-tuple-element.48), kind=kLoop, calls=%fused_computation.11 | loop fusion | bytes 393216
  19.4 3.3 %collective-permute-start.14 = (bf16[48,1152]{1,0:T(8,128)(2,1)}, bf16[48,1152]{1,0:T(8,128)(2,1)S(1)}, u32[]{:S(2)}, u32[]{:S(2)}) collective-permute-start(bf16[48,1152]{1,0:T(8,128)(2,1)} %get-tuple-element.62), channel_id=1, source_target_pairs={{0,20},{4,16},{8,28},{12,24},{16,4},{20,0},{24,12},{28,8},{1,21},{... | collective-permute-start | bytes 331784 | tf_op jit(solution)/shard_map/ppermute | solution.py:134
  22.8 0.9 %pad_maximum_fusion.1 = bf16[96,1152]{1,0:T(8,128)(2,1)S(1)} fusion(bf16[48,1152]{1,0:T(8,128)(2,1)S(1)} %collective-permute-done.own_b_ref, bf16[48,1152]{1,0:T(8,128)(2,1)} %get-tuple-element.42.own_a_ref), kind=kLoop, calls=%fused_computation.5 | loop fusion | flops 442368 | bytes 442368 | tf_op jit(solution)/shard_map/concatenate | solution.py:182
  24.3 1.1 %pad_maximum_fusion = bf16[64,3072]{1,0:T(8,128)(2,1)S(1)} fusion(bf16[32,3072]{1,0:T(8,128)(2,1)S(1)} %collective-permute-done.6, bf16[32,3072]{1,0:T(8,128)(2,1)} %get-tuple-element.48), kind=kLoop, calls=%fused_computation | loop fusion | flops 786432 | bytes 786432 | tf_op jit(solution)/shard_map/concatenate | solution.py:182
  25.5 1.7 %collective-permute-start.8 = (bf16[48,1152]{1,0:T(8,128)(2,1)}, bf16[48,1152]{1,0:T(8,128)(2,1)S(1)}, u32[]{:S(2)}, u32[]{:S(2)}) collective-permute-start(bf16[48,1152]{1,0:T(8,128)(2,1)} %get-tuple-element.54), channel_id=1, source_target_pairs={{0,16},{4,20},{8,24},{12,28},{16,0},{20,4},{24,8},{28,12},{1,17},{... | collective-permute-start | bytes 331784 | tf_op jit(solution)/shard_map/ppermute | solution.py:134
  27.3 1.6 %collective-permute-start.16 = (bf16[96,1152]{1,0:T(8,128)(2,1)S(1)}, bf16[96,1152]{1,0:T(8,128)(2,1)S(1)}, u32[]{:S(2)}, u32[]{:S(2)}) collective-permute-start(bf16[96,1152]{1,0:T(8,128)(2,1)S(1)} %pad_maximum_fusion.4), channel_id=1, source_target_pairs={{0,2},{1,3},{2,0},{3,1},{4,6},{5,7},{6,4},{7,5},{8,10},{9,11},{10,... | collective-permute-start | bytes 663560 | tf_op jit(solution)/shard_map/ppermute | solution.py:134
  28.9 0.6 collective-permute-start.10
  29.5 5.1 %collective-permute-done.8.own_a_ref = bf16[48,1152]{1,0:T(8,128)(2,1)S(1)} collective-permute-done((bf16[48,1152]{1,0:T(8,128)(2,1)}, bf16[48,1152]{1,0:T(8,128)(2,1)S(1)}, u32[]{:S(2)}, u32[]{:S(2)}) %collective-permute-start.8) | collective-permute-done | bytes 110624 | tf_op jit(solution)/shard_map/ppermute | solution.py:134
  34.6 1.5 %collective-permute-start.15 = (bf16[96,1152]{1,0:T(8,128)(2,1)S(1)}, bf16[96,1152]{1,0:T(8,128)(2,1)S(1)}, u32[]{:S(2)}, u32[]{:S(2)}) collective-permute-start(bf16[96,1152]{1,0:T(8,128)(2,1)S(1)} %pad_maximum_fusion.3), channel_id=1, source_target_pairs={{0,2},{1,3},{2,0},{3,1},{4,6},{5,7},{6,4},{7,5},{8,10},{9,11},{10,... | collective-permute-start | bytes 663560 | tf_op jit(solution)/shard_map/ppermute | solution.py:134
  36.2 2.2 %expert.4 = (bf16[96,1024]{1,0:T(8,128)(2,1)S(1)}, f32[96,1024]{1,0:T(8,128)S(1)}) custom-call(bf16[96,1152]{1,0:T(8,128)(2,1)S(1)} %collective-permute-done.2.peer_ref, bf16[48,1152]{1,0:T(8,128)(2,1)S(1)} %copy-done.2, bf16[48,1152]{1,0:T(8,128)(2,1)S(1)} %collective-permute-done.own_b_ref, bf16[1024,1024]{1,0:T(8,128)(2,1)S(1)} %bitcast.7, ...), custom_call_target="tpu_custom_call" | custom-call | flops 1610612736 | bytes 10485760 | tf_op jit(solution)/shard_map/expert/pallas_call | solution.py:162
  38.5 2.3 %expert.5 = (bf16[96,1024]{1,0:T(8,128)(2,1)S(1)}, f32[96,1024]{1,0:T(8,128)S(1)}) custom-call(bf16[96,1152]{1,0:T(8,128)(2,1)S(1)} %collective-permute-done.16.peer_ref, bf16[48,1152]{1,0:T(8,128)(2,1)S(1)} %collective-permute-done.1.own_a_ref, bf16[48,1152]{1,0:T(8,128)(2,1)S(1)} %collective-permute-done.4.own_b_ref, bf16[1024,1024]{1,0:T(8,128)(2,1)S(1)} %bitcast.8, ...), custom_call_target="tpu_custom_call" | custom-call | flops 1610612736 | bytes 10485760 | tf_op jit(solution)/shard_map/expert/pallas_call | solution.py:162
  40.8 0.7 collective-permute-start.18
  41.4 1.4 %collective-permute-start.9 = (bf16[96,1024]{1,0:T(8,128)(2,1)S(1)}, bf16[96,1024]{1,0:T(8,128)(2,1)S(1)}, u32[]{:S(2)}, u32[]{:S(2)}) collective-permute-start(bf16[96,1024]{1,0:T(8,128)(2,1)S(1)} %get-tuple-element.55), channel_id=1, source_target_pairs={{0,2},{1,3},{2,0},{3,1},{4,6},{5,7},{6,4},{7,5},{8,10},{9,11},{10,... | collective-permute-start | bytes 589832 | tf_op jit(solution)/shard_map/ppermute | solution.py:134
  42.9 2.3 %expert.6 = (bf16[96,1024]{1,0:T(8,128)(2,1)S(1)}, f32[96,1024]{1,0:T(8,128)S(1)}) custom-call(bf16[96,1152]{1,0:T(8,128)(2,1)S(1)} %collective-permute-done.15.peer_ref, bf16[48,1152]{1,0:T(8,128)(2,1)S(1)} %collective-permute-done.8.own_a_ref, bf16[48,1152]{1,0:T(8,128)(2,1)S(1)} %collective-permute-done.14.own_b_ref, bf16[1024,1024]{1,0:T(8,128)(2,1)S(1)} %bitcast.9, ...), custom_call_target="tpu_custom_call" | custom-call | flops 1610612736 | bytes 10485760 | tf_op jit(solution)/shard_map/expert/pallas_call | solution.py:162
  45.1 1.9 %collective-permute-done.11.own_b_ref = bf16[48,1152]{1,0:T(8,128)(2,1)S(1)} collective-permute-done((bf16[48,1152]{1,0:T(8,128)(2,1)S(1)}, bf16[48,1152]{1,0:T(8,128)(2,1)S(1)}, u32[]{:S(2)}, u32[]{:S(2)}) %collective-permute-start.11) | collective-permute-done | bytes 110624 | tf_op jit(solution)/shard_map/ppermute | solution.py:134
  47.1 1.5 %collective-permute-start.12 = (bf16[96,1152]{1,0:T(8,128)(2,1)S(1)}, bf16[96,1152]{1,0:T(8,128)(2,1)S(1)}, u32[]{:S(2)}, u32[]{:S(2)}) collective-permute-start(bf16[96,1152]{1,0:T(8,128)(2,1)S(1)} %pad_maximum_fusion.2), channel_id=1, source_target_pairs={{0,2},{1,3},{2,0},{3,1},{4,6},{5,7},{6,4},{7,5},{8,10},{9,11},{10,... | collective-permute-start | bytes 663560 | tf_op jit(solution)/shard_map/ppermute | solution.py:134
  48.7 1.9 %collective-permute-start.23 = (bf16[48,1024]{1,0:T(8,128)(2,1)S(1)}, bf16[48,1024]{1,0:T(8,128)(2,1)S(1)}, u32[]{:S(2)}, u32[]{:S(2)}) collective-permute-start(bf16[48,1024]{1,0:T(8,128)(2,1)S(1)} %get-tuple-element.80), channel_id=1, source_target_pairs={{0,28},{4,24},{8,20},{12,16},{16,12},{20,8},{24,4},{28,0},{1,29},{... | collective-permute-start | bytes 294920 | tf_op jit(solution)/shard_map/ppermute | solution.py:134
  51.1 2.1 %collective-permute-start.25 = (bf16[48,1024]{1,0:T(8,128)(2,1)S(1)}, bf16[48,1024]{1,0:T(8,128)(2,1)S(1)}, u32[]{:S(2)}, u32[]{:S(2)}) collective-permute-start(bf16[48,1024]{1,0:T(8,128)(2,1)S(1)} %get-tuple-element.79), channel_id=1, source_target_pairs={{0,24},{4,28},{8,16},{12,20},{16,8},{20,12},{24,0},{28,4},{1,25},{... | collective-permute-start | bytes 294920 | tf_op jit(solution)/shard_map/ppermute | solution.py:134
  53.3 4.3 %collective-permute-done.12.peer_ref = bf16[96,1152]{1,0:T(8,128)(2,1)S(1)} collective-permute-done((bf16[96,1152]{1,0:T(8,128)(2,1)S(1)}, bf16[96,1152]{1,0:T(8,128)(2,1)S(1)}, u32[]{:S(2)}, u32[]{:S(2)}) %collective-permute-start.12) | collective-permute-done | bytes 221216 | tf_op jit(solution)/shard_map/ppermute | solution.py:134
  57.6 2.3 %expert.7 = (bf16[96,1024]{1,0:T(8,128)(2,1)S(1)}, f32[96,1024]{1,0:T(8,128)S(1)}) custom-call(bf16[96,1152]{1,0:T(8,128)(2,1)S(1)} %collective-permute-done.12.peer_ref, bf16[48,1152]{1,0:T(8,128)(2,1)S(1)} %collective-permute-done.10.own_a_ref, bf16[48,1152]{1,0:T(8,128)(2,1)S(1)} %collective-permute-done.11.own_b_ref, bf16[1024,1024]{1,0:T(8,128)(2,1)S(1)} %bitcast.10, ...), custom_call_target="tpu_custom_call" | custom-call | flops 1610612736 | bytes 10485760 | tf_op jit(solution)/shard_map/expert/pallas_call | solution.py:162
  59.9 0.7 collective-permute-start.17
  61.8 3.3 %collective-permute-start.22 = (bf16[48,1024]{1,0:T(8,128)(2,1)S(1)}, bf16[48,1024]{1,0:T(8,128)(2,1)S(1)}, u32[]{:S(2)}, u32[]{:S(2)}) collective-permute-start(bf16[48,1024]{1,0:T(8,128)(2,1)S(1)} %get-tuple-element.82), channel_id=1, source_target_pairs={{0,16},{4,20},{8,24},{12,28},{16,0},{20,4},{24,8},{28,12},{1,17},{... | collective-permute-start | bytes 294920 | tf_op jit(solution)/shard_map/ppermute | solution.py:134
  65.8 2.1 %collective-permute-start.20 = (bf16[48,1024]{1,0:T(8,128)(2,1)S(1)}, bf16[48,1024]{1,0:T(8,128)(2,1)S(1)}, u32[]{:S(2)}, u32[]{:S(2)}) collective-permute-start(bf16[48,1024]{1,0:T(8,128)(2,1)S(1)} %get-tuple-element.74), channel_id=1, source_target_pairs={{0,8},{4,12},{8,0},{12,4},{16,24},{20,28},{24,16},{28,20},{1,9},{5... | collective-permute-start | bytes 294920 | tf_op jit(solution)/shard_map/ppermute | solution.py:134
  68.5 1.7 %collective-permute-done.22.refs_4_ = bf16[48,1024]{1,0:T(8,128)(2,1)S(1)} collective-permute-done((bf16[48,1024]{1,0:T(8,128)(2,1)S(1)}, bf16[48,1024]{1,0:T(8,128)(2,1)S(1)}, u32[]{:S(2)}, u32[]{:S(2)}) %collective-permute-start.22) | collective-permute-done | bytes 98336 | tf_op jit(solution)/shard_map/ppermute | solution.py:134
  70.2 1.4 %collective-permute-done.21.refs_3_ = bf16[48,1024]{1,0:T(8,128)(2,1)S(1)} collective-permute-done((bf16[48,1024]{1,0:T(8,128)(2,1)S(1)}, bf16[48,1024]{1,0:T(8,128)(2,1)S(1)}, u32[]{:S(2)}, u32[]{:S(2)}) %collective-permute-start.21) | collective-permute-done | bytes 98336 | tf_op jit(solution)/shard_map/ppermute | solution.py:134
  72.0 1.5 %mix.1 = bf16[128,1024]{1,0:T(8,128)(2,1)} custom-call(s32[128,2]{1,0:T(8,128)S(1)} %copy.10.ids_ref, f32[128,2]{1,0:T(8,128)S(1)} %copy.11.combine_ref, bf16[48,1024]{1,0:T(8,128)(2,1)S(1)} %get-tuple-element.86.refs_0_, bf16[48,1024]{1,0:T(8,128)(2,1)S(1)} %collective-permute-done.13.refs_1_, bf16[48,1024]{1,0:T(8,128)(2,1)S(1)} %collective-permute-done.20.refs_2_, ...), custom_call_target="tpu_custom_call" | custom-call | flops 200000000 | bytes 2000000 | tf_op jit(solution)/shard_map/mix/pallas_call | solution.py:234
  (60 shorter events, 4.5 us)
Async XLA Ops:
  2.5 26.3 %copy-start.6 = (bf16[48,1152]{1,0:T(8,128)(2,1)S(1)}, bf16[48,1152]{1,0:T(8,128)(2,1)}, u32[]{:S(2)}) copy-start(bf16[48,1152]{1,0:T(8,128)(2,1)} %get-tuple-element.57) | copy-start | bytes 331780
  2.6 9.4 %collective-permute-start.4 = (bf16[48,1152]{1,0:T(8,128)(2,1)}, bf16[48,1152]{1,0:T(8,128)(2,1)S(1)}, u32[]{:S(2)}, u32[]{:S(2)}) collective-permute-start(bf16[48,1152]{1,0:T(8,128)(2,1)} %get-tuple-element.46), channel_id=1, source_target_pairs={{0,28},{4,24},{8,20},{12,16},{16,12},{20,8},{24,4},{28,0},{1,29},{... | collective-permute-start | bytes 331784 | tf_op jit(solution)/shard_map/ppermute | solution.py:134
  8.6 16.9 %collective-permute-start.3 = (bf16[1024,1024]{1,0:T(8,128)(2,1)}, bf16[1024,1024]{1,0:T(8,128)(2,1)S(1)}, u32[]{:S(2)}, u32[]{:S(2)}) collective-permute-start(bf16[1024,1024]{1,0:T(8,128)(2,1)} %bitcast.6), channel_id=1, source_target_pairs={{0,1},{1,0},{2,3},{3,2},{4,5},{5,4},{6,7},{7,6},{8,9},{9,8},{10,11... | collective-permute-start | bytes 6291464 | tf_op jit(solution)/shard_map/ppermute | solution.py:134
  11.9 13.6 %collective-permute-start.5 = (bf16[1024,1024]{1,0:T(8,128)(2,1)}, bf16[1024,1024]{1,0:T(8,128)(2,1)S(1)}, u32[]{:S(2)}, u32[]{:S(2)}) collective-permute-start(bf16[1024,1024]{1,0:T(8,128)(2,1)} %bitcast.11), channel_id=1, source_target_pairs={{0,1},{1,0},{2,3},{3,2},{4,5},{5,4},{6,7},{7,6},{8,9},{9,8},{10,11... | collective-permute-start | bytes 6291464 | tf_op jit(solution)/shard_map/ppermute | solution.py:134
  11.9 12.4 %collective-permute-start.6 = (bf16[32,3072]{1,0:T(8,128)(2,1)}, bf16[32,3072]{1,0:T(8,128)(2,1)S(1)}, u32[]{:S(2)}, u32[]{:S(2)}) collective-permute-start(bf16[32,3072]{1,0:T(8,128)(2,1)} %get-tuple-element.49), channel_id=1, source_target_pairs={{0,2},{1,3},{2,0},{3,1},{4,6},{5,7},{6,4},{7,5},{8,10},{9,11},{10,... | collective-permute-start | bytes 589832 | tf_op jit(solution)/shard_map/ppermute | solution.py:134
  13.5 5.9 %collective-permute-start = (bf16[48,1152]{1,0:T(8,128)(2,1)}, bf16[48,1152]{1,0:T(8,128)(2,1)S(1)}, u32[]{:S(2)}, u32[]{:S(2)}) collective-permute-start(bf16[48,1152]{1,0:T(8,128)(2,1)} %get-tuple-element.43), channel_id=1, source_target_pairs={{0,4},{4,0},{8,12},{12,8},{16,20},{20,16},{24,28},{28,24},{1,5},{5... | collective-permute-start | bytes 331784 | tf_op jit(solution)/shard_map/ppermute | solution.py:134
  14.9 8.8 %collective-permute-start.1 = (bf16[48,1152]{1,0:T(8,128)(2,1)}, bf16[48,1152]{1,0:T(8,128)(2,1)S(1)}, u32[]{:S(2)}, u32[]{:S(2)}) collective-permute-start(bf16[48,1152]{1,0:T(8,128)(2,1)} %get-tuple-element.44), channel_id=1, source_target_pairs={{0,24},{4,28},{8,16},{12,20},{16,8},{20,12},{24,0},{28,4},{1,25},{... | collective-permute-start | bytes 331784 | tf_op jit(solution)/shard_map/ppermute | solution.py:134
  19.4 9.4 %collective-permute-start.14 = (bf16[48,1152]{1,0:T(8,128)(2,1)}, bf16[48,1152]{1,0:T(8,128)(2,1)S(1)}, u32[]{:S(2)}, u32[]{:S(2)}) collective-permute-start(bf16[48,1152]{1,0:T(8,128)(2,1)} %get-tuple-element.62), channel_id=1, source_target_pairs={{0,20},{4,16},{8,28},{12,24},{16,4},{20,0},{24,12},{28,8},{1,21},{... | collective-permute-start | bytes 331784 | tf_op jit(solution)/shard_map/ppermute | solution.py:134
  23.7 12.5 %collective-permute-start.2 = (bf16[96,1152]{1,0:T(8,128)(2,1)S(1)}, bf16[96,1152]{1,0:T(8,128)(2,1)S(1)}, u32[]{:S(2)}, u32[]{:S(2)}) collective-permute-start(bf16[96,1152]{1,0:T(8,128)(2,1)S(1)} %pad_maximum_fusion.1), channel_id=1, source_target_pairs={{0,2},{1,3},{2,0},{3,1},{4,6},{5,7},{6,4},{7,5},{8,10},{9,11},{10,... | collective-permute-start | bytes 663560 | tf_op jit(solution)/shard_map/ppermute | solution.py:134
  24.3 11.9 %copy-start.1 = (bf16[1,1024,1024]{2,1,0:T(8,128)(2,1)S(1)}, bf16[1,1024,1024]{2,1,0:T(8,128)(2,1)}, u32[]{:S(2)}) copy-start(bf16[1,1024,1024]{2,1,0:T(8,128)(2,1)} %param.15) | copy-start | bytes 6291460
  24.3 11.9 %copy-start = (bf16[1,1024,1024]{2,1,0:T(8,128)(2,1)S(1)}, bf16[1,1024,1024]{2,1,0:T(8,128)(2,1)}, u32[]{:S(2)}) copy-start(bf16[1,1024,1024]{2,1,0:T(8,128)(2,1)} %param.14) | copy-start | bytes 6291460
  24.3 11.9 %copy-start.2 = (bf16[48,1152]{1,0:T(8,128)(2,1)S(1)}, bf16[48,1152]{1,0:T(8,128)(2,1)}, u32[]{:S(2)}) copy-start(bf16[48,1152]{1,0:T(8,128)(2,1)} %get-tuple-element.42.own_a_ref) | copy-start | bytes 331780
  25.4 10.7 %collective-permute-start.7 = (bf16[64,3072]{1,0:T(8,128)(2,1)S(1)}, bf16[64,3072]{1,0:T(8,128)(2,1)S(1)}, u32[]{:S(2)}, u32[]{:S(2)}) collective-permute-start(bf16[64,3072]{1,0:T(8,128)(2,1)S(1)} %pad_maximum_fusion), channel_id=1, source_target_pairs={{0,1},{1,0},{2,3},{3,2},{4,5},{5,4},{6,7},{7,6},{8,9},{9,8},{10,11... | collective-permute-start | bytes 1179656 | tf_op jit(solution)/shard_map/ppermute | solution.py:134
  25.5 9.1 %collective-permute-start.8 = (bf16[48,1152]{1,0:T(8,128)(2,1)}, bf16[48,1152]{1,0:T(8,128)(2,1)S(1)}, u32[]{:S(2)}, u32[]{:S(2)}) collective-permute-start(bf16[48,1152]{1,0:T(8,128)(2,1)} %get-tuple-element.54), channel_id=1, source_target_pairs={{0,16},{4,20},{8,24},{12,28},{16,0},{20,4},{24,8},{28,12},{1,17},{... | collective-permute-start | bytes 331784 | tf_op jit(solution)/shard_map/ppermute | solution.py:134
  27.3 11.2 %collective-permute-start.16 = (bf16[96,1152]{1,0:T(8,128)(2,1)S(1)}, bf16[96,1152]{1,0:T(8,128)(2,1)S(1)}, u32[]{:S(2)}, u32[]{:S(2)}) collective-permute-start(bf16[96,1152]{1,0:T(8,128)(2,1)S(1)} %pad_maximum_fusion.4), channel_id=1, source_target_pairs={{0,2},{1,3},{2,0},{3,1},{4,6},{5,7},{6,4},{7,5},{8,10},{9,11},{10,... | collective-permute-start | bytes 663560 | tf_op jit(solution)/shard_map/ppermute | solution.py:134
  28.9 16.3 %collective-permute-start.10 = (bf16[48,1152]{1,0:T(8,128)(2,1)S(1)}, bf16[48,1152]{1,0:T(8,128)(2,1)S(1)}, u32[]{:S(2)}, u32[]{:S(2)}) collective-permute-start(bf16[48,1152]{1,0:T(8,128)(2,1)S(1)} %copy-done.6), channel_id=1, source_target_pairs={{0,8},{4,12},{8,0},{12,4},{16,24},{20,28},{24,16},{28,20},{1,9},{5... | collective-permute-start | bytes 331784 | tf_op jit(solution)/shard_map/ppermute | solution.py:134
  34.6 8.3 %collective-permute-start.15 = (bf16[96,1152]{1,0:T(8,128)(2,1)S(1)}, bf16[96,1152]{1,0:T(8,128)(2,1)S(1)}, u32[]{:S(2)}, u32[]{:S(2)}) collective-permute-start(bf16[96,1152]{1,0:T(8,128)(2,1)S(1)} %pad_maximum_fusion.3), channel_id=1, source_target_pairs={{0,2},{1,3},{2,0},{3,1},{4,6},{5,7},{6,4},{7,5},{8,10},{9,11},{10,... | collective-permute-start | bytes 663560 | tf_op jit(solution)/shard_map/ppermute | solution.py:134
  40.8 7.9 %collective-permute-start.18 = (bf16[96,1024]{1,0:T(8,128)(2,1)S(1)}, bf16[96,1024]{1,0:T(8,128)(2,1)S(1)}, u32[]{:S(2)}, u32[]{:S(2)}) collective-permute-start(bf16[96,1024]{1,0:T(8,128)(2,1)S(1)} %get-tuple-element.66), channel_id=1, source_target_pairs={{0,2},{1,3},{2,0},{3,1},{4,6},{5,7},{6,4},{7,5},{8,10},{9,11},{10,... | collective-permute-start | bytes 589832 | tf_op jit(solution)/shard_map/ppermute | solution.py:134
  41.4 5.6 %collective-permute-start.11 = (bf16[48,1152]{1,0:T(8,128)(2,1)S(1)}, bf16[48,1152]{1,0:T(8,128)(2,1)S(1)}, u32[]{:S(2)}, u32[]{:S(2)}) collective-permute-start(bf16[48,1152]{1,0:T(8,128)(2,1)S(1)} %copy-done.5), channel_id=1, source_target_pairs={{0,12},{4,8},{8,4},{12,0},{16,28},{20,24},{24,20},{28,16},{1,13},{... | collective-permute-start | bytes 331784 | tf_op jit(solution)/shard_map/ppermute | solution.py:134
  41.4 11.8 %collective-permute-start.9 = (bf16[96,1024]{1,0:T(8,128)(2,1)S(1)}, bf16[96,1024]{1,0:T(8,128)(2,1)S(1)}, u32[]{:S(2)}, u32[]{:S(2)}) collective-permute-start(bf16[96,1024]{1,0:T(8,128)(2,1)S(1)} %get-tuple-element.55), channel_id=1, source_target_pairs={{0,2},{1,3},{2,0},{3,1},{4,6},{5,7},{6,4},{7,5},{8,10},{9,11},{10,... | collective-permute-start | bytes 589832 | tf_op jit(solution)/shard_map/ppermute | solution.py:134
  47.1 10.5 %collective-permute-start.12 = (bf16[96,1152]{1,0:T(8,128)(2,1)S(1)}, bf16[96,1152]{1,0:T(8,128)(2,1)S(1)}, u32[]{:S(2)}, u32[]{:S(2)}) collective-permute-start(bf16[96,1152]{1,0:T(8,128)(2,1)S(1)} %pad_maximum_fusion.2), channel_id=1, source_target_pairs={{0,2},{1,3},{2,0},{3,1},{4,6},{5,7},{6,4},{7,5},{8,10},{9,11},{10,... | collective-permute-start | bytes 663560 | tf_op jit(solution)/shard_map/ppermute | solution.py:134
  48.7 12.4 %collective-permute-start.23 = (bf16[48,1024]{1,0:T(8,128)(2,1)S(1)}, bf16[48,1024]{1,0:T(8,128)(2,1)S(1)}, u32[]{:S(2)}, u32[]{:S(2)}) collective-permute-start(bf16[48,1024]{1,0:T(8,128)(2,1)S(1)} %get-tuple-element.80), channel_id=1, source_target_pairs={{0,28},{4,24},{8,20},{12,16},{16,12},{20,8},{24,4},{28,0},{1,29},{... | collective-permute-start | bytes 294920 | tf_op jit(solution)/shard_map/ppermute | solution.py:134
  50.6 10.5 %collective-permute-start.19 = (bf16[96,1024]{1,0:T(8,128)(2,1)S(1)}, bf16[96,1024]{1,0:T(8,128)(2,1)S(1)}, u32[]{:S(2)}, u32[]{:S(2)}) collective-permute-start(bf16[96,1024]{1,0:T(8,128)(2,1)S(1)} %get-tuple-element.73), channel_id=1, source_target_pairs={{0,2},{1,3},{2,0},{3,1},{4,6},{5,7},{6,4},{7,5},{8,10},{9,11},{10,... | collective-permute-start | bytes 589832 | tf_op jit(solution)/shard_map/ppermute | solution.py:134
  51.1 14.7 %collective-permute-start.25 = (bf16[48,1024]{1,0:T(8,128)(2,1)S(1)}, bf16[48,1024]{1,0:T(8,128)(2,1)S(1)}, u32[]{:S(2)}, u32[]{:S(2)}) collective-permute-start(bf16[48,1024]{1,0:T(8,128)(2,1)S(1)} %get-tuple-element.79), channel_id=1, source_target_pairs={{0,24},{4,28},{8,16},{12,20},{16,8},{20,12},{24,0},{28,4},{1,25},{... | collective-permute-start | bytes 294920 | tf_op jit(solution)/shard_map/ppermute | solution.py:134
  59.9 8.0 %copy-start.3 = (s32[128,2]{0,1:T(2,128)S(1)}, s32[128,2]{0,1:T(2,128)}, u32[]{:S(2)}) copy-start(s32[128,2]{0,1:T(2,128)} %param.10) | copy-start | bytes 3076
  59.9 8.1 %copy-start.4 = (f32[128,2]{0,1:T(2,128)S(1)}, f32[128,2]{0,1:T(2,128)}, u32[]{:S(2)}) copy-start(f32[128,2]{0,1:T(2,128)} %param.11) | copy-start | bytes 3076
  59.9 5.7 %collective-permute-start.17 = (bf16[96,1024]{1,0:T(8,128)(2,1)S(1)}, bf16[96,1024]{1,0:T(8,128)(2,1)S(1)}, u32[]{:S(2)}, u32[]{:S(2)}) collective-permute-start(bf16[96,1024]{1,0:T(8,128)(2,1)S(1)} %get-tuple-element.72), channel_id=1, source_target_pairs={{0,2},{1,3},{2,0},{3,1},{4,6},{5,7},{6,4},{7,5},{8,10},{9,11},{10,... | collective-permute-start | bytes 589832 | tf_op jit(solution)/shard_map/ppermute | solution.py:134
  60.6 7.6 %collective-permute-start.13 = (bf16[48,1024]{1,0:T(8,128)(2,1)S(1)}, bf16[48,1024]{1,0:T(8,128)(2,1)S(1)}, u32[]{:S(2)}, u32[]{:S(2)}) collective-permute-start(bf16[48,1024]{1,0:T(8,128)(2,1)S(1)} %get-tuple-element.61), channel_id=1, source_target_pairs={{0,4},{4,0},{8,12},{12,8},{16,20},{20,16},{24,28},{28,24},{1,5},{5... | collective-permute-start | bytes 294920 | tf_op jit(solution)/shard_map/ppermute | solution.py:134
  61.2 7.3 %collective-permute-start.24 = (bf16[48,1024]{1,0:T(8,128)(2,1)S(1)}, bf16[48,1024]{1,0:T(8,128)(2,1)S(1)}, u32[]{:S(2)}, u32[]{:S(2)}) collective-permute-start(bf16[48,1024]{1,0:T(8,128)(2,1)S(1)} %get-tuple-element.78), channel_id=1, source_target_pairs={{0,20},{4,16},{8,28},{12,24},{16,4},{20,0},{24,12},{28,8},{1,21},{... | collective-permute-start | bytes 294920 | tf_op jit(solution)/shard_map/ppermute | solution.py:134
  61.8 8.4 %collective-permute-start.22 = (bf16[48,1024]{1,0:T(8,128)(2,1)S(1)}, bf16[48,1024]{1,0:T(8,128)(2,1)S(1)}, u32[]{:S(2)}, u32[]{:S(2)}) collective-permute-start(bf16[48,1024]{1,0:T(8,128)(2,1)S(1)} %get-tuple-element.82), channel_id=1, source_target_pairs={{0,16},{4,20},{8,24},{12,28},{16,0},{20,4},{24,8},{28,12},{1,17},{... | collective-permute-start | bytes 294920 | tf_op jit(solution)/shard_map/ppermute | solution.py:134
  65.7 5.9 %collective-permute-start.21 = (bf16[48,1024]{1,0:T(8,128)(2,1)S(1)}, bf16[48,1024]{1,0:T(8,128)(2,1)S(1)}, u32[]{:S(2)}, u32[]{:S(2)}) collective-permute-start(bf16[48,1024]{1,0:T(8,128)(2,1)S(1)} %get-tuple-element.75), channel_id=1, source_target_pairs={{0,12},{4,8},{8,4},{12,0},{16,28},{20,24},{24,20},{28,16},{1,13},{... | collective-permute-start | bytes 294920 | tf_op jit(solution)/shard_map/ppermute | solution.py:134
  65.8 6.2 %collective-permute-start.20 = (bf16[48,1024]{1,0:T(8,128)(2,1)S(1)}, bf16[48,1024]{1,0:T(8,128)(2,1)S(1)}, u32[]{:S(2)}, u32[]{:S(2)}) collective-permute-start(bf16[48,1024]{1,0:T(8,128)(2,1)S(1)} %get-tuple-element.74), channel_id=1, source_target_pairs={{0,8},{4,12},{8,0},{12,4},{16,24},{20,28},{24,16},{28,20},{1,9},{5... | collective-permute-start | bytes 294920 | tf_op jit(solution)/shard_map/ppermute | solution.py:134
  (1 other events, 2.9 us)

commit v3 on v2

--- a/solution.py
+++ b/solution.py
@@ -7,9 +7,10 @@
 from jax.experimental.pallas import tpu as pltpu
 from jax.sharding import PartitionSpec as P
 
-ORDER = tuple(
-    "e6 e7 e1 a d:e7 y0:e6 u e4:d,e1 b:u y3:a,d e5 r0:e4 e3:b r3 y2:e5 e2:d y1:e2 o7 o6 r2:r3 r1:y2 o4 o5:o7 o2:r2 o1:y1 "
-    "o3:r1".split()
+ORDER = (
+    "e6", "e7", "e1", "a", "d:e7", "y0:e6", "u", "e4:d,e1", "b:u", "y3:a,d", "e5", "r0", "e3:b",
+    "r3", "y2:e5", "e2:d", "y1:e2", "o7", "o6", "r2:r3", "r1:E0,y2", "o4", "o5:o7", "o2:r2",
+    "o1:y1", "o3:r1",
 )
 
 F32 = jnp.float32
@@ -198,7 +199,7 @@
             if "last" in state:
                 peer = after(peer, state["last"])
             parts[k] = run_expert(peer, *rows_of(k))
-            state["last"] = parts[k][0]
+            state["last"] = got["E%d" % k] = parts[k][0]
         return parts[k]
 
     def run_sum(k):

time: 73.7 us -> 73.5 us (level)
  waiting for transfers between devices: 19.3 us -> 17.6 us
  starting transfers between devices: 37.3 us -> 38.7 us
    ppermute x26, waiting for transfers between devices: 19.3 us -> 17.6 us  [flip(): return lax.ppermute(x, axis, [(i, i ^ bit) for i in range(size)])]
    ppermute x26, starting transfers between devices: 37.3 us -> 38.7 us  [flip(): return lax.ppermute(x, axis, [(i, i ^ bit) for i in range(size)])]
  transfers between devices with their start and end apart: 26 -> 26, of which waited for: 10 -> 8; matrix products, arithmetic and copies ran while one was open for 5% -> 5% of each run, Pallas kernels for 12% -> 12%
where the time goes in v3:
time: 73.5 us; the launch traced here: 73.3 us
  starting transfers between devices  38.7 us (53%)
  waiting for transfers between devices  17.6 us (24%)
  Pallas kernels  13.1 us (18%)
  other arithmetic  2.27 us (3%)
  local copies, waits for them, and re-layouts  1.36 us (2%)
    ppermute x26, starting transfers between devices, flip(): return lax.ppermute(x, axis, [(i, i ^ bit) for i in range(size)])  38.7 us
    ppermute x26, waiting for transfers between devices, flip(): return lax.ppermute(x, axis, [(i, i ^ bit) for i in range(size)])  17.6 us
    pallas_call x4, Pallas kernels, run_expert(): pl.pallas_call(functools.partial(expert_kernel, rank), out_shape=[jax.Sha...  9 us
    pallas_call x1, Pallas kernels, local_pairs(): pl.pallas_call(functools.partial(prep_kernel, cap), out_shape=[jax.ShapeD...  2.55 us
    concatenate x5, other arithmetic, both(): return jnp.concatenate([a, b], axis=0)  2.08 us
    pallas_call x1, Pallas kernels, local_pairs(): pl.pallas_call(functools.partial(mix_kernel, cap), out_shape=jax.ShapeDty...  1.51 us
  transfers between devices with their start and end apart: 26, of which 8 were waited for; matrix products, arithmetic and copies ran while one was open for 5% of the time, Pallas kernels for 12%

profile of v3, /device:TPU:0, one launch (start us, length us, event | category | flops | bytes accessed | tf_op | source)
XLA Modules:
  0.0 73.3 jit_solution(13528621090741723411)
XLA Ops:
  0.0 2.5 %prep.1 = (bf16[32,3072]{1,0:T(8,128)(2,1)}, bf16[32,3072]{1,0:T(8,128)(2,1)}, bf16[48,1152]{1,0:T(8,128)(2,1)}, bf16[48,1152]{1,0:T(8,128)(2,1)}, bf16[48,1152]...) custom-call(s32[8]{0:T(128)} %slot_ref.1, ...), custom_call_target="tpu_custom_call" | custom-call | flops 100000000 | bytes 2000000 | tf_op jit(solution)/shard_map/prep/pallas_call | solution.py:150
  2.6 6.0 %collective-permute-start.4 = (bf16[48,1152]{1,0:T(8,128)(2,1)}, bf16[48,1152]{1,0:T(8,128)(2,1)S(1)}, u32[]{:S(2)}, u32[]{:S(2)}) collective-permute-start(bf16[48,1152]{1,0:T(8,128)(2,1)} %get-tuple-element.45), channel_id=1, source_target_pairs={{0,28},{4,24},{8,20},{12,16},{16,12},{20,8},{24,4},{28,0},{1,29},{... | collective-permute-start | bytes 331784 | tf_op jit(solution)/shard_map/ppermute | solution.py:135
  8.6 3.4 %collective-permute-done.4.own_b_ref = bf16[48,1152]{1,0:T(8,128)(2,1)S(1)} collective-permute-done((bf16[48,1152]{1,0:T(8,128)(2,1)}, bf16[48,1152]{1,0:T(8,128)(2,1)S(1)}, u32[]{:S(2)}, u32[]{:S(2)}) %collective-permute-start.4) | collective-permute-done | bytes 110624 | tf_op jit(solution)/shard_map/ppermute | solution.py:135
  11.9 1.5 %collective-permute-start.6 = (bf16[32,3072]{1,0:T(8,128)(2,1)}, bf16[32,3072]{1,0:T(8,128)(2,1)S(1)}, u32[]{:S(2)}, u32[]{:S(2)}) collective-permute-start(bf16[32,3072]{1,0:T(8,128)(2,1)} %get-tuple-element.48), channel_id=1, source_target_pairs={{0,2},{1,3},{2,0},{3,1},{4,6},{5,7},{6,4},{7,5},{8,10},{9,11},{10,... | collective-permute-start | bytes 589832 | tf_op jit(solution)/shard_map/ppermute | solution.py:135
  13.5 1.4 %collective-permute-start = (bf16[48,1152]{1,0:T(8,128)(2,1)}, bf16[48,1152]{1,0:T(8,128)(2,1)S(1)}, u32[]{:S(2)}, u32[]{:S(2)}) collective-permute-start(bf16[48,1152]{1,0:T(8,128)(2,1)} %get-tuple-element.42), channel_id=1, source_target_pairs={{0,4},{4,0},{8,12},{12,8},{16,20},{20,16},{24,28},{28,24},{1,5},{5... | collective-permute-start | bytes 331784 | tf_op jit(solution)/shard_map/ppermute | solution.py:135
  14.9 3.6 %collective-permute-start.1 = (bf16[48,1152]{1,0:T(8,128)(2,1)}, bf16[48,1152]{1,0:T(8,128)(2,1)S(1)}, u32[]{:S(2)}, u32[]{:S(2)}) collective-permute-start(bf16[48,1152]{1,0:T(8,128)(2,1)} %get-tuple-element.43), channel_id=1, source_target_pairs={{0,24},{4,28},{8,16},{12,20},{16,8},{20,12},{24,0},{28,4},{1,25},{... | collective-permute-start | bytes 331784 | tf_op jit(solution)/shard_map/ppermute | solution.py:135
  18.5 0.9 %constant_dynamic-update-slice_fusion.2 = bf16[128,3072]{1,0:T(8,128)(2,1)S(1)} fusion(bf16[32,3072]{1,0:T(8,128)(2,1)} %get-tuple-element.47), kind=kLoop, calls=%fused_computation.11 | loop fusion | bytes 393216
  19.4 3.3 %collective-permute-start.14 = (bf16[48,1152]{1,0:T(8,128)(2,1)}, bf16[48,1152]{1,0:T(8,128)(2,1)S(1)}, u32[]{:S(2)}, u32[]{:S(2)}) collective-permute-start(bf16[48,1152]{1,0:T(8,128)(2,1)} %get-tuple-element.60), channel_id=1, source_target_pairs={{0,20},{4,16},{8,28},{12,24},{16,4},{20,0},{24,12},{28,8},{1,21},{... | collective-permute-start | bytes 331784 | tf_op jit(solution)/shard_map/ppermute | solution.py:135
  22.8 0.9 %pad_maximum_fusion.1 = bf16[96,1152]{1,0:T(8,128)(2,1)S(1)} fusion(bf16[48,1152]{1,0:T(8,128)(2,1)S(1)} %collective-permute-done.own_b_ref, bf16[48,1152]{1,0:T(8,128)(2,1)} %get-tuple-element.41.own_a_ref), kind=kLoop, calls=%fused_computation.5 | loop fusion | flops 442368 | bytes 442368 | tf_op jit(solution)/shard_map/concatenate | solution.py:183
  24.3 1.1 %pad_maximum_fusion = bf16[64,3072]{1,0:T(8,128)(2,1)S(1)} fusion(bf16[32,3072]{1,0:T(8,128)(2,1)S(1)} %collective-permute-done.6, bf16[32,3072]{1,0:T(8,128)(2,1)} %get-tuple-element.47), kind=kLoop, calls=%fused_computation | loop fusion | flops 786432 | bytes 786432 | tf_op jit(solution)/shard_map/concatenate | solution.py:183
  25.5 1.7 %collective-permute-start.13 = (bf16[48,1152]{1,0:T(8,128)(2,1)}, bf16[48,1152]{1,0:T(8,128)(2,1)S(1)}, u32[]{:S(2)}, u32[]{:S(2)}) collective-permute-start(bf16[48,1152]{1,0:T(8,128)(2,1)} %get-tuple-element.59), channel_id=1, source_target_pairs={{0,16},{4,20},{8,24},{12,28},{16,0},{20,4},{24,8},{28,12},{1,17},{... | collective-permute-start | bytes 331784 | tf_op jit(solution)/shard_map/ppermute | solution.py:135
  27.3 1.6 %collective-permute-start.16 = (bf16[96,1152]{1,0:T(8,128)(2,1)S(1)}, bf16[96,1152]{1,0:T(8,128)(2,1)S(1)}, u32[]{:S(2)}, u32[]{:S(2)}) collective-permute-start(bf16[96,1152]{1,0:T(8,128)(2,1)S(1)} %pad_maximum_fusion.4), channel_id=1, source_target_pairs={{0,2},{1,3},{2,0},{3,1},{4,6},{5,7},{6,4},{7,5},{8,10},{9,11},{10,... | collective-permute-start | bytes 663560 | tf_op jit(solution)/shard_map/ppermute | solution.py:135
  29.5 5.1 %collective-permute-done.13.own_a_ref = bf16[48,1152]{1,0:T(8,128)(2,1)S(1)} collective-permute-done((bf16[48,1152]{1,0:T(8,128)(2,1)}, bf16[48,1152]{1,0:T(8,128)(2,1)S(1)}, u32[]{:S(2)}, u32[]{:S(2)}) %collective-permute-start.13) | collective-permute-done | bytes 110624 | tf_op jit(solution)/shard_map/ppermute | solution.py:135
  34.6 1.5 %collective-permute-start.15 = (bf16[96,1152]{1,0:T(8,128)(2,1)S(1)}, bf16[96,1152]{1,0:T(8,128)(2,1)S(1)}, u32[]{:S(2)}, u32[]{:S(2)}) collective-permute-start(bf16[96,1152]{1,0:T(8,128)(2,1)S(1)} %pad_maximum_fusion.3), channel_id=1, source_target_pairs={{0,2},{1,3},{2,0},{3,1},{4,6},{5,7},{6,4},{7,5},{8,10},{9,11},{10,... | collective-permute-start | bytes 663560 | tf_op jit(solution)/shard_map/ppermute | solution.py:135
  36.2 2.2 %expert.4 = (bf16[96,1024]{1,0:T(8,128)(2,1)S(1)}, f32[96,1024]{1,0:T(8,128)S(1)}) custom-call(bf16[96,1152]{1,0:T(8,128)(2,1)S(1)} %collective-permute-done.2.peer_ref, bf16[48,1152]{1,0:T(8,128)(2,1)S(1)} %copy-done.2, bf16[48,1152]{1,0:T(8,128)(2,1)S(1)} %collective-permute-done.own_b_ref, bf16[1024,1024]{1,0:T(8,128)(2,1)S(1)} %bitcast.7, ...), custom_call_target="tpu_custom_call" | custom-call | flops 1610612736 | bytes 10485760 | tf_op jit(solution)/shard_map/expert/pallas_call | solution.py:163
  38.5 0.7 collective-permute-start.8
  39.2 2.3 %expert.5 = (bf16[96,1024]{1,0:T(8,128)(2,1)S(1)}, f32[96,1024]{1,0:T(8,128)S(1)}) custom-call(bf16[96,1152]{1,0:T(8,128)(2,1)S(1)} %collective-permute-done.16.peer_ref, bf16[48,1152]{1,0:T(8,128)(2,1)S(1)} %collective-permute-done.1.own_a_ref, bf16[48,1152]{1,0:T(8,128)(2,1)S(1)} %collective-permute-done.4.own_b_ref, bf16[1024,1024]{1,0:T(8,128)(2,1)S(1)} %bitcast.8, ...), custom_call_target="tpu_custom_call" | custom-call | flops 1610612736 | bytes 10485760 | tf_op jit(solution)/shard_map/expert/pallas_call | solution.py:163
  41.4 1.5 %collective-permute-start.18 = (bf16[96,1024]{1,0:T(8,128)(2,1)S(1)}, bf16[96,1024]{1,0:T(8,128)(2,1)S(1)}, u32[]{:S(2)}, u32[]{:S(2)}) collective-permute-start(bf16[96,1024]{1,0:T(8,128)(2,1)S(1)} %get-tuple-element.64), channel_id=1, source_target_pairs={{0,2},{1,3},{2,0},{3,1},{4,6},{5,7},{6,4},{7,5},{8,10},{9,11},{10,... | collective-permute-start | bytes 589832 | tf_op jit(solution)/shard_map/ppermute | solution.py:135
  42.9 2.3 %expert.6 = (bf16[96,1024]{1,0:T(8,128)(2,1)S(1)}, f32[96,1024]{1,0:T(8,128)S(1)}) custom-call(bf16[96,1152]{1,0:T(8,128)(2,1)S(1)} %collective-permute-done.15.peer_ref, bf16[48,1152]{1,0:T(8,128)(2,1)S(1)} %collective-permute-done.13.own_a_ref, bf16[48,1152]{1,0:T(8,128)(2,1)S(1)} %collective-permute-done.14.own_b_ref, bf16[1024,1024]{1,0:T(8,128)(2,1)S(1)} %bitcast.9, ...), custom_call_target="tpu_custom_call" | custom-call | flops 1610612736 | bytes 10485760 | tf_op jit(solution)/shard_map/expert/pallas_call | solution.py:163
  45.2 3.4 %collective-permute-done.10.own_b_ref = bf16[48,1152]{1,0:T(8,128)(2,1)S(1)} collective-permute-done((bf16[48,1152]{1,0:T(8,128)(2,1)S(1)}, bf16[48,1152]{1,0:T(8,128)(2,1)S(1)}, u32[]{:S(2)}, u32[]{:S(2)}) %collective-permute-start.10) | collective-permute-done | bytes 110624 | tf_op jit(solution)/shard_map/ppermute | solution.py:135
  49.2 1.7 %collective-permute-done.18 = bf16[96,1024]{1,0:T(8,128)(2,1)S(1)} collective-permute-done((bf16[96,1024]{1,0:T(8,128)(2,1)S(1)}, bf16[96,1024]{1,0:T(8,128)(2,1)S(1)}, u32[]{:S(2)}, u32[]{:S(2)}) %collective-permute-start.18) | collective-permute-done | bytes 196640 | tf_op jit(solution)/shard_map/ppermute | solution.py:135
  51.0 1.8 %collective-permute-start.23 = (bf16[48,1024]{1,0:T(8,128)(2,1)S(1)}, bf16[48,1024]{1,0:T(8,128)(2,1)S(1)}, u32[]{:S(2)}, u32[]{:S(2)}) collective-permute-start(bf16[48,1024]{1,0:T(8,128)(2,1)S(1)} %get-tuple-element.78), channel_id=1, source_target_pairs={{0,28},{4,24},{8,20},{12,16},{16,12},{20,8},{24,4},{28,0},{1,29},{... | collective-permute-start | bytes 294920 | tf_op jit(solution)/shard_map/ppermute | solution.py:135
  52.8 2.0 %collective-permute-start.19 = (bf16[96,1024]{1,0:T(8,128)(2,1)S(1)}, bf16[96,1024]{1,0:T(8,128)(2,1)S(1)}, u32[]{:S(2)}, u32[]{:S(2)}) collective-permute-start(bf16[96,1024]{1,0:T(8,128)(2,1)S(1)} %get-tuple-element.71), channel_id=1, source_target_pairs={{0,2},{1,3},{2,0},{3,1},{4,6},{5,7},{6,4},{7,5},{8,10},{9,11},{10,... | collective-permute-start | bytes 589832 | tf_op jit(solution)/shard_map/ppermute | solution.py:135
  54.8 2.1 %collective-permute-start.25 = (bf16[48,1024]{1,0:T(8,128)(2,1)S(1)}, bf16[48,1024]{1,0:T(8,128)(2,1)S(1)}, u32[]{:S(2)}, u32[]{:S(2)}) collective-permute-start(bf16[48,1024]{1,0:T(8,128)(2,1)S(1)} %get-tuple-element.77), channel_id=1, source_target_pairs={{0,24},{4,28},{8,16},{12,20},{16,8},{20,12},{24,0},{28,4},{1,25},{... | collective-permute-start | bytes 294920 | tf_op jit(solution)/shard_map/ppermute | solution.py:135
  57.0 2.3 %expert.7 = (bf16[96,1024]{1,0:T(8,128)(2,1)S(1)}, f32[96,1024]{1,0:T(8,128)S(1)}) custom-call(bf16[96,1152]{1,0:T(8,128)(2,1)S(1)} %collective-permute-done.11.peer_ref, bf16[48,1152]{1,0:T(8,128)(2,1)S(1)} %collective-permute-done.9.own_a_ref, bf16[48,1152]{1,0:T(8,128)(2,1)S(1)} %collective-permute-done.10.own_b_ref, bf16[1024,1024]{1,0:T(8,128)(2,1)S(1)} %bitcast.10, ...), custom_call_target="tpu_custom_call" | custom-call | flops 1610612736 | bytes 10485760 | tf_op jit(solution)/shard_map/expert/pallas_call | solution.py:163
  59.3 0.7 collective-permute-start.17
  60.0 0.9 %collective-permute-start.12 = (bf16[48,1024]{1,0:T(8,128)(2,1)S(1)}, bf16[48,1024]{1,0:T(8,128)(2,1)S(1)}, u32[]{:S(2)}, u32[]{:S(2)}) collective-permute-start(bf16[48,1024]{1,0:T(8,128)(2,1)S(1)} %get-tuple-element.57), channel_id=1, source_target_pairs={{0,4},{4,0},{8,12},{12,8},{16,20},{20,16},{24,28},{28,24},{1,5},{5... | collective-permute-start | bytes 294920 | tf_op jit(solution)/shard_map/ppermute | solution.py:135
  61.4 3.1 %collective-permute-start.22 = (bf16[48,1024]{1,0:T(8,128)(2,1)S(1)}, bf16[48,1024]{1,0:T(8,128)(2,1)S(1)}, u32[]{:S(2)}, u32[]{:S(2)}) collective-permute-start(bf16[48,1024]{1,0:T(8,128)(2,1)S(1)} %get-tuple-element.80), channel_id=1, source_target_pairs={{0,16},{4,20},{8,24},{12,28},{16,0},{20,4},{24,8},{28,12},{1,17},{... | collective-permute-start | bytes 294920 | tf_op jit(solution)/shard_map/ppermute | solution.py:135
  65.2 2.8 %collective-permute-start.20 = (bf16[48,1024]{1,0:T(8,128)(2,1)S(1)}, bf16[48,1024]{1,0:T(8,128)(2,1)S(1)}, u32[]{:S(2)}, u32[]{:S(2)}) collective-permute-start(bf16[48,1024]{1,0:T(8,128)(2,1)S(1)} %get-tuple-element.72), channel_id=1, source_target_pairs={{0,8},{4,12},{8,0},{12,4},{16,24},{20,28},{24,16},{28,20},{1,9},{5... | collective-permute-start | bytes 294920 | tf_op jit(solution)/shard_map/ppermute | solution.py:135
  68.3 1.4 %collective-permute-done.22.refs_4_ = bf16[48,1024]{1,0:T(8,128)(2,1)S(1)} collective-permute-done((bf16[48,1024]{1,0:T(8,128)(2,1)S(1)}, bf16[48,1024]{1,0:T(8,128)(2,1)S(1)}, u32[]{:S(2)}, u32[]{:S(2)}) %collective-permute-start.22) | collective-permute-done | bytes 98336 | tf_op jit(solution)/shard_map/ppermute | solution.py:135
  69.7 1.7 %collective-permute-done.21.refs_3_ = bf16[48,1024]{1,0:T(8,128)(2,1)S(1)} collective-permute-done((bf16[48,1024]{1,0:T(8,128)(2,1)S(1)}, bf16[48,1024]{1,0:T(8,128)(2,1)S(1)}, u32[]{:S(2)}, u32[]{:S(2)}) %collective-permute-start.21) | collective-permute-done | bytes 98336 | tf_op jit(solution)/shard_map/ppermute | solution.py:135
  71.8 1.5 %mix.1 = bf16[128,1024]{1,0:T(8,128)(2,1)} custom-call(s32[128,2]{1,0:T(8,128)S(1)} %copy.10.ids_ref, f32[128,2]{1,0:T(8,128)S(1)} %copy.11.combine_ref, bf16[48,1024]{1,0:T(8,128)(2,1)S(1)} %get-tuple-element.84.refs_0_, bf16[48,1024]{1,0:T(8,128)(2,1)S(1)} %collective-permute-done.12.refs_1_, bf16[48,1024]{1,0:T(8,128)(2,1)S(1)} %collective-permute-done.20.refs_2_, ...), custom_call_target="tpu_custom_call" | custom-call | flops 200000000 | bytes 2000000 | tf_op jit(solution)/shard_map/mix/pallas_call | solution.py:235
  (60 shorter events, 4.1 us)
Async XLA Ops:
  2.5 26.3 %copy-start.6 = (bf16[48,1152]{1,0:T(8,128)(2,1)S(1)}, bf16[48,1152]{1,0:T(8,128)(2,1)}, u32[]{:S(2)}) copy-start(bf16[48,1152]{1,0:T(8,128)(2,1)} %get-tuple-element.53) | copy-start | bytes 331780
  2.6 9.4 %collective-permute-start.4 = (bf16[48,1152]{1,0:T(8,128)(2,1)}, bf16[48,1152]{1,0:T(8,128)(2,1)S(1)}, u32[]{:S(2)}, u32[]{:S(2)}) collective-permute-start(bf16[48,1152]{1,0:T(8,128)(2,1)} %get-tuple-element.45), channel_id=1, source_target_pairs={{0,28},{4,24},{8,20},{12,16},{16,12},{20,8},{24,4},{28,0},{1,29},{... | collective-permute-start | bytes 331784 | tf_op jit(solution)/shard_map/ppermute | solution.py:135
  8.6 16.9 %collective-permute-start.3 = (bf16[1024,1024]{1,0:T(8,128)(2,1)}, bf16[1024,1024]{1,0:T(8,128)(2,1)S(1)}, u32[]{:S(2)}, u32[]{:S(2)}) collective-permute-start(bf16[1024,1024]{1,0:T(8,128)(2,1)} %bitcast.6), channel_id=1, source_target_pairs={{0,1},{1,0},{2,3},{3,2},{4,5},{5,4},{6,7},{7,6},{8,9},{9,8},{10,11... | collective-permute-start | bytes 6291464 | tf_op jit(solution)/shard_map/ppermute | solution.py:135
  11.9 13.6 %collective-permute-start.5 = (bf16[1024,1024]{1,0:T(8,128)(2,1)}, bf16[1024,1024]{1,0:T(8,128)(2,1)S(1)}, u32[]{:S(2)}, u32[]{:S(2)}) collective-permute-start(bf16[1024,1024]{1,0:T(8,128)(2,1)} %bitcast.11), channel_id=1, source_target_pairs={{0,1},{1,0},{2,3},{3,2},{4,5},{5,4},{6,7},{7,6},{8,9},{9,8},{10,11... | collective-permute-start | bytes 6291464 | tf_op jit(solution)/shard_map/ppermute | solution.py:135
  11.9 12.4 %collective-permute-start.6 = (bf16[32,3072]{1,0:T(8,128)(2,1)}, bf16[32,3072]{1,0:T(8,128)(2,1)S(1)}, u32[]{:S(2)}, u32[]{:S(2)}) collective-permute-start(bf16[32,3072]{1,0:T(8,128)(2,1)} %get-tuple-element.48), channel_id=1, source_target_pairs={{0,2},{1,3},{2,0},{3,1},{4,6},{5,7},{6,4},{7,5},{8,10},{9,11},{10,... | collective-permute-start | bytes 589832 | tf_op jit(solution)/shard_map/ppermute | solution.py:135
  13.5 5.9 %collective-permute-start = (bf16[48,1152]{1,0:T(8,128)(2,1)}, bf16[48,1152]{1,0:T(8,128)(2,1)S(1)}, u32[]{:S(2)}, u32[]{:S(2)}) collective-permute-start(bf16[48,1152]{1,0:T(8,128)(2,1)} %get-tuple-element.42), channel_id=1, source_target_pairs={{0,4},{4,0},{8,12},{12,8},{16,20},{20,16},{24,28},{28,24},{1,5},{5... | collective-permute-start | bytes 331784 | tf_op jit(solution)/shard_map/ppermute | solution.py:135
  14.9 8.8 %collective-permute-start.1 = (bf16[48,1152]{1,0:T(8,128)(2,1)}, bf16[48,1152]{1,0:T(8,128)(2,1)S(1)}, u32[]{:S(2)}, u32[]{:S(2)}) collective-permute-start(bf16[48,1152]{1,0:T(8,128)(2,1)} %get-tuple-element.43), channel_id=1, source_target_pairs={{0,24},{4,28},{8,16},{12,20},{16,8},{20,12},{24,0},{28,4},{1,25},{... | collective-permute-start | bytes 331784 | tf_op jit(solution)/shard_map/ppermute | solution.py:135
  19.4 9.4 %collective-permute-start.14 = (bf16[48,1152]{1,0:T(8,128)(2,1)}, bf16[48,1152]{1,0:T(8,128)(2,1)S(1)}, u32[]{:S(2)}, u32[]{:S(2)}) collective-permute-start(bf16[48,1152]{1,0:T(8,128)(2,1)} %get-tuple-element.60), channel_id=1, source_target_pairs={{0,20},{4,16},{8,28},{12,24},{16,4},{20,0},{24,12},{28,8},{1,21},{... | collective-permute-start | bytes 331784 | tf_op jit(solution)/shard_map/ppermute | solution.py:135
  23.7 12.5 %collective-permute-start.2 = (bf16[96,1152]{1,0:T(8,128)(2,1)S(1)}, bf16[96,1152]{1,0:T(8,128)(2,1)S(1)}, u32[]{:S(2)}, u32[]{:S(2)}) collective-permute-start(bf16[96,1152]{1,0:T(8,128)(2,1)S(1)} %pad_maximum_fusion.1), channel_id=1, source_target_pairs={{0,2},{1,3},{2,0},{3,1},{4,6},{5,7},{6,4},{7,5},{8,10},{9,11},{10,... | collective-permute-start | bytes 663560 | tf_op jit(solution)/shard_map/ppermute | solution.py:135
  24.3 11.9 %copy-start.1 = (bf16[1,1024,1024]{2,1,0:T(8,128)(2,1)S(1)}, bf16[1,1024,1024]{2,1,0:T(8,128)(2,1)}, u32[]{:S(2)}) copy-start(bf16[1,1024,1024]{2,1,0:T(8,128)(2,1)} %param.15) | copy-start | bytes 6291460
  24.3 11.9 %copy-start = (bf16[1,1024,1024]{2,1,0:T(8,128)(2,1)S(1)}, bf16[1,1024,1024]{2,1,0:T(8,128)(2,1)}, u32[]{:S(2)}) copy-start(bf16[1,1024,1024]{2,1,0:T(8,128)(2,1)} %param.14) | copy-start | bytes 6291460
  24.3 11.9 %copy-start.2 = (bf16[48,1152]{1,0:T(8,128)(2,1)S(1)}, bf16[48,1152]{1,0:T(8,128)(2,1)}, u32[]{:S(2)}) copy-start(bf16[48,1152]{1,0:T(8,128)(2,1)} %get-tuple-element.41.own_a_ref) | copy-start | bytes 331780
  25.4 10.7 %collective-permute-start.7 = (bf16[64,3072]{1,0:T(8,128)(2,1)S(1)}, bf16[64,3072]{1,0:T(8,128)(2,1)S(1)}, u32[]{:S(2)}, u32[]{:S(2)}) collective-permute-start(bf16[64,3072]{1,0:T(8,128)(2,1)S(1)} %pad_maximum_fusion), channel_id=1, source_target_pairs={{0,1},{1,0},{2,3},{3,2},{4,5},{5,4},{6,7},{7,6},{8,9},{9,8},{10,11... | collective-permute-start | bytes 1179656 | tf_op jit(solution)/shard_map/ppermute | solution.py:135
  25.5 9.1 %collective-permute-start.13 = (bf16[48,1152]{1,0:T(8,128)(2,1)}, bf16[48,1152]{1,0:T(8,128)(2,1)S(1)}, u32[]{:S(2)}, u32[]{:S(2)}) collective-permute-start(bf16[48,1152]{1,0:T(8,128)(2,1)} %get-tuple-element.59), channel_id=1, source_target_pairs={{0,16},{4,20},{8,24},{12,28},{16,0},{20,4},{24,8},{28,12},{1,17},{... | collective-permute-start | bytes 331784 | tf_op jit(solution)/shard_map/ppermute | solution.py:135
  27.3 11.9 %collective-permute-start.16 = (bf16[96,1152]{1,0:T(8,128)(2,1)S(1)}, bf16[96,1152]{1,0:T(8,128)(2,1)S(1)}, u32[]{:S(2)}, u32[]{:S(2)}) collective-permute-start(bf16[96,1152]{1,0:T(8,128)(2,1)S(1)} %pad_maximum_fusion.4), channel_id=1, source_target_pairs={{0,2},{1,3},{2,0},{3,1},{4,6},{5,7},{6,4},{7,5},{8,10},{9,11},{10,... | collective-permute-start | bytes 663560 | tf_op jit(solution)/shard_map/ppermute | solution.py:135
  28.9 16.3 %collective-permute-start.9 = (bf16[48,1152]{1,0:T(8,128)(2,1)S(1)}, bf16[48,1152]{1,0:T(8,128)(2,1)S(1)}, u32[]{:S(2)}, u32[]{:S(2)}) collective-permute-start(bf16[48,1152]{1,0:T(8,128)(2,1)S(1)} %copy-done.6), channel_id=1, source_target_pairs={{0,8},{4,12},{8,0},{12,4},{16,24},{20,28},{24,16},{28,20},{1,9},{5... | collective-permute-start | bytes 331784 | tf_op jit(solution)/shard_map/ppermute | solution.py:135
  34.6 8.3 %collective-permute-start.15 = (bf16[96,1152]{1,0:T(8,128)(2,1)S(1)}, bf16[96,1152]{1,0:T(8,128)(2,1)S(1)}, u32[]{:S(2)}, u32[]{:S(2)}) collective-permute-start(bf16[96,1152]{1,0:T(8,128)(2,1)S(1)} %pad_maximum_fusion.3), channel_id=1, source_target_pairs={{0,2},{1,3},{2,0},{3,1},{4,6},{5,7},{6,4},{7,5},{8,10},{9,11},{10,... | collective-permute-start | bytes 663560 | tf_op jit(solution)/shard_map/ppermute | solution.py:135
  38.5 18.4 %collective-permute-start.8 = (bf16[96,1024]{1,0:T(8,128)(2,1)S(1)}, bf16[96,1024]{1,0:T(8,128)(2,1)S(1)}, u32[]{:S(2)}, u32[]{:S(2)}) collective-permute-start(bf16[96,1024]{1,0:T(8,128)(2,1)S(1)} %get-tuple-element.51), channel_id=1, source_target_pairs={{0,2},{1,3},{2,0},{3,1},{4,6},{5,7},{6,4},{7,5},{8,10},{9,11},{10,... | collective-permute-start | bytes 589832 | tf_op jit(solution)/shard_map/ppermute | solution.py:135
  41.4 9.5 %collective-permute-start.18 = (bf16[96,1024]{1,0:T(8,128)(2,1)S(1)}, bf16[96,1024]{1,0:T(8,128)(2,1)S(1)}, u32[]{:S(2)}, u32[]{:S(2)}) collective-permute-start(bf16[96,1024]{1,0:T(8,128)(2,1)S(1)} %get-tuple-element.64), channel_id=1, source_target_pairs={{0,2},{1,3},{2,0},{3,1},{4,6},{5,7},{6,4},{7,5},{8,10},{9,11},{10,... | collective-permute-start | bytes 589832 | tf_op jit(solution)/shard_map/ppermute | solution.py:135
  42.9 5.6 %collective-permute-start.10 = (bf16[48,1152]{1,0:T(8,128)(2,1)S(1)}, bf16[48,1152]{1,0:T(8,128)(2,1)S(1)}, u32[]{:S(2)}, u32[]{:S(2)}) collective-permute-start(bf16[48,1152]{1,0:T(8,128)(2,1)S(1)} %copy-done.5), channel_id=1, source_target_pairs={{0,12},{4,8},{8,4},{12,0},{16,28},{20,24},{24,20},{28,16},{1,13},{... | collective-permute-start | bytes 331784 | tf_op jit(solution)/shard_map/ppermute | solution.py:135
  48.6 8.4 %collective-permute-start.11 = (bf16[96,1152]{1,0:T(8,128)(2,1)S(1)}, bf16[96,1152]{1,0:T(8,128)(2,1)S(1)}, u32[]{:S(2)}, u32[]{:S(2)}) collective-permute-start(bf16[96,1152]{1,0:T(8,128)(2,1)S(1)} %pad_maximum_fusion.2), channel_id=1, source_target_pairs={{0,2},{1,3},{2,0},{3,1},{4,6},{5,7},{6,4},{7,5},{8,10},{9,11},{10,... | collective-permute-start | bytes 663560 | tf_op jit(solution)/shard_map/ppermute | solution.py:135
  51.0 9.9 %collective-permute-start.23 = (bf16[48,1024]{1,0:T(8,128)(2,1)S(1)}, bf16[48,1024]{1,0:T(8,128)(2,1)S(1)}, u32[]{:S(2)}, u32[]{:S(2)}) collective-permute-start(bf16[48,1024]{1,0:T(8,128)(2,1)S(1)} %get-tuple-element.78), channel_id=1, source_target_pairs={{0,28},{4,24},{8,20},{12,16},{16,12},{20,8},{24,4},{28,0},{1,29},{... | collective-permute-start | bytes 294920 | tf_op jit(solution)/shard_map/ppermute | solution.py:135
  52.8 8.0 %collective-permute-start.19 = (bf16[96,1024]{1,0:T(8,128)(2,1)S(1)}, bf16[96,1024]{1,0:T(8,128)(2,1)S(1)}, u32[]{:S(2)}, u32[]{:S(2)}) collective-permute-start(bf16[96,1024]{1,0:T(8,128)(2,1)S(1)} %get-tuple-element.71), channel_id=1, source_target_pairs={{0,2},{1,3},{2,0},{3,1},{4,6},{5,7},{6,4},{7,5},{8,10},{9,11},{10,... | collective-permute-start | bytes 589832 | tf_op jit(solution)/shard_map/ppermute | solution.py:135
  54.8 10.4 %collective-permute-start.25 = (bf16[48,1024]{1,0:T(8,128)(2,1)S(1)}, bf16[48,1024]{1,0:T(8,128)(2,1)S(1)}, u32[]{:S(2)}, u32[]{:S(2)}) collective-permute-start(bf16[48,1024]{1,0:T(8,128)(2,1)S(1)} %get-tuple-element.77), channel_id=1, source_target_pairs={{0,24},{4,28},{8,16},{12,20},{16,8},{20,12},{24,0},{28,4},{1,25},{... | collective-permute-start | bytes 294920 | tf_op jit(solution)/shard_map/ppermute | solution.py:135
  59.3 8.8 %copy-start.3 = (s32[128,2]{0,1:T(2,128)S(1)}, s32[128,2]{0,1:T(2,128)}, u32[]{:S(2)}) copy-start(s32[128,2]{0,1:T(2,128)} %param.10) | copy-start | bytes 3076
  59.3 8.9 %copy-start.4 = (f32[128,2]{0,1:T(2,128)S(1)}, f32[128,2]{0,1:T(2,128)}, u32[]{:S(2)}) copy-start(f32[128,2]{0,1:T(2,128)} %param.11) | copy-start | bytes 3076
  59.3 5.7 %collective-permute-start.17 = (bf16[96,1024]{1,0:T(8,128)(2,1)S(1)}, bf16[96,1024]{1,0:T(8,128)(2,1)S(1)}, u32[]{:S(2)}, u32[]{:S(2)}) collective-permute-start(bf16[96,1024]{1,0:T(8,128)(2,1)S(1)} %get-tuple-element.70), channel_id=1, source_target_pairs={{0,2},{1,3},{2,0},{3,1},{4,6},{5,7},{6,4},{7,5},{8,10},{9,11},{10,... | collective-permute-start | bytes 589832 | tf_op jit(solution)/shard_map/ppermute | solution.py:135
  60.0 8.3 %collective-permute-start.12 = (bf16[48,1024]{1,0:T(8,128)(2,1)S(1)}, bf16[48,1024]{1,0:T(8,128)(2,1)S(1)}, u32[]{:S(2)}, u32[]{:S(2)}) collective-permute-start(bf16[48,1024]{1,0:T(8,128)(2,1)S(1)} %get-tuple-element.57), channel_id=1, source_target_pairs={{0,4},{4,0},{8,12},{12,8},{16,20},{20,16},{24,28},{28,24},{1,5},{5... | collective-permute-start | bytes 294920 | tf_op jit(solution)/shard_map/ppermute | solution.py:135
  60.9 7.4 %collective-permute-start.24 = (bf16[48,1024]{1,0:T(8,128)(2,1)S(1)}, bf16[48,1024]{1,0:T(8,128)(2,1)S(1)}, u32[]{:S(2)}, u32[]{:S(2)}) collective-permute-start(bf16[48,1024]{1,0:T(8,128)(2,1)S(1)} %get-tuple-element.76), channel_id=1, source_target_pairs={{0,20},{4,16},{8,28},{12,24},{16,4},{20,0},{24,12},{28,8},{1,21},{... | collective-permute-start | bytes 294920 | tf_op jit(solution)/shard_map/ppermute | solution.py:135
  61.4 8.3 %collective-permute-start.22 = (bf16[48,1024]{1,0:T(8,128)(2,1)S(1)}, bf16[48,1024]{1,0:T(8,128)(2,1)S(1)}, u32[]{:S(2)}, u32[]{:S(2)}) collective-permute-start(bf16[48,1024]{1,0:T(8,128)(2,1)S(1)} %get-tuple-element.80), channel_id=1, source_target_pairs={{0,16},{4,20},{8,24},{12,28},{16,0},{20,4},{24,8},{28,12},{1,17},{... | collective-permute-start | bytes 294920 | tf_op jit(solution)/shard_map/ppermute | solution.py:135
  65.1 6.3 %collective-permute-start.21 = (bf16[48,1024]{1,0:T(8,128)(2,1)S(1)}, bf16[48,1024]{1,0:T(8,128)(2,1)S(1)}, u32[]{:S(2)}, u32[]{:S(2)}) collective-permute-start(bf16[48,1024]{1,0:T(8,128)(2,1)S(1)} %get-tuple-element.73), channel_id=1, source_target_pairs={{0,12},{4,8},{8,4},{12,0},{16,28},{20,24},{24,20},{28,16},{1,13},{... | collective-permute-start | bytes 294920 | tf_op jit(solution)/shard_map/ppermute | solution.py:135
  65.2 6.6 %collective-permute-start.20 = (bf16[48,1024]{1,0:T(8,128)(2,1)S(1)}, bf16[48,1024]{1,0:T(8,128)(2,1)S(1)}, u32[]{:S(2)}, u32[]{:S(2)}) collective-permute-start(bf16[48,1024]{1,0:T(8,128)(2,1)S(1)} %get-tuple-element.72), channel_id=1, source_target_pairs={{0,8},{4,12},{8,0},{12,4},{16,24},{20,28},{24,16},{28,20},{1,9},{5... | collective-permute-start | bytes 294920 | tf_op jit(solution)/shard_map/ppermute | solution.py:135
  (1 other events, 4.4 us)

commit v4 on v3

--- a/solution.py
+++ b/solution.py
@@ -115,14 +115,13 @@
     place = jnp.dot(earlier, hit, preferred_element_type=F32)
     back = jnp.concatenate([b[...] for b in backs], axis=0)
     spot = iota((count, experts * cap), 1).astype(F32)
-    mixed = None
-    for k, choice in enumerate((first, second)):
+    selects = []
+    for choice in (first, second):
         at = jnp.sum(jnp.where(choice == lane, place, 0.0), axis=1, keepdims=True)
         at = at + (choice * cap).astype(F32)
-        select = (at == spot).astype(F32).astype(BF16)
-        picked = jnp.dot(select, back, preferred_element_type=F32)
-        term = combine_ref[:, k : k + 1] * picked
-        mixed = term if mixed is None else mixed + term
+        selects.append((at == spot).astype(F32).astype(BF16))
+    picked = jnp.dot(jnp.concatenate(selects, axis=0), back, preferred_element_type=F32)
+    mixed = combine_ref[:, 0:1] * picked[:count] + combine_ref[:, 1:2] * picked[count:]
     out_ref[...] = mixed.astype(BF16)
 
 

time: 73.5 us -> 73.5 us (level)
  no operation moved by 1% of the time
where the time goes in v4:
time: 73.5 us; the launch traced here: 73.3 us
  starting transfers between devices  38.7 us (53%)
  waiting for transfers between devices  17.6 us (24%)
  Pallas kernels  13.1 us (18%)
  other arithmetic  2.27 us (3%)
  local copies, waits for them, and re-layouts  1.36 us (2%)
    ppermute x26, starting transfers between devices, flip(): return lax.ppermute(x, axis, [(i, i ^ bit) for i in range(size)])  38.7 us
    ppermute x26, waiting for transfers between devices, flip(): return lax.ppermute(x, axis, [(i, i ^ bit) for i in range(size)])  17.6 us
    pallas_call x4, Pallas kernels, run_expert(): pl.pallas_call(functools.partial(expert_kernel, rank), out_shape=[jax.Sha...  9 us
    pallas_call x1, Pallas kernels, local_pairs(): pl.pallas_call(functools.partial(prep_kernel, cap), out_shape=[jax.ShapeD...  2.55 us
    concatenate x5, other arithmetic, both(): return jnp.concatenate([a, b], axis=0)  2.08 us
    pallas_call x1, Pallas kernels, local_pairs(): pl.pallas_call(functools.partial(mix_kernel, cap), out_shape=jax.ShapeDty...  1.55 us
  transfers between devices with their start and end apart: 26, of which 8 were waited for; matrix products, arithmetic and copies ran while one was open for 5% of the time, Pallas kernels for 12%

profile of v4, /device:TPU:0, one launch (start us, length us, event | category | flops | bytes accessed | tf_op | source)
XLA Modules:
  0.0 73.3 jit_solution(240616138024738106)
XLA Ops:
  0.0 2.5 %prep.1 = (bf16[32,3072]{1,0:T(8,128)(2,1)}, bf16[32,3072]{1,0:T(8,128)(2,1)}, bf16[48,1152]{1,0:T(8,128)(2,1)}, bf16[48,1152]{1,0:T(8,128)(2,1)}, bf16[48,1152]...) custom-call(s32[8]{0:T(128)} %slot_ref.1, ...), custom_call_target="tpu_custom_call" | custom-call | flops 100000000 | bytes 2000000 | tf_op jit(solution)/shard_map/prep/pallas_call | solution.py:149
  2.6 6.0 %collective-permute-start.4 = (bf16[48,1152]{1,0:T(8,128)(2,1)}, bf16[48,1152]{1,0:T(8,128)(2,1)S(1)}, u32[]{:S(2)}, u32[]{:S(2)}) collective-permute-start(bf16[48,1152]{1,0:T(8,128)(2,1)} %get-tuple-element.45), channel_id=1, source_target_pairs={{0,28},{4,24},{8,20},{12,16},{16,12},{20,8},{24,4},{28,0},{1,29},{... | collective-permute-start | bytes 331784 | tf_op jit(solution)/shard_map/ppermute | solution.py:134
  8.6 3.4 %collective-permute-done.4.own_b_ref = bf16[48,1152]{1,0:T(8,128)(2,1)S(1)} collective-permute-done((bf16[48,1152]{1,0:T(8,128)(2,1)}, bf16[48,1152]{1,0:T(8,128)(2,1)S(1)}, u32[]{:S(2)}, u32[]{:S(2)}) %collective-permute-start.4) | collective-permute-done | bytes 110624 | tf_op jit(solution)/shard_map/ppermute | solution.py:134
  11.9 1.5 %collective-permute-start.6 = (bf16[32,3072]{1,0:T(8,128)(2,1)}, bf16[32,3072]{1,0:T(8,128)(2,1)S(1)}, u32[]{:S(2)}, u32[]{:S(2)}) collective-permute-start(bf16[32,3072]{1,0:T(8,128)(2,1)} %get-tuple-element.48), channel_id=1, source_target_pairs={{0,2},{1,3},{2,0},{3,1},{4,6},{5,7},{6,4},{7,5},{8,10},{9,11},{10,... | collective-permute-start | bytes 589832 | tf_op jit(solution)/shard_map/ppermute | solution.py:134
  13.5 1.4 %collective-permute-start = (bf16[48,1152]{1,0:T(8,128)(2,1)}, bf16[48,1152]{1,0:T(8,128)(2,1)S(1)}, u32[]{:S(2)}, u32[]{:S(2)}) collective-permute-start(bf16[48,1152]{1,0:T(8,128)(2,1)} %get-tuple-element.42), channel_id=1, source_target_pairs={{0,4},{4,0},{8,12},{12,8},{16,20},{20,16},{24,28},{28,24},{1,5},{5... | collective-permute-start | bytes 331784 | tf_op jit(solution)/shard_map/ppermute | solution.py:134
  14.9 3.6 %collective-permute-start.1 = (bf16[48,1152]{1,0:T(8,128)(2,1)}, bf16[48,1152]{1,0:T(8,128)(2,1)S(1)}, u32[]{:S(2)}, u32[]{:S(2)}) collective-permute-start(bf16[48,1152]{1,0:T(8,128)(2,1)} %get-tuple-element.43), channel_id=1, source_target_pairs={{0,24},{4,28},{8,16},{12,20},{16,8},{20,12},{24,0},{28,4},{1,25},{... | collective-permute-start | bytes 331784 | tf_op jit(solution)/shard_map/ppermute | solution.py:134
  18.5 0.9 %constant_dynamic-update-slice_fusion.2 = bf16[128,3072]{1,0:T(8,128)(2,1)S(1)} fusion(bf16[32,3072]{1,0:T(8,128)(2,1)} %get-tuple-element.47), kind=kLoop, calls=%fused_computation.11 | loop fusion | bytes 393216
  19.4 3.3 %collective-permute-start.14 = (bf16[48,1152]{1,0:T(8,128)(2,1)}, bf16[48,1152]{1,0:T(8,128)(2,1)S(1)}, u32[]{:S(2)}, u32[]{:S(2)}) collective-permute-start(bf16[48,1152]{1,0:T(8,128)(2,1)} %get-tuple-element.60), channel_id=1, source_target_pairs={{0,20},{4,16},{8,28},{12,24},{16,4},{20,0},{24,12},{28,8},{1,21},{... | collective-permute-start | bytes 331784 | tf_op jit(solution)/shard_map/ppermute | solution.py:134
  22.8 0.9 %pad_maximum_fusion.1 = bf16[96,1152]{1,0:T(8,128)(2,1)S(1)} fusion(bf16[48,1152]{1,0:T(8,128)(2,1)S(1)} %collective-permute-done.own_b_ref, bf16[48,1152]{1,0:T(8,128)(2,1)} %get-tuple-element.41.own_a_ref), kind=kLoop, calls=%fused_computation.5 | loop fusion | flops 442368 | bytes 442368 | tf_op jit(solution)/shard_map/concatenate | solution.py:182
  24.3 1.1 %pad_maximum_fusion = bf16[64,3072]{1,0:T(8,128)(2,1)S(1)} fusion(bf16[32,3072]{1,0:T(8,128)(2,1)S(1)} %collective-permute-done.6, bf16[32,3072]{1,0:T(8,128)(2,1)} %get-tuple-element.47), kind=kLoop, calls=%fused_computation | loop fusion | flops 786432 | bytes 786432 | tf_op jit(solution)/shard_map/concatenate | solution.py:182
  25.5 1.7 %collective-permute-start.13 = (bf16[48,1152]{1,0:T(8,128)(2,1)}, bf16[48,1152]{1,0:T(8,128)(2,1)S(1)}, u32[]{:S(2)}, u32[]{:S(2)}) collective-permute-start(bf16[48,1152]{1,0:T(8,128)(2,1)} %get-tuple-element.59), channel_id=1, source_target_pairs={{0,16},{4,20},{8,24},{12,28},{16,0},{20,4},{24,8},{28,12},{1,17},{... | collective-permute-start | bytes 331784 | tf_op jit(solution)/shard_map/ppermute | solution.py:134
  27.3 1.6 %collective-permute-start.16 = (bf16[96,1152]{1,0:T(8,128)(2,1)S(1)}, bf16[96,1152]{1,0:T(8,128)(2,1)S(1)}, u32[]{:S(2)}, u32[]{:S(2)}) collective-permute-start(bf16[96,1152]{1,0:T(8,128)(2,1)S(1)} %pad_maximum_fusion.4), channel_id=1, source_target_pairs={{0,2},{1,3},{2,0},{3,1},{4,6},{5,7},{6,4},{7,5},{8,10},{9,11},{10,... | collective-permute-start | bytes 663560 | tf_op jit(solution)/shard_map/ppermute | solution.py:134
  29.5 5.1 %collective-permute-done.13.own_a_ref = bf16[48,1152]{1,0:T(8,128)(2,1)S(1)} collective-permute-done((bf16[48,1152]{1,0:T(8,128)(2,1)}, bf16[48,1152]{1,0:T(8,128)(2,1)S(1)}, u32[]{:S(2)}, u32[]{:S(2)}) %collective-permute-start.13) | collective-permute-done | bytes 110624 | tf_op jit(solution)/shard_map/ppermute | solution.py:134
  34.6 1.5 %collective-permute-start.15 = (bf16[96,1152]{1,0:T(8,128)(2,1)S(1)}, bf16[96,1152]{1,0:T(8,128)(2,1)S(1)}, u32[]{:S(2)}, u32[]{:S(2)}) collective-permute-start(bf16[96,1152]{1,0:T(8,128)(2,1)S(1)} %pad_maximum_fusion.3), channel_id=1, source_target_pairs={{0,2},{1,3},{2,0},{3,1},{4,6},{5,7},{6,4},{7,5},{8,10},{9,11},{10,... | collective-permute-start | bytes 663560 | tf_op jit(solution)/shard_map/ppermute | solution.py:134
  36.2 2.2 %expert.4 = (bf16[96,1024]{1,0:T(8,128)(2,1)S(1)}, f32[96,1024]{1,0:T(8,128)S(1)}) custom-call(bf16[96,1152]{1,0:T(8,128)(2,1)S(1)} %collective-permute-done.2.peer_ref, bf16[48,1152]{1,0:T(8,128)(2,1)S(1)} %copy-done.2, bf16[48,1152]{1,0:T(8,128)(2,1)S(1)} %collective-permute-done.own_b_ref, bf16[1024,1024]{1,0:T(8,128)(2,1)S(1)} %bitcast.7, ...), custom_call_target="tpu_custom_call" | custom-call | flops 1610612736 | bytes 10485760 | tf_op jit(solution)/shard_map/expert/pallas_call | solution.py:162
  38.5 0.7 collective-permute-start.8
  39.2 2.3 %expert.5 = (bf16[96,1024]{1,0:T(8,128)(2,1)S(1)}, f32[96,1024]{1,0:T(8,128)S(1)}) custom-call(bf16[96,1152]{1,0:T(8,128)(2,1)S(1)} %collective-permute-done.16.peer_ref, bf16[48,1152]{1,0:T(8,128)(2,1)S(1)} %collective-permute-done.1.own_a_ref, bf16[48,1152]{1,0:T(8,128)(2,1)S(1)} %collective-permute-done.4.own_b_ref, bf16[1024,1024]{1,0:T(8,128)(2,1)S(1)} %bitcast.8, ...), custom_call_target="tpu_custom_call" | custom-call | flops 1610612736 | bytes 10485760 | tf_op jit(solution)/shard_map/expert/pallas_call | solution.py:162
  41.4 1.5 %collective-permute-start.18 = (bf16[96,1024]{1,0:T(8,128)(2,1)S(1)}, bf16[96,1024]{1,0:T(8,128)(2,1)S(1)}, u32[]{:S(2)}, u32[]{:S(2)}) collective-permute-start(bf16[96,1024]{1,0:T(8,128)(2,1)S(1)} %get-tuple-element.64), channel_id=1, source_target_pairs={{0,2},{1,3},{2,0},{3,1},{4,6},{5,7},{6,4},{7,5},{8,10},{9,11},{10,... | collective-permute-start | bytes 589832 | tf_op jit(solution)/shard_map/ppermute | solution.py:134
  42.9 2.3 %expert.6 = (bf16[96,1024]{1,0:T(8,128)(2,1)S(1)}, f32[96,1024]{1,0:T(8,128)S(1)}) custom-call(bf16[96,1152]{1,0:T(8,128)(2,1)S(1)} %collective-permute-done.15.peer_ref, bf16[48,1152]{1,0:T(8,128)(2,1)S(1)} %collective-permute-done.13.own_a_ref, bf16[48,1152]{1,0:T(8,128)(2,1)S(1)} %collective-permute-done.14.own_b_ref, bf16[1024,1024]{1,0:T(8,128)(2,1)S(1)} %bitcast.9, ...), custom_call_target="tpu_custom_call" | custom-call | flops 1610612736 | bytes 10485760 | tf_op jit(solution)/shard_map/expert/pallas_call | solution.py:162
  45.2 3.4 %collective-permute-done.10.own_b_ref = bf16[48,1152]{1,0:T(8,128)(2,1)S(1)} collective-permute-done((bf16[48,1152]{1,0:T(8,128)(2,1)S(1)}, bf16[48,1152]{1,0:T(8,128)(2,1)S(1)}, u32[]{:S(2)}, u32[]{:S(2)}) %collective-permute-start.10) | collective-permute-done | bytes 110624 | tf_op jit(solution)/shard_map/ppermute | solution.py:134
  49.2 1.7 %collective-permute-done.18 = bf16[96,1024]{1,0:T(8,128)(2,1)S(1)} collective-permute-done((bf16[96,1024]{1,0:T(8,128)(2,1)S(1)}, bf16[96,1024]{1,0:T(8,128)(2,1)S(1)}, u32[]{:S(2)}, u32[]{:S(2)}) %collective-permute-start.18) | collective-permute-done | bytes 196640 | tf_op jit(solution)/shard_map/ppermute | solution.py:134
  51.0 1.8 %collective-permute-start.23 = (bf16[48,1024]{1,0:T(8,128)(2,1)S(1)}, bf16[48,1024]{1,0:T(8,128)(2,1)S(1)}, u32[]{:S(2)}, u32[]{:S(2)}) collective-permute-start(bf16[48,1024]{1,0:T(8,128)(2,1)S(1)} %get-tuple-element.78), channel_id=1, source_target_pairs={{0,28},{4,24},{8,20},{12,16},{16,12},{20,8},{24,4},{28,0},{1,29},{... | collective-permute-start | bytes 294920 | tf_op jit(solution)/shard_map/ppermute | solution.py:134
  52.8 2.0 %collective-permute-start.19 = (bf16[96,1024]{1,0:T(8,128)(2,1)S(1)}, bf16[96,1024]{1,0:T(8,128)(2,1)S(1)}, u32[]{:S(2)}, u32[]{:S(2)}) collective-permute-start(bf16[96,1024]{1,0:T(8,128)(2,1)S(1)} %get-tuple-element.71), channel_id=1, source_target_pairs={{0,2},{1,3},{2,0},{3,1},{4,6},{5,7},{6,4},{7,5},{8,10},{9,11},{10,... | collective-permute-start | bytes 589832 | tf_op jit(solution)/shard_map/ppermute | solution.py:134
  54.8 2.1 %collective-permute-start.25 = (bf16[48,1024]{1,0:T(8,128)(2,1)S(1)}, bf16[48,1024]{1,0:T(8,128)(2,1)S(1)}, u32[]{:S(2)}, u32[]{:S(2)}) collective-permute-start(bf16[48,1024]{1,0:T(8,128)(2,1)S(1)} %get-tuple-element.77), channel_id=1, source_target_pairs={{0,24},{4,28},{8,16},{12,20},{16,8},{20,12},{24,0},{28,4},{1,25},{... | collective-permute-start | bytes 294920 | tf_op jit(solution)/shard_map/ppermute | solution.py:134
  57.0 2.3 %expert.7 = (bf16[96,1024]{1,0:T(8,128)(2,1)S(1)}, f32[96,1024]{1,0:T(8,128)S(1)}) custom-call(bf16[96,1152]{1,0:T(8,128)(2,1)S(1)} %collective-permute-done.11.peer_ref, bf16[48,1152]{1,0:T(8,128)(2,1)S(1)} %collective-permute-done.9.own_a_ref, bf16[48,1152]{1,0:T(8,128)(2,1)S(1)} %collective-permute-done.10.own_b_ref, bf16[1024,1024]{1,0:T(8,128)(2,1)S(1)} %bitcast.10, ...), custom_call_target="tpu_custom_call" | custom-call | flops 1610612736 | bytes 10485760 | tf_op jit(solution)/shard_map/expert/pallas_call | solution.py:162
  59.3 0.7 collective-permute-start.17
  60.0 0.9 %collective-permute-start.12 = (bf16[48,1024]{1,0:T(8,128)(2,1)S(1)}, bf16[48,1024]{1,0:T(8,128)(2,1)S(1)}, u32[]{:S(2)}, u32[]{:S(2)}) collective-permute-start(bf16[48,1024]{1,0:T(8,128)(2,1)S(1)} %get-tuple-element.57), channel_id=1, source_target_pairs={{0,4},{4,0},{8,12},{12,8},{16,20},{20,16},{24,28},{28,24},{1,5},{5... | collective-permute-start | bytes 294920 | tf_op jit(solution)/shard_map/ppermute | solution.py:134
  61.4 3.1 %collective-permute-start.22 = (bf16[48,1024]{1,0:T(8,128)(2,1)S(1)}, bf16[48,1024]{1,0:T(8,128)(2,1)S(1)}, u32[]{:S(2)}, u32[]{:S(2)}) collective-permute-start(bf16[48,1024]{1,0:T(8,128)(2,1)S(1)} %get-tuple-element.80), channel_id=1, source_target_pairs={{0,16},{4,20},{8,24},{12,28},{16,0},{20,4},{24,8},{28,12},{1,17},{... | collective-permute-start | bytes 294920 | tf_op jit(solution)/shard_map/ppermute | solution.py:134
  65.2 2.8 %collective-permute-start.20 = (bf16[48,1024]{1,0:T(8,128)(2,1)S(1)}, bf16[48,1024]{1,0:T(8,128)(2,1)S(1)}, u32[]{:S(2)}, u32[]{:S(2)}) collective-permute-start(bf16[48,1024]{1,0:T(8,128)(2,1)S(1)} %get-tuple-element.72), channel_id=1, source_target_pairs={{0,8},{4,12},{8,0},{12,4},{16,24},{20,28},{24,16},{28,20},{1,9},{5... | collective-permute-start | bytes 294920 | tf_op jit(solution)/shard_map/ppermute | solution.py:134
  68.3 1.4 %collective-permute-done.22.refs_4_ = bf16[48,1024]{1,0:T(8,128)(2,1)S(1)} collective-permute-done((bf16[48,1024]{1,0:T(8,128)(2,1)S(1)}, bf16[48,1024]{1,0:T(8,128)(2,1)S(1)}, u32[]{:S(2)}, u32[]{:S(2)}) %collective-permute-start.22) | collective-permute-done | bytes 98336 | tf_op jit(solution)/shard_map/ppermute | solution.py:134
  69.7 1.7 %collective-permute-done.21.refs_3_ = bf16[48,1024]{1,0:T(8,128)(2,1)S(1)} collective-permute-done((bf16[48,1024]{1,0:T(8,128)(2,1)S(1)}, bf16[48,1024]{1,0:T(8,128)(2,1)S(1)}, u32[]{:S(2)}, u32[]{:S(2)}) %collective-permute-start.21) | collective-permute-done | bytes 98336 | tf_op jit(solution)/shard_map/ppermute | solution.py:134
  71.8 1.6 %mix.1 = bf16[128,1024]{1,0:T(8,128)(2,1)} custom-call(s32[128,2]{1,0:T(8,128)S(1)} %copy.10.ids_ref, f32[128,2]{1,0:T(8,128)S(1)} %copy.11.combine_ref, bf16[48,1024]{1,0:T(8,128)(2,1)S(1)} %get-tuple-element.84.refs_0_, bf16[48,1024]{1,0:T(8,128)(2,1)S(1)} %collective-permute-done.12.refs_1_, bf16[48,1024]{1,0:T(8,128)(2,1)S(1)} %collective-permute-done.20.refs_2_, ...), custom_call_target="tpu_custom_call" | custom-call | flops 200000000 | bytes 2000000 | tf_op jit(solution)/shard_map/mix/pallas_call | solution.py:234
  (60 shorter events, 4.1 us)
Async XLA Ops:
  2.5 26.3 %copy-start.6 = (bf16[48,1152]{1,0:T(8,128)(2,1)S(1)}, bf16[48,1152]{1,0:T(8,128)(2,1)}, u32[]{:S(2)}) copy-start(bf16[48,1152]{1,0:T(8,128)(2,1)} %get-tuple-element.53) | copy-start | bytes 331780
  2.6 9.4 %collective-permute-start.4 = (bf16[48,1152]{1,0:T(8,128)(2,1)}, bf16[48,1152]{1,0:T(8,128)(2,1)S(1)}, u32[]{:S(2)}, u32[]{:S(2)}) collective-permute-start(bf16[48,1152]{1,0:T(8,128)(2,1)} %get-tuple-element.45), channel_id=1, source_target_pairs={{0,28},{4,24},{8,20},{12,16},{16,12},{20,8},{24,4},{28,0},{1,29},{... | collective-permute-start | bytes 331784 | tf_op jit(solution)/shard_map/ppermute | solution.py:134
  8.6 16.9 %collective-permute-start.3 = (bf16[1024,1024]{1,0:T(8,128)(2,1)}, bf16[1024,1024]{1,0:T(8,128)(2,1)S(1)}, u32[]{:S(2)}, u32[]{:S(2)}) collective-permute-start(bf16[1024,1024]{1,0:T(8,128)(2,1)} %bitcast.6), channel_id=1, source_target_pairs={{0,1},{1,0},{2,3},{3,2},{4,5},{5,4},{6,7},{7,6},{8,9},{9,8},{10,11... | collective-permute-start | bytes 6291464 | tf_op jit(solution)/shard_map/ppermute | solution.py:134
  11.9 13.6 %collective-permute-start.5 = (bf16[1024,1024]{1,0:T(8,128)(2,1)}, bf16[1024,1024]{1,0:T(8,128)(2,1)S(1)}, u32[]{:S(2)}, u32[]{:S(2)}) collective-permute-start(bf16[1024,1024]{1,0:T(8,128)(2,1)} %bitcast.11), channel_id=1, source_target_pairs={{0,1},{1,0},{2,3},{3,2},{4,5},{5,4},{6,7},{7,6},{8,9},{9,8},{10,11... | collective-permute-start | bytes 6291464 | tf_op jit(solution)/shard_map/ppermute | solution.py:134
  11.9 12.4 %collective-permute-start.6 = (bf16[32,3072]{1,0:T(8,128)(2,1)}, bf16[32,3072]{1,0:T(8,128)(2,1)S(1)}, u32[]{:S(2)}, u32[]{:S(2)}) collective-permute-start(bf16[32,3072]{1,0:T(8,128)(2,1)} %get-tuple-element.48), channel_id=1, source_target_pairs={{0,2},{1,3},{2,0},{3,1},{4,6},{5,7},{6,4},{7,5},{8,10},{9,11},{10,... | collective-permute-start | bytes 589832 | tf_op jit(solution)/shard_map/ppermute | solution.py:134
  13.5 5.9 %collective-permute-start = (bf16[48,1152]{1,0:T(8,128)(2,1)}, bf16[48,1152]{1,0:T(8,128)(2,1)S(1)}, u32[]{:S(2)}, u32[]{:S(2)}) collective-permute-start(bf16[48,1152]{1,0:T(8,128)(2,1)} %get-tuple-element.42), channel_id=1, source_target_pairs={{0,4},{4,0},{8,12},{12,8},{16,20},{20,16},{24,28},{28,24},{1,5},{5... | collective-permute-start | bytes 331784 | tf_op jit(solution)/shard_map/ppermute | solution.py:134
  14.9 8.8 %collective-permute-start.1 = (bf16[48,1152]{1,0:T(8,128)(2,1)}, bf16[48,1152]{1,0:T(8,128)(2,1)S(1)}, u32[]{:S(2)}, u32[]{:S(2)}) collective-permute-start(bf16[48,1152]{1,0:T(8,128)(2,1)} %get-tuple-element.43), channel_id=1, source_target_pairs={{0,24},{4,28},{8,16},{12,20},{16,8},{20,12},{24,0},{28,4},{1,25},{... | collective-permute-start | bytes 331784 | tf_op jit(solution)/shard_map/ppermute | solution.py:134
  19.4 9.4 %collective-permute-start.14 = (bf16[48,1152]{1,0:T(8,128)(2,1)}, bf16[48,1152]{1,0:T(8,128)(2,1)S(1)}, u32[]{:S(2)}, u32[]{:S(2)}) collective-permute-start(bf16[48,1152]{1,0:T(8,128)(2,1)} %get-tuple-element.60), channel_id=1, source_target_pairs={{0,20},{4,16},{8,28},{12,24},{16,4},{20,0},{24,12},{28,8},{1,21},{... | collective-permute-start | bytes 331784 | tf_op jit(solution)/shard_map/ppermute | solution.py:134
  23.7 12.5 %collective-permute-start.2 = (bf16[96,1152]{1,0:T(8,128)(2,1)S(1)}, bf16[96,1152]{1,0:T(8,128)(2,1)S(1)}, u32[]{:S(2)}, u32[]{:S(2)}) collective-permute-start(bf16[96,1152]{1,0:T(8,128)(2,1)S(1)} %pad_maximum_fusion.1), channel_id=1, source_target_pairs={{0,2},{1,3},{2,0},{3,1},{4,6},{5,7},{6,4},{7,5},{8,10},{9,11},{10,... | collective-permute-start | bytes 663560 | tf_op jit(solution)/shard_map/ppermute | solution.py:134
  24.3 11.9 %copy-start.1 = (bf16[1,1024,1024]{2,1,0:T(8,128)(2,1)S(1)}, bf16[1,1024,1024]{2,1,0:T(8,128)(2,1)}, u32[]{:S(2)}) copy-start(bf16[1,1024,1024]{2,1,0:T(8,128)(2,1)} %param.15) | copy-start | bytes 6291460
  24.3 11.9 %copy-start = (bf16[1,1024,1024]{2,1,0:T(8,128)(2,1)S(1)}, bf16[1,1024,1024]{2,1,0:T(8,128)(2,1)}, u32[]{:S(2)}) copy-start(bf16[1,1024,1024]{2,1,0:T(8,128)(2,1)} %param.14) | copy-start | bytes 6291460
  24.3 11.9 %copy-start.2 = (bf16[48,1152]{1,0:T(8,128)(2,1)S(1)}, bf16[48,1152]{1,0:T(8,128)(2,1)}, u32[]{:S(2)}) copy-start(bf16[48,1152]{1,0:T(8,128)(2,1)} %get-tuple-element.41.own_a_ref) | copy-start | bytes 331780
  25.4 10.7 %collective-permute-start.7 = (bf16[64,3072]{1,0:T(8,128)(2,1)S(1)}, bf16[64,3072]{1,0:T(8,128)(2,1)S(1)}, u32[]{:S(2)}, u32[]{:S(2)}) collective-permute-start(bf16[64,3072]{1,0:T(8,128)(2,1)S(1)} %pad_maximum_fusion), channel_id=1, source_target_pairs={{0,1},{1,0},{2,3},{3,2},{4,5},{5,4},{6,7},{7,6},{8,9},{9,8},{10,11... | collective-permute-start | bytes 1179656 | tf_op jit(solution)/shard_map/ppermute | solution.py:134
  25.5 9.1 %collective-permute-start.13 = (bf16[48,1152]{1,0:T(8,128)(2,1)}, bf16[48,1152]{1,0:T(8,128)(2,1)S(1)}, u32[]{:S(2)}, u32[]{:S(2)}) collective-permute-start(bf16[48,1152]{1,0:T(8,128)(2,1)} %get-tuple-element.59), channel_id=1, source_target_pairs={{0,16},{4,20},{8,24},{12,28},{16,0},{20,4},{24,8},{28,12},{1,17},{... | collective-permute-start | bytes 331784 | tf_op jit(solution)/shard_map/ppermute | solution.py:134
  27.3 11.9 %collective-permute-start.16 = (bf16[96,1152]{1,0:T(8,128)(2,1)S(1)}, bf16[96,1152]{1,0:T(8,128)(2,1)S(1)}, u32[]{:S(2)}, u32[]{:S(2)}) collective-permute-start(bf16[96,1152]{1,0:T(8,128)(2,1)S(1)} %pad_maximum_fusion.4), channel_id=1, source_target_pairs={{0,2},{1,3},{2,0},{3,1},{4,6},{5,7},{6,4},{7,5},{8,10},{9,11},{10,... | collective-permute-start | bytes 663560 | tf_op jit(solution)/shard_map/ppermute | solution.py:134
  28.9 16.3 %collective-permute-start.9 = (bf16[48,1152]{1,0:T(8,128)(2,1)S(1)}, bf16[48,1152]{1,0:T(8,128)(2,1)S(1)}, u32[]{:S(2)}, u32[]{:S(2)}) collective-permute-start(bf16[48,1152]{1,0:T(8,128)(2,1)S(1)} %copy-done.6), channel_id=1, source_target_pairs={{0,8},{4,12},{8,0},{12,4},{16,24},{20,28},{24,16},{28,20},{1,9},{5... | collective-permute-start | bytes 331784 | tf_op jit(solution)/shard_map/ppermute | solution.py:134
  34.6 8.3 %collective-permute-start.15 = (bf16[96,1152]{1,0:T(8,128)(2,1)S(1)}, bf16[96,1152]{1,0:T(8,128)(2,1)S(1)}, u32[]{:S(2)}, u32[]{:S(2)}) collective-permute-start(bf16[96,1152]{1,0:T(8,128)(2,1)S(1)} %pad_maximum_fusion.3), channel_id=1, source_target_pairs={{0,2},{1,3},{2,0},{3,1},{4,6},{5,7},{6,4},{7,5},{8,10},{9,11},{10,... | collective-permute-start | bytes 663560 | tf_op jit(solution)/shard_map/ppermute | solution.py:134
  38.5 18.4 %collective-permute-start.8 = (bf16[96,1024]{1,0:T(8,128)(2,1)S(1)}, bf16[96,1024]{1,0:T(8,128)(2,1)S(1)}, u32[]{:S(2)}, u32[]{:S(2)}) collective-permute-start(bf16[96,1024]{1,0:T(8,128)(2,1)S(1)} %get-tuple-element.51), channel_id=1, source_target_pairs={{0,2},{1,3},{2,0},{3,1},{4,6},{5,7},{6,4},{7,5},{8,10},{9,11},{10,... | collective-permute-start | bytes 589832 | tf_op jit(solution)/shard_map/ppermute | solution.py:134
  41.4 9.5 %collective-permute-start.18 = (bf16[96,1024]{1,0:T(8,128)(2,1)S(1)}, bf16[96,1024]{1,0:T(8,128)(2,1)S(1)}, u32[]{:S(2)}, u32[]{:S(2)}) collective-permute-start(bf16[96,1024]{1,0:T(8,128)(2,1)S(1)} %get-tuple-element.64), channel_id=1, source_target_pairs={{0,2},{1,3},{2,0},{3,1},{4,6},{5,7},{6,4},{7,5},{8,10},{9,11},{10,... | collective-permute-start | bytes 589832 | tf_op jit(solution)/shard_map/ppermute | solution.py:134
  42.9 5.6 %collective-permute-start.10 = (bf16[48,1152]{1,0:T(8,128)(2,1)S(1)}, bf16[48,1152]{1,0:T(8,128)(2,1)S(1)}, u32[]{:S(2)}, u32[]{:S(2)}) collective-permute-start(bf16[48,1152]{1,0:T(8,128)(2,1)S(1)} %copy-done.5), channel_id=1, source_target_pairs={{0,12},{4,8},{8,4},{12,0},{16,28},{20,24},{24,20},{28,16},{1,13},{... | collective-permute-start | bytes 331784 | tf_op jit(solution)/shard_map/ppermute | solution.py:134
  48.6 8.4 %collective-permute-start.11 = (bf16[96,1152]{1,0:T(8,128)(2,1)S(1)}, bf16[96,1152]{1,0:T(8,128)(2,1)S(1)}, u32[]{:S(2)}, u32[]{:S(2)}) collective-permute-start(bf16[96,1152]{1,0:T(8,128)(2,1)S(1)} %pad_maximum_fusion.2), channel_id=1, source_target_pairs={{0,2},{1,3},{2,0},{3,1},{4,6},{5,7},{6,4},{7,5},{8,10},{9,11},{10,... | collective-permute-start | bytes 663560 | tf_op jit(solution)/shard_map/ppermute | solution.py:134
  51.0 9.9 %collective-permute-start.23 = (bf16[48,1024]{1,0:T(8,128)(2,1)S(1)}, bf16[48,1024]{1,0:T(8,128)(2,1)S(1)}, u32[]{:S(2)}, u32[]{:S(2)}) collective-permute-start(bf16[48,1024]{1,0:T(8,128)(2,1)S(1)} %get-tuple-element.78), channel_id=1, source_target_pairs={{0,28},{4,24},{8,20},{12,16},{16,12},{20,8},{24,4},{28,0},{1,29},{... | collective-permute-start | bytes 294920 | tf_op jit(solution)/shard_map/ppermute | solution.py:134
  52.8 8.0 %collective-permute-start.19 = (bf16[96,1024]{1,0:T(8,128)(2,1)S(1)}, bf16[96,1024]{1,0:T(8,128)(2,1)S(1)}, u32[]{:S(2)}, u32[]{:S(2)}) collective-permute-start(bf16[96,1024]{1,0:T(8,128)(2,1)S(1)} %get-tuple-element.71), channel_id=1, source_target_pairs={{0,2},{1,3},{2,0},{3,1},{4,6},{5,7},{6,4},{7,5},{8,10},{9,11},{10,... | collective-permute-start | bytes 589832 | tf_op jit(solution)/shard_map/ppermute | solution.py:134
  54.8 10.4 %collective-permute-start.25 = (bf16[48,1024]{1,0:T(8,128)(2,1)S(1)}, bf16[48,1024]{1,0:T(8,128)(2,1)S(1)}, u32[]{:S(2)}, u32[]{:S(2)}) collective-permute-start(bf16[48,1024]{1,0:T(8,128)(2,1)S(1)} %get-tuple-element.77), channel_id=1, source_target_pairs={{0,24},{4,28},{8,16},{12,20},{16,8},{20,12},{24,0},{28,4},{1,25},{... | collective-permute-start | bytes 294920 | tf_op jit(solution)/shard_map/ppermute | solution.py:134
  59.3 8.8 %copy-start.3 = (s32[128,2]{0,1:T(2,128)S(1)}, s32[128,2]{0,1:T(2,128)}, u32[]{:S(2)}) copy-start(s32[128,2]{0,1:T(2,128)} %param.10) | copy-start | bytes 3076
  59.3 8.9 %copy-start.4 = (f32[128,2]{0,1:T(2,128)S(1)}, f32[128,2]{0,1:T(2,128)}, u32[]{:S(2)}) copy-start(f32[128,2]{0,1:T(2,128)} %param.11) | copy-start | bytes 3076
  59.3 5.7 %collective-permute-start.17 = (bf16[96,1024]{1,0:T(8,128)(2,1)S(1)}, bf16[96,1024]{1,0:T(8,128)(2,1)S(1)}, u32[]{:S(2)}, u32[]{:S(2)}) collective-permute-start(bf16[96,1024]{1,0:T(8,128)(2,1)S(1)} %get-tuple-element.70), channel_id=1, source_target_pairs={{0,2},{1,3},{2,0},{3,1},{4,6},{5,7},{6,4},{7,5},{8,10},{9,11},{10,... | collective-permute-start | bytes 589832 | tf_op jit(solution)/shard_map/ppermute | solution.py:134
  60.0 8.3 %collective-permute-start.12 = (bf16[48,1024]{1,0:T(8,128)(2,1)S(1)}, bf16[48,1024]{1,0:T(8,128)(2,1)S(1)}, u32[]{:S(2)}, u32[]{:S(2)}) collective-permute-start(bf16[48,1024]{1,0:T(8,128)(2,1)S(1)} %get-tuple-element.57), channel_id=1, source_target_pairs={{0,4},{4,0},{8,12},{12,8},{16,20},{20,16},{24,28},{28,24},{1,5},{5... | collective-permute-start | bytes 294920 | tf_op jit(solution)/shard_map/ppermute | solution.py:134
  60.9 7.4 %collective-permute-start.24 = (bf16[48,1024]{1,0:T(8,128)(2,1)S(1)}, bf16[48,1024]{1,0:T(8,128)(2,1)S(1)}, u32[]{:S(2)}, u32[]{:S(2)}) collective-permute-start(bf16[48,1024]{1,0:T(8,128)(2,1)S(1)} %get-tuple-element.76), channel_id=1, source_target_pairs={{0,20},{4,16},{8,28},{12,24},{16,4},{20,0},{24,12},{28,8},{1,21},{... | collective-permute-start | bytes 294920 | tf_op jit(solution)/shard_map/ppermute | solution.py:134
  61.4 8.3 %collective-permute-start.22 = (bf16[48,1024]{1,0:T(8,128)(2,1)S(1)}, bf16[48,1024]{1,0:T(8,128)(2,1)S(1)}, u32[]{:S(2)}, u32[]{:S(2)}) collective-permute-start(bf16[48,1024]{1,0:T(8,128)(2,1)S(1)} %get-tuple-element.80), channel_id=1, source_target_pairs={{0,16},{4,20},{8,24},{12,28},{16,0},{20,4},{24,8},{28,12},{1,17},{... | collective-permute-start | bytes 294920 | tf_op jit(solution)/shard_map/ppermute | solution.py:134
  65.1 6.3 %collective-permute-start.21 = (bf16[48,1024]{1,0:T(8,128)(2,1)S(1)}, bf16[48,1024]{1,0:T(8,128)(2,1)S(1)}, u32[]{:S(2)}, u32[]{:S(2)}) collective-permute-start(bf16[48,1024]{1,0:T(8,128)(2,1)S(1)} %get-tuple-element.73), channel_id=1, source_target_pairs={{0,12},{4,8},{8,4},{12,0},{16,28},{20,24},{24,20},{28,16},{1,13},{... | collective-permute-start | bytes 294920 | tf_op jit(solution)/shard_map/ppermute | solution.py:134
  65.2 6.6 %collective-permute-start.20 = (bf16[48,1024]{1,0:T(8,128)(2,1)S(1)}, bf16[48,1024]{1,0:T(8,128)(2,1)S(1)}, u32[]{:S(2)}, u32[]{:S(2)}) collective-permute-start(bf16[48,1024]{1,0:T(8,128)(2,1)S(1)} %get-tuple-element.72), channel_id=1, source_target_pairs={{0,8},{4,12},{8,0},{12,4},{16,24},{20,28},{24,16},{28,20},{1,9},{5... | collective-permute-start | bytes 294920 | tf_op jit(solution)/shard_map/ppermute | solution.py:134
  (1 other events, 4.4 us)
